TPU v7x, 32 devices: a whole 2x2x4 slice. The times are simulated.
32 devices in a mesh: loop: 8 (over z, core), rep: 4 (over y, x).
Axes of the slice: x: 2, y: 2, z: 4, core: 2. Of those that a mesh axis runs over, the one named last changes fastest.
Arguments:
- lam: bfloat16 [8, 384, 1024], P(None, None, ('rep', 'loop')), may hold values from -6 to 6
- integrals: bfloat16 [8, 1024, 2048], P(None, 'rep', 'loop'), may hold values from -0.1875 to 0.1875
- block_mask: int32 [8, 32], P(None, 'rep'), may hold values 0 or 1
Outputs:
- ladder: bfloat16 [8, 384, 2048], P(None, 'rep', 'loop')
All inputs are finite; a program needn't handle non-finite values. No bound on the sum of `block_mask` on one device may be relied on, other than what follows from the above.
Results may differ from a plain program's by a relative error of at most 0.001.
Values may be sent and summed in bfloat16 or wider, within the bound.
No kernel may reach another device: no remote copies, remote signals or barrier semaphores. Data moves between devices by JAX's collectives and lax.ppermute only.
A program may use at most 64 MiB of HBM per device.

v0:
```python
import jax
import jax.numpy as jnp
from jax import lax
from jax.sharding import PartitionSpec as P


def per_device(lam, integrals, block_mask):
    block_rows = lam.shape[2]
    live = jnp.repeat(block_mask, block_rows, axis=1) == 1
    kept = jnp.where(live[:, :, None], integrals, jnp.zeros_like(integrals))
    layer_lam = lax.all_gather(lam, "loop", axis=2, tiled=True)
    partial_sum = jnp.einsum("hpk,hka->hpa", layer_lam, kept, preferred_element_type=jnp.float32)
    own_rows = lam.shape[1] // lax.axis_size("rep")
    summed = lax.psum(partial_sum, "rep")
    result = lax.dynamic_slice_in_dim(summed, lax.axis_index("rep") * own_rows, own_rows, 1)
    return result.astype(jnp.bfloat16)


def solution(mesh):
    return jax.shard_map(
        per_device,
        mesh=mesh,
        in_specs=(P(None, None, ("rep", "loop")), P(None, "rep", "loop"), P(None, "rep")),
        out_specs=P(None, "rep", "loop"),
        check_vma=False,
    )
```

profile of v0, /device:TPU:0, one launch (start us, length us, event | category | flops | bytes accessed | tf_op | source)
XLA Modules:
  0.0 158.6 jit_solution(18445953542589369292)
XLA Ops:
  6.5 0.0 all-gather.2.cloned.1.call-start
  6.5 0.7 all-gather.2.cloned.1.call-update
  7.3 0.7 broadcast_compare_fusion
  8.0 0.1 broadcast_in_dim.15
  8.0 0.1 eq.16
  8.1 28.6 %all-gather.2.cloned.1.call-done = bf16[8,384,256]{1,2,0:T(8,128)(2,1)} async-done(((bf16[8,384,32]{1,2,0:T(8,128)(2,1)}), bf16[8,384,256]{1,2,0:T(8,128)(2,1)}) %all-gather.2.cloned.1.call-update) | async-done | bytes 1572880 | tf_op jit(solution)/shard_map/all_gather | solution.py:11
  36.8 2.7 %convolution_bitcast_fusion = f32[8,384,256]{2,1,0:T(8,128)S(1)} fusion(bf16[8,384,256]{1,2,0:T(8,128)(2,1)} %all-gather.2.cloned.1.call-done, bf16[8,256,256]{2,1,0:T(8,128)(2,1)} %param.4, pred[8,256]{1,0:T(8,128)(4,1)S(1)} %eq.16), kind=kOutput, calls=%fused_computation | convolution fusion | flops 403177472 | bytes 5769216 | tf_op jit(solution)/shard_map/hpk,hka->hpa/dot_general | solution.py:12
  39.4 110.6 %all-reduce.1 = bf16[8,384,256]{2,1,0:T(8,128)(2,1)} all-reduce(f32[8,384,256]{2,1,0:T(8,128)S(1)} %convolution_bitcast_fusion), channel_id=1, replica_groups=mesh['loop'=8,'rep'=4] {'rep'}, use_global_device_ids=true, to_apply=%region_0.1 | all-reduce | flops 786432 | bytes 4718592 | tf_op jit(solution)/shard_map/psum | solution.py:14
  150.0 1.8 %dynamic-slice_convert_fusion = bf16[8,96,256]{2,1,0:T(8,128)(2,1)} fusion(bf16[8,384,256]{2,1,0:T(8,128)(2,1)} %all-reduce.1, s32[]{:T(128)S(6)} %select_n.8), kind=kLoop, calls=%fused_computation.3 | loop fusion | bytes 786436 | tf_op jit(solution)/shard_map/convert_element_type | solution.py:16
Async XLA Ops:
  6.5 30.2 %all-gather.2.cloned.1.call-start = ((), (), s32[]{:S(2)}) async-start(), calls=%async_computation | async-start | bytes 1769472 | tf_op jit(solution)/shard_map/all_gather | solution.py:11
Sparse Core Ops, SparseCore 0:
  9.0 27.7 all-gather.1
where the time goes:
time: 159 us
  blocking collectives  111 us (70%)
  waiting for transfers between devices  29.3 us (18%)
  between operations  13.4 us (8%)
  matrix products  2.67 us (2%)
  local copies, waits for them, and re-layouts  1.94 us (1%)
    psum x1, blocking collectives, per_device(): summed = lax.psum(partial_sum, 'rep')  111 us
    all_gather x1, waiting for transfers between devices, per_device(): layer_lam = lax.all_gather(lam, 'loop', axis=2, tiled=True)  28.6 us
  transfers between devices with their start and end apart: 1, of which 1 were waited for; matrix products, arithmetic and copies ran while one was open for 1% of the time, Pallas kernels for 0%

commit v1 on v0

v1 whole, which is shorter than its diff:
```python
import functools

import jax
import jax.numpy as jnp
from jax import lax
from jax.experimental import pallas as pl
from jax.experimental.pallas import tpu as pltpu
from jax.sharding import PartitionSpec as P

VMEM = pltpu.VMEM


def pack_kernel(halves, mask_ref, lam_ref, own_ref, to_x_ref, to_y_ref, turned):
    spot = lax.axis_index("loop")
    y, x = lax.axis_index("rep") // 2, lax.axis_index("rep") % 2
    rows = turned.shape[2]
    for kind in range(2):
        live = [mask_ref[kind * halves + h, spot] == 1 for h in range(halves)]
        block = jnp.concatenate(
            [jnp.where(live[h], lam_ref[kind * halves + h], 0).astype(jnp.bfloat16) for h in range(halves)], axis=0
        )
        flipped = block.T
        for quarter in range(4):
            turned[kind, quarter] = flipped[quarter * rows : (quarter + 1) * rows]
    ny, nx = 1 - y, 1 - x
    own_ref[0, 0] = turned[0, ny * 2 + x]
    own_ref[0, 1] = turned[1, y * 2 + nx]
    own_ref[1, 0] = turned[0, y * 2 + x]
    own_ref[1, 1] = turned[1, y * 2 + x]
    to_x_ref[0] = turned[0, ny * 2 + nx]
    to_x_ref[1] = turned[0, y * 2 + nx]
    to_y_ref[0] = turned[1, ny * 2 + nx]
    to_y_ref[1] = turned[1, ny * 2 + x]


def products(mine_ref, other_ref, own_ref, from_x_ref, from_y_ref, pieces):
    spot = lax.axis_index("loop")
    chips = mine_ref.shape[0]
    z, core = spot // 2, spot % 2
    for step in range(chips):
        source = lax.rem(z - step + chips, chips) * 2
        pieces[source + core] = mine_ref[step]
        pieces[source + 1 - core] = other_ref[step]
    halves = from_x_ref.shape[0]
    depth = pieces.shape[3] // halves
    for kind, far_ref in ((0, from_x_ref), (1, from_y_ref)):
        near = [pieces[s, kind] for s in range(2 * chips)]
        far = [pieces[s, 2 + kind] for s in range(2 * chips)]
        for h in range(halves):
            cut = slice(h * depth, (h + 1) * depth)
            near_lam = jnp.concatenate([p[:, cut] for p in near], axis=1)
            far_lam = jnp.concatenate([p[:, cut] for p in far], axis=1)
            yield kind * halves + h, (
                jnp.dot(near_lam, own_ref[kind * halves + h], preferred_element_type=jnp.float32)
                + jnp.dot(far_lam, far_ref[h], preferred_element_type=jnp.float32)
            )


def sent_kernel(mine_ref, other_ref, own_ref, from_x_ref, from_y_ref, to_y_ref, to_x_ref, pieces):
    halves = from_x_ref.shape[0]
    for h, value in products(mine_ref, other_ref, own_ref, from_x_ref, from_y_ref, pieces):
        if h < halves:
            to_y_ref[h] = value
        else:
            to_x_ref[h - halves] = value


def kept_kernel(mine_ref, other_ref, own_ref, from_x_ref, from_y_ref, sum_y_ref, sum_x_ref, out_ref, pieces):
    halves = from_x_ref.shape[0]
    for h, value in products(mine_ref, other_ref, own_ref, from_x_ref, from_y_ref, pieces):
        arrived = sum_y_ref[h] if h < halves else sum_x_ref[h - halves]
        out_ref[h] = (value + arrived).astype(out_ref.dtype)


def square(lam, integrals, block_mask):
    irreps, occ, depth = lam.shape
    halves = irreps // 2
    rows = occ // 4
    columns = integrals.shape[2]
    loops = lax.axis_size("loop")
    chips = loops // 2
    over_x = [(r, r ^ 1) for r in range(4)]
    over_y = [(r, r ^ 2) for r in range(4)]
    over_core = [(s, s ^ 1) for s in range(loops)]
    turn = lambda k: [(s, (s + 2 * k) % loops) for s in range(loops)]
    bf16, f32 = jnp.bfloat16, jnp.float32
    lanes = halves * depth

    own, to_x, to_y = pl.pallas_call(
        functools.partial(pack_kernel, halves),
        out_shape=(
            jax.ShapeDtypeStruct((2, 2, rows, lanes), bf16),
            jax.ShapeDtypeStruct((2, rows, lanes), bf16),
            jax.ShapeDtypeStruct((2, rows, lanes), bf16),
        ),
        in_specs=[pl.BlockSpec(memory_space=pltpu.SMEM), pl.BlockSpec(memory_space=VMEM)],
        out_specs=[pl.BlockSpec(memory_space=VMEM)] * 3,
        scratch_shapes=[VMEM((2, 4, rows, lanes), bf16)],
    )(block_mask, lam.transpose(0, 2, 1))

    lam_x = lax.ppermute(to_x, "rep", over_x)
    lam_y = lax.ppermute(to_y, "rep", over_y)
    far_x = lax.ppermute(integrals[:halves], "rep", over_x)
    far_y = lax.ppermute(integrals[halves:], "rep", over_y)

    def gathered(which):
        mine = jnp.concatenate([own[which], lam_x[which][None], lam_y[which][None]], axis=0)
        mine = jnp.stack([mine] + [lax.ppermute(mine, "loop", turn(k)) for k in range(1, chips)])
        return mine, lax.ppermute(mine, "loop", over_core)

    scratch = [VMEM((loops, 4, rows, lanes), bf16)]
    mine, other = gathered(0)
    partial_y, partial_x = pl.pallas_call(
        sent_kernel,
        out_shape=(jax.ShapeDtypeStruct((halves, rows, columns), f32),) * 2,
        in_specs=[pl.BlockSpec(memory_space=VMEM)] * 5,
        out_specs=[pl.BlockSpec(memory_space=VMEM)] * 2,
        scratch_shapes=scratch,
    )(mine, other, integrals, far_x, far_y)
    sum_y = lax.ppermute(partial_y, "rep", over_y)
    sum_x = lax.ppermute(partial_x, "rep", over_x)
    mine, other = gathered(1)
    return pl.pallas_call(
        kept_kernel,
        out_shape=jax.ShapeDtypeStruct((irreps, rows, columns), bf16),
        in_specs=[pl.BlockSpec(memory_space=VMEM)] * 7,
        out_specs=pl.BlockSpec(memory_space=VMEM),
        scratch_shapes=scratch,
    )(mine, other, integrals, far_x, far_y, sum_y, sum_x)


def general(lam, integrals, block_mask):
    live = jnp.repeat(block_mask, lam.shape[2], axis=1) == 1
    kept = jnp.where(live[:, :, None], integrals, jnp.zeros_like(integrals))
    layer_lam = lax.all_gather(lam, "loop", axis=2, tiled=True)
    partial_sum = jnp.einsum("hpk,hka->hpa", layer_lam, kept, preferred_element_type=jnp.float32)
    return lax.psum_scatter(partial_sum, "rep", scatter_dimension=1, tiled=True).astype(jnp.bfloat16)


def solution(mesh):
    return jax.shard_map(
        square if mesh.shape["rep"] == 4 else general,
        mesh=mesh,
        in_specs=(P(None, None, ("rep", "loop")), P(None, "rep", "loop"), P(None, "rep")),
        out_specs=P(None, "rep", "loop"),
        check_vma=False,
    )
```

time: 159 us -> 56.5 us (0.36)
  blocking collectives: 111 us -> 0 us
  starting transfers between devices: 0.01 us -> 16.1 us
  between operations: 13.4 us -> 0.14 us
  Pallas kernels: 0 us -> 8.73 us
  waiting for transfers between devices: 29.3 us -> 26.5 us
  local copies, waits for them, and re-layouts: 1.94 us -> 4.65 us
  matrix products: 2.67 us -> 0 us
    psum x1 -> x0, blocking collectives: 111 us -> none  [per_device(): summed = lax.psum(partial_sum, 'rep')]
    all_gather x1 -> x0, waiting for transfers between devices: 28.6 us -> none  [per_device(): layer_lam = lax.all_gather(lam, 'loop', axis=2, tiled=True)]
    ppermute x0 -> x14, waiting for transfers between devices: none -> 26.5 us  [the longest x6 13.7 us: gathered(): lax.ppermute(mine, 'loop', turn(k))]
    ppermute x0 -> x14, starting transfers between devices: none -> 16.1 us  [the longest x6 7.32 us: gathered(): lax.ppermute(mine, 'loop', turn(k))]
    pallas_call x0 -> x3, Pallas kernels: none -> 8.73 us  [the longest x1 3.61 us: square(): pl.pallas_call(kept_kernel, out_shape=jax.ShapeDtypeStruct((irreps, rows,...]
    dot_general x1 -> x0, matrix products: 2.67 us -> none  [per_device(): jnp.einsum('hpk,hka->hpa', layer_lam, kept, preferred_element_type=jnp.fl...]
    unnamed x0 -> x16, local copies, waits for them, and re-layouts: none -> 2.54 us
    convert_element_type x1 -> x0, local copies, waits for them, and re-layouts: 1.77 us -> none  [per_device(): return result.astype(jnp.bfloat16)]
  transfers between devices with their start and end apart: 1 -> 14, of which waited for: 1 -> 8; matrix products, arithmetic and copies ran while one was open for 1% -> 4% of each run, Pallas kernels for 0% -> 6%
where the time goes in v1:
time: 56.5 us; the launch traced here: 56.3 us
  waiting for transfers between devices  26.5 us (47%)
  starting transfers between devices  16.1 us (28%)
  Pallas kernels  8.73 us (15%)
  local copies, waits for them, and re-layouts  4.65 us (8%)
    ppermute x6, waiting for transfers between devices, gathered(): lax.ppermute(mine, 'loop', turn(k))  13.7 us
    ppermute x1, waiting for transfers between devices, square(): sum_y = lax.ppermute(partial_y, 'rep', over_y)  9.61 us
    ppermute x6, starting transfers between devices, gathered(): lax.ppermute(mine, 'loop', turn(k))  7.32 us
    pallas_call x1, Pallas kernels, square(): pl.pallas_call(kept_kernel, out_shape=jax.ShapeDtypeStruct((irreps, rows,...  3.61 us
    pallas_call x1, Pallas kernels, square(): pl.pallas_call(sent_kernel, out_shape=(jax.ShapeDtypeStruct((halves, rows...  3.39 us
    ppermute x1, starting transfers between devices, square(): lam_x = lax.ppermute(to_x, 'rep', over_x)  2.94 us
    unnamed x16, local copies, waits for them, and re-layouts  2.54 us
    ppermute x1, waiting for transfers between devices, square(): lam_y = lax.ppermute(to_y, 'rep', over_y)  1.93 us
  transfers between devices with their start and end apart: 14, of which 8 were waited for; matrix products, arithmetic and copies ran while one was open for 4% of the time, Pallas kernels for 6%

profile of v1, /device:TPU:0, one launch (start us, length us, event | category | flops | bytes accessed | tf_op | source)
XLA Modules:
  0.0 56.3 jit_solution(13691360901047049115)
XLA Ops:
  0.0 1.7 %shard_map.37 = (bf16[2,2,96,128]{3,2,1,0:T(8,128)(2,1)}, bf16[2,96,128]{2,1,0:T(8,128)(2,1)}, bf16[2,96,128]{2,1,0:T(8,128)(2,1)}) custom-call(s32[8,8]{1,0:T(8,128)} %mask_ref.1, bf16[8,32,384]{2,1,0:T(8,128)(2,1)} %bitcast.15), custom_call_target="tpu_custom_call" | custom-call | tf_op jit(solution)/shard_map/pallas_call | solution.py:89
  1.7 2.9 %collective-permute-start = (bf16[2,96,128]{2,1,0:T(8,128)(2,1)}, bf16[2,96,128]{2,1,0:T(8,128)(2,1)S(1)}, u32[]{:S(2)}, u32[]{:S(2)}) collective-permute-start(bf16[2,96,128]{2,1,0:T(8,128)(2,1)} %get-tuple-element.11), channel_id=1, source_target_pairs={{0,1},{1,0},{2,3},{3,2},{4,5},{5,4},{6,7},{7,6},{8,9},{9,8},{10,11... | collective-permute-start | bytes 147464 | tf_op jit(solution)/shard_map/ppermute | solution.py:101
  4.7 1.5 %collective-permute-start.1 = (bf16[2,96,128]{2,1,0:T(8,128)(2,1)}, bf16[2,96,128]{2,1,0:T(8,128)(2,1)S(1)}, u32[]{:S(2)}, u32[]{:S(2)}) collective-permute-start(bf16[2,96,128]{2,1,0:T(8,128)(2,1)} %get-tuple-element.12), channel_id=1, source_target_pairs={{0,2},{1,3},{2,0},{3,1},{4,6},{5,7},{6,4},{7,5},{8,10},{9,11},{10,... | collective-permute-start | bytes 147464 | tf_op jit(solution)/shard_map/ppermute | solution.py:102
  6.2 0.8 %slice_bitcast_fusion = (bf16[2,96,128]{2,1,0:T(8,128)(2,1)S(1)}, bf16[2,96,128]{2,1,0:T(8,128)(2,1)S(1)}) fusion(bf16[2,2,96,128]{3,2,1,0:T(8,128)(2,1)} %get-tuple-element.10), kind=kLoop, calls=%fused_computation.4 | loop fusion | bytes 196608 | tf_op jit(solution)/shard_map/squeeze | solution.py:107
  7.0 0.0 collective-permute-done
  7.0 1.9 %collective-permute-done.1 = bf16[2,96,128]{2,1,0:T(8,128)(2,1)S(1)} collective-permute-done((bf16[2,96,128]{2,1,0:T(8,128)(2,1)}, bf16[2,96,128]{2,1,0:T(8,128)(2,1)S(1)}, u32[]{:S(2)}, u32[]{:S(2)}) %collective-permute-start.1) | collective-permute-done | bytes 49184 | tf_op jit(solution)/shard_map/ppermute | solution.py:102
  9.0 3.7 %collective-permute-start.10 = (bf16[4,96,128]{2,1,0:T(8,128)(2,1)S(1)}, bf16[4,96,128]{2,1,0:T(8,128)(2,1)S(1)}, u32[]{:S(2)}, u32[]{:S(2)}) collective-permute-start(bf16[4,96,128]{2,1,0:T(8,128)(2,1)S(1)} %get-tuple-element.18), channel_id=1, source_target_pairs={{0,24},{4,28},{8,0},{12,4},{16,8},{20,12},{24,16},{28,20},{1,25},{... | collective-permute-start | bytes 294920 | tf_op jit(solution)/shard_map/ppermute | solution.py:108
  12.7 0.0 collective-permute-start.8
  12.7 1.0 %collective-permute-start.9 = (bf16[4,96,128]{2,1,0:T(8,128)(2,1)S(1)}, bf16[4,96,128]{2,1,0:T(8,128)(2,1)S(1)}, u32[]{:S(2)}, u32[]{:S(2)}) collective-permute-start(bf16[4,96,128]{2,1,0:T(8,128)(2,1)S(1)} %get-tuple-element.18), channel_id=1, source_target_pairs={{0,16},{4,20},{8,24},{12,28},{16,0},{20,4},{24,8},{28,12},{1,17},{... | collective-permute-start | bytes 294920 | tf_op jit(solution)/shard_map/ppermute | solution.py:108
  13.7 1.3 %fusion.2 = (bf16[4,256,256]{2,1,0:T(8,128)(2,1)S(1)}, bf16[4,256,256]{2,1,0:T(8,128)(2,1)S(1)}) fusion(bf16[8,256,256]{2,1,0:T(8,128)(2,1)} %own_ref.3), kind=kLoop, calls=%fused_computation.8 | loop fusion | bytes 2097152 | tf_op jit(solution)/shard_map/slice | solution.py:104
  14.9 0.6 %collective-permute-start.6 = (bf16[4,256,256]{2,1,0:T(8,128)(2,1)S(1)}, bf16[4,256,256]{2,1,0:T(8,128)(2,1)S(1)}, u32[]{:S(2)}, u32[]{:S(2)}) collective-permute-start(bf16[4,256,256]{2,1,0:T(8,128)(2,1)S(1)} %get-tuple-element.16), channel_id=1, source_target_pairs={{0,1},{1,0},{2,3},{3,2},{4,5},{5,4},{6,7},{7,6},{8,9},{9,8},{10,11... | collective-permute-start | bytes 1572872 | tf_op jit(solution)/shard_map/ppermute | solution.py:103
  15.5 1.5 %collective-permute-start.7 = (bf16[4,256,256]{2,1,0:T(8,128)(2,1)S(1)}, bf16[4,256,256]{2,1,0:T(8,128)(2,1)S(1)}, u32[]{:S(2)}, u32[]{:S(2)}) collective-permute-start(bf16[4,256,256]{2,1,0:T(8,128)(2,1)S(1)} %get-tuple-element.15), channel_id=1, source_target_pairs={{0,2},{1,3},{2,0},{3,1},{4,6},{5,7},{6,4},{7,5},{8,10},{9,11},{10,... | collective-permute-start | bytes 1572872 | tf_op jit(solution)/shard_map/ppermute | solution.py:104
  17.1 0.0 collective-permute-done.10
  17.1 2.0 %collective-permute-done.8 = bf16[4,96,128]{2,1,0:T(8,128)(2,1)S(1)} collective-permute-done((bf16[4,96,128]{2,1,0:T(8,128)(2,1)S(1)}, bf16[4,96,128]{2,1,0:T(8,128)(2,1)S(1)}, u32[]{:S(2)}, u32[]{:S(2)}) %collective-permute-start.8) | collective-permute-done | bytes 98336 | tf_op jit(solution)/shard_map/ppermute | solution.py:108
  19.1 1.9 %collective-permute-done.9 = bf16[4,96,128]{2,1,0:T(8,128)(2,1)S(1)} collective-permute-done((bf16[4,96,128]{2,1,0:T(8,128)(2,1)S(1)}, bf16[4,96,128]{2,1,0:T(8,128)(2,1)S(1)}, u32[]{:S(2)}, u32[]{:S(2)}) %collective-permute-start.9) | collective-permute-done | bytes 98336 | tf_op jit(solution)/shard_map/ppermute | solution.py:108
  21.0 0.1 pad_maximum_fusion.1.mine_ref
  21.1 0.0 copy-start.2
  21.1 0.1 collective-permute-start.11
  21.2 0.1 collective-permute-start.2
  21.2 2.6 %collective-permute-start.3 = (bf16[4,96,128]{2,1,0:T(8,128)(2,1)S(1)}, bf16[4,96,128]{2,1,0:T(8,128)(2,1)S(1)}, u32[]{:S(2)}, u32[]{:S(2)}) collective-permute-start(bf16[4,96,128]{2,1,0:T(8,128)(2,1)S(1)} %get-tuple-element.22), channel_id=1, source_target_pairs={{0,16},{4,20},{8,24},{12,28},{16,0},{20,4},{24,8},{28,12},{1,17},{... | collective-permute-start | bytes 294920 | tf_op jit(solution)/shard_map/ppermute | solution.py:108
  23.8 4.9 %collective-permute-done.2 = bf16[4,96,128]{2,1,0:T(8,128)(2,1)S(1)} collective-permute-done((bf16[4,96,128]{2,1,0:T(8,128)(2,1)S(1)}, bf16[4,96,128]{2,1,0:T(8,128)(2,1)S(1)}, u32[]{:S(2)}, u32[]{:S(2)}) %collective-permute-start.2) | collective-permute-done | bytes 98336 | tf_op jit(solution)/shard_map/ppermute | solution.py:108
  28.7 0.0 collective-permute-start.4
  28.7 3.3 %collective-permute-done.3 = bf16[4,96,128]{2,1,0:T(8,128)(2,1)S(1)} collective-permute-done((bf16[4,96,128]{2,1,0:T(8,128)(2,1)S(1)}, bf16[4,96,128]{2,1,0:T(8,128)(2,1)S(1)}, u32[]{:S(2)}, u32[]{:S(2)}) %collective-permute-start.3) | collective-permute-done | bytes 98336 | tf_op jit(solution)/shard_map/ppermute | solution.py:108
  32.0 1.6 %collective-permute-done.4 = bf16[4,96,128]{2,1,0:T(8,128)(2,1)S(1)} collective-permute-done((bf16[4,96,128]{2,1,0:T(8,128)(2,1)S(1)}, bf16[4,96,128]{2,1,0:T(8,128)(2,1)S(1)}, u32[]{:S(2)}, u32[]{:S(2)}) %collective-permute-start.4) | collective-permute-done | bytes 98336 | tf_op jit(solution)/shard_map/ppermute | solution.py:108
  33.6 0.1 pad_maximum_fusion.mine_ref
  33.7 0.0 copy-done.2
  33.7 0.0 copy-start.3
  33.7 0.1 collective-permute-start.5
  33.8 0.0 collective-permute-done.6.from_x_ref
  33.8 0.0 copy-start
  33.8 0.0 collective-permute-done.7.from_y_ref
  33.8 0.0 copy-start.1
  33.8 0.0 collective-permute-done.11.other_ref
  33.8 0.8 %copy-done = bf16[4,256,256]{2,1,0:T(8,128)(2,1)} copy-done((bf16[4,256,256]{2,1,0:T(8,128)(2,1)}, bf16[4,256,256]{2,1,0:T(8,128)(2,1)S(1)}, u32[]{:S(2)}) %copy-start) | copy-done | bytes 524312
  34.6 0.2 copy-done.1
  34.8 0.0 copy-start.4
  34.8 0.8 %copy-done.4 = bf16[4,4,96,128]{3,2,1,0:T(8,128)(2,1)} copy-done((bf16[4,4,96,128]{3,2,1,0:T(8,128)(2,1)}, bf16[4,4,96,128]{3,2,1,0:T(8,128)(2,1)S(1)}, u32[]{:S(2)}) %copy-start.4) | copy-done | bytes 393240
  35.6 3.4 %shard_map.38 = (f32[4,96,256]{2,1,0:T(8,128)}, f32[4,96,256]{2,1,0:T(8,128)}) custom-call(bf16[4,4,96,128]{3,2,1,0:T(8,128)(2,1)} %copy-done.2, bf16[4,4,96,128]{3,2,1,0:T(8,128)(2,1)} %copy-done.4, bf16[8,256,256]{2,1,0:T(8,128)(2,1)} %own_ref.3, bf16[4,256,256]{2,1,0:T(8,128)(2,1)} %copy-done, bf16[4,256,256]{2,1,0:T(8,128)(2,1)} %copy-done.1), custom_call_target="tpu_custom_call" | custom-call | tf_op jit(solution)/shard_map/pallas_call | solution.py:113
  39.0 0.0 copy-done.3
  39.0 1.5 %collective-permute-start.12 = (f32[4,96,256]{2,1,0:T(8,128)}, f32[4,96,256]{2,1,0:T(8,128)S(1)}, u32[]{:S(2)}, u32[]{:S(2)}) collective-permute-start(f32[4,96,256]{2,1,0:T(8,128)} %get-tuple-element.13), channel_id=1, source_target_pairs={{0,2},{1,3},{2,0},{3,1},{4,6},{5,7},{6,4},{7,5},{8,10},{9,11},{10,... | collective-permute-start | bytes 1179656 | tf_op jit(solution)/shard_map/ppermute | solution.py:120
  40.5 0.5 collective-permute-start.13
  41.0 0.0 collective-permute-done.5.other_ref
  41.0 9.6 %collective-permute-done.12.sum_y_ref = f32[4,96,256]{2,1,0:T(8,128)S(1)} collective-permute-done((f32[4,96,256]{2,1,0:T(8,128)}, f32[4,96,256]{2,1,0:T(8,128)S(1)}, u32[]{:S(2)}, u32[]{:S(2)}) %collective-permute-start.12) | collective-permute-done | bytes 393248 | tf_op jit(solution)/shard_map/ppermute | solution.py:120
  50.6 1.2 %collective-permute-done.13.sum_x_ref = f32[4,96,256]{2,1,0:T(8,128)S(1)} collective-permute-done((f32[4,96,256]{2,1,0:T(8,128)}, f32[4,96,256]{2,1,0:T(8,128)S(1)}, u32[]{:S(2)}, u32[]{:S(2)}) %collective-permute-start.13) | collective-permute-done | bytes 393248 | tf_op jit(solution)/shard_map/ppermute | solution.py:121
  51.9 0.0 copy-done.5
  51.9 0.0 copy-done.6
  51.9 0.8 %copy-done.7 = f32[4,96,256]{2,1,0:T(8,128)} copy-done((f32[4,96,256]{2,1,0:T(8,128)}, f32[4,96,256]{2,1,0:T(8,128)S(1)}, u32[]{:S(2)}) %copy-start.7) | copy-done | bytes 393240
  52.6 3.6 %shard_map.39 = bf16[8,96,256]{2,1,0:T(8,128)(2,1)} custom-call(bf16[4,4,96,128]{3,2,1,0:T(8,128)(2,1)} %copy-done.3, bf16[4,4,96,128]{3,2,1,0:T(8,128)(2,1)} %copy-done.5, bf16[8,256,256]{2,1,0:T(8,128)(2,1)} %own_ref.3, bf16[4,256,256]{2,1,0:T(8,128)(2,1)} %copy-done, bf16[4,256,256]{2,1,0:T(8,128)(2,1)} %copy-done.1, f32[4,96,256]{2,1,0:T(8,128)} %copy-done.6, ...), custom_call_target="tpu_custom_call" | custom-call | tf_op jit(solution)/shard_map/pallas_call | solution.py:123
  (7 shorter events, 0.1 us)
Async XLA Ops:
  1.7 5.3 %collective-permute-start = (bf16[2,96,128]{2,1,0:T(8,128)(2,1)}, bf16[2,96,128]{2,1,0:T(8,128)(2,1)S(1)}, u32[]{:S(2)}, u32[]{:S(2)}) collective-permute-start(bf16[2,96,128]{2,1,0:T(8,128)(2,1)} %get-tuple-element.11), channel_id=1, source_target_pairs={{0,1},{1,0},{2,3},{3,2},{4,5},{5,4},{6,7},{7,6},{8,9},{9,8},{10,11... | collective-permute-start | bytes 147464 | tf_op jit(solution)/shard_map/ppermute | solution.py:101
  4.7 4.3 %collective-permute-start.1 = (bf16[2,96,128]{2,1,0:T(8,128)(2,1)}, bf16[2,96,128]{2,1,0:T(8,128)(2,1)S(1)}, u32[]{:S(2)}, u32[]{:S(2)}) collective-permute-start(bf16[2,96,128]{2,1,0:T(8,128)(2,1)} %get-tuple-element.12), channel_id=1, source_target_pairs={{0,2},{1,3},{2,0},{3,1},{4,6},{5,7},{6,4},{7,5},{8,10},{9,11},{10,... | collective-permute-start | bytes 147464 | tf_op jit(solution)/shard_map/ppermute | solution.py:102
  9.0 8.1 %collective-permute-start.10 = (bf16[4,96,128]{2,1,0:T(8,128)(2,1)S(1)}, bf16[4,96,128]{2,1,0:T(8,128)(2,1)S(1)}, u32[]{:S(2)}, u32[]{:S(2)}) collective-permute-start(bf16[4,96,128]{2,1,0:T(8,128)(2,1)S(1)} %get-tuple-element.18), channel_id=1, source_target_pairs={{0,24},{4,28},{8,0},{12,4},{16,8},{20,12},{24,16},{28,20},{1,25},{... | collective-permute-start | bytes 294920 | tf_op jit(solution)/shard_map/ppermute | solution.py:108
  12.7 6.4 %collective-permute-start.8 = (bf16[4,96,128]{2,1,0:T(8,128)(2,1)S(1)}, bf16[4,96,128]{2,1,0:T(8,128)(2,1)S(1)}, u32[]{:S(2)}, u32[]{:S(2)}) collective-permute-start(bf16[4,96,128]{2,1,0:T(8,128)(2,1)S(1)} %get-tuple-element.18), channel_id=1, source_target_pairs={{0,8},{4,12},{8,16},{12,20},{16,24},{20,28},{24,0},{28,4},{1,9},{5... | collective-permute-start | bytes 294920 | tf_op jit(solution)/shard_map/ppermute | solution.py:108
  12.7 8.3 %collective-permute-start.9 = (bf16[4,96,128]{2,1,0:T(8,128)(2,1)S(1)}, bf16[4,96,128]{2,1,0:T(8,128)(2,1)S(1)}, u32[]{:S(2)}, u32[]{:S(2)}) collective-permute-start(bf16[4,96,128]{2,1,0:T(8,128)(2,1)S(1)} %get-tuple-element.18), channel_id=1, source_target_pairs={{0,16},{4,20},{8,24},{12,28},{16,0},{20,4},{24,8},{28,12},{1,17},{... | collective-permute-start | bytes 294920 | tf_op jit(solution)/shard_map/ppermute | solution.py:108
  14.9 18.8 %collective-permute-start.6 = (bf16[4,256,256]{2,1,0:T(8,128)(2,1)S(1)}, bf16[4,256,256]{2,1,0:T(8,128)(2,1)S(1)}, u32[]{:S(2)}, u32[]{:S(2)}) collective-permute-start(bf16[4,256,256]{2,1,0:T(8,128)(2,1)S(1)} %get-tuple-element.16), channel_id=1, source_target_pairs={{0,1},{1,0},{2,3},{3,2},{4,5},{5,4},{6,7},{7,6},{8,9},{9,8},{10,11... | collective-permute-start | bytes 1572872 | tf_op jit(solution)/shard_map/ppermute | solution.py:103
  15.5 18.3 %collective-permute-start.7 = (bf16[4,256,256]{2,1,0:T(8,128)(2,1)S(1)}, bf16[4,256,256]{2,1,0:T(8,128)(2,1)S(1)}, u32[]{:S(2)}, u32[]{:S(2)}) collective-permute-start(bf16[4,256,256]{2,1,0:T(8,128)(2,1)S(1)} %get-tuple-element.15), channel_id=1, source_target_pairs={{0,2},{1,3},{2,0},{3,1},{4,6},{5,7},{6,4},{7,5},{8,10},{9,11},{10,... | collective-permute-start | bytes 1572872 | tf_op jit(solution)/shard_map/ppermute | solution.py:104
  21.1 12.6 %copy-start.2 = (bf16[4,4,96,128]{3,2,1,0:T(8,128)(2,1)}, bf16[4,4,96,128]{3,2,1,0:T(8,128)(2,1)S(1)}, u32[]{:S(2)}) copy-start(bf16[4,4,96,128]{3,2,1,0:T(8,128)(2,1)S(1)} %pad_maximum_fusion.1.mine_ref) | copy-start | bytes 1179652
  21.1 12.7 %collective-permute-start.11 = (bf16[4,4,96,128]{3,2,1,0:T(8,128)(2,1)S(1)}, bf16[4,4,96,128]{3,2,1,0:T(8,128)(2,1)S(1)}, u32[]{:S(2)}, u32[]{:S(2)}) collective-permute-start(bf16[4,4,96,128]{3,2,1,0:T(8,128)(2,1)S(1)} %pad_maximum_fusion.1.mine_ref), channel_id=1, source_target_pairs={{0,4},{4,0},{8,12},{12,8},{16,20},{20,16},{24,28},{28,24},{1,5},{5... | collective-permute-start | bytes 1179656 | tf_op jit(solution)/shard_map/ppermute | solution.py:109
  21.2 7.5 %collective-permute-start.2 = (bf16[4,96,128]{2,1,0:T(8,128)(2,1)S(1)}, bf16[4,96,128]{2,1,0:T(8,128)(2,1)S(1)}, u32[]{:S(2)}, u32[]{:S(2)}) collective-permute-start(bf16[4,96,128]{2,1,0:T(8,128)(2,1)S(1)} %get-tuple-element.22), channel_id=1, source_target_pairs={{0,8},{4,12},{8,16},{12,20},{16,24},{20,28},{24,0},{28,4},{1,9},{5... | collective-permute-start | bytes 294920 | tf_op jit(solution)/shard_map/ppermute | solution.py:108
  21.2 10.8 %collective-permute-start.3 = (bf16[4,96,128]{2,1,0:T(8,128)(2,1)S(1)}, bf16[4,96,128]{2,1,0:T(8,128)(2,1)S(1)}, u32[]{:S(2)}, u32[]{:S(2)}) collective-permute-start(bf16[4,96,128]{2,1,0:T(8,128)(2,1)S(1)} %get-tuple-element.22), channel_id=1, source_target_pairs={{0,16},{4,20},{8,24},{12,28},{16,0},{20,4},{24,8},{28,12},{1,17},{... | collective-permute-start | bytes 294920 | tf_op jit(solution)/shard_map/ppermute | solution.py:108
  28.7 4.9 %collective-permute-start.4 = (bf16[4,96,128]{2,1,0:T(8,128)(2,1)S(1)}, bf16[4,96,128]{2,1,0:T(8,128)(2,1)S(1)}, u32[]{:S(2)}, u32[]{:S(2)}) collective-permute-start(bf16[4,96,128]{2,1,0:T(8,128)(2,1)S(1)} %get-tuple-element.22), channel_id=1, source_target_pairs={{0,24},{4,28},{8,0},{12,4},{16,8},{20,12},{24,16},{28,20},{1,25},{... | collective-permute-start | bytes 294920 | tf_op jit(solution)/shard_map/ppermute | solution.py:108
  33.7 5.3 %copy-start.3 = (bf16[4,4,96,128]{3,2,1,0:T(8,128)(2,1)}, bf16[4,4,96,128]{3,2,1,0:T(8,128)(2,1)S(1)}, u32[]{:S(2)}) copy-start(bf16[4,4,96,128]{3,2,1,0:T(8,128)(2,1)S(1)} %pad_maximum_fusion.mine_ref) | copy-start | bytes 1179652
  33.7 7.3 %collective-permute-start.5 = (bf16[4,4,96,128]{3,2,1,0:T(8,128)(2,1)S(1)}, bf16[4,4,96,128]{3,2,1,0:T(8,128)(2,1)S(1)}, u32[]{:S(2)}, u32[]{:S(2)}) collective-permute-start(bf16[4,4,96,128]{3,2,1,0:T(8,128)(2,1)S(1)} %pad_maximum_fusion.mine_ref), channel_id=1, source_target_pairs={{0,4},{4,0},{8,12},{12,8},{16,20},{20,16},{24,28},{28,24},{1,5},{5... | collective-permute-start | bytes 1179656 | tf_op jit(solution)/shard_map/ppermute | solution.py:109
  33.8 0.9 %copy-start = (bf16[4,256,256]{2,1,0:T(8,128)(2,1)}, bf16[4,256,256]{2,1,0:T(8,128)(2,1)S(1)}, u32[]{:S(2)}) copy-start(bf16[4,256,256]{2,1,0:T(8,128)(2,1)S(1)} %collective-permute-done.6.from_x_ref) | copy-start | bytes 1572868
  33.8 1.0 %copy-start.1 = (bf16[4,256,256]{2,1,0:T(8,128)(2,1)}, bf16[4,256,256]{2,1,0:T(8,128)(2,1)S(1)}, u32[]{:S(2)}) copy-start(bf16[4,256,256]{2,1,0:T(8,128)(2,1)S(1)} %collective-permute-done.7.from_y_ref) | copy-start | bytes 1572868
  34.8 0.8 %copy-start.4 = (bf16[4,4,96,128]{3,2,1,0:T(8,128)(2,1)}, bf16[4,4,96,128]{3,2,1,0:T(8,128)(2,1)S(1)}, u32[]{:S(2)}) copy-start(bf16[4,4,96,128]{3,2,1,0:T(8,128)(2,1)S(1)} %collective-permute-done.11.other_ref) | copy-start | bytes 1179652
  39.0 11.7 %collective-permute-start.12 = (f32[4,96,256]{2,1,0:T(8,128)}, f32[4,96,256]{2,1,0:T(8,128)S(1)}, u32[]{:S(2)}, u32[]{:S(2)}) collective-permute-start(f32[4,96,256]{2,1,0:T(8,128)} %get-tuple-element.13), channel_id=1, source_target_pairs={{0,2},{1,3},{2,0},{3,1},{4,6},{5,7},{6,4},{7,5},{8,10},{9,11},{10,... | collective-permute-start | bytes 1179656 | tf_op jit(solution)/shard_map/ppermute | solution.py:120
  40.5 11.4 %collective-permute-start.13 = (f32[4,96,256]{2,1,0:T(8,128)}, f32[4,96,256]{2,1,0:T(8,128)S(1)}, u32[]{:S(2)}, u32[]{:S(2)}) collective-permute-start(f32[4,96,256]{2,1,0:T(8,128)} %get-tuple-element.14), channel_id=1, source_target_pairs={{0,1},{1,0},{2,3},{3,2},{4,5},{5,4},{6,7},{7,6},{8,9},{9,8},{10,11... | collective-permute-start | bytes 1179656 | tf_op jit(solution)/shard_map/ppermute | solution.py:121
  41.0 10.9 %copy-start.5 = (bf16[4,4,96,128]{3,2,1,0:T(8,128)(2,1)}, bf16[4,4,96,128]{3,2,1,0:T(8,128)(2,1)S(1)}, u32[]{:S(2)}) copy-start(bf16[4,4,96,128]{3,2,1,0:T(8,128)(2,1)S(1)} %collective-permute-done.5.other_ref) | copy-start | bytes 1179652
  50.6 1.2 %copy-start.6 = (f32[4,96,256]{2,1,0:T(8,128)}, f32[4,96,256]{2,1,0:T(8,128)S(1)}, u32[]{:S(2)}) copy-start(f32[4,96,256]{2,1,0:T(8,128)S(1)} %collective-permute-done.12.sum_y_ref) | copy-start | bytes 1179652
  51.9 0.8 %copy-start.7 = (f32[4,96,256]{2,1,0:T(8,128)}, f32[4,96,256]{2,1,0:T(8,128)S(1)}, u32[]{:S(2)}) copy-start(f32[4,96,256]{2,1,0:T(8,128)S(1)} %collective-permute-done.13.sum_x_ref) | copy-start | bytes 1179652

commit v2 on v1

v2 whole, which is shorter than its diff:
```python
import functools

import jax
import jax.numpy as jnp
from jax import lax
from jax.experimental import pallas as pl
from jax.experimental.pallas import tpu as pltpu
from jax.sharding import PartitionSpec as P

VMEM = pltpu.VMEM
PARAMS = pltpu.CompilerParams(vmem_limit_bytes=16 << 20)
CHIPS = 4


def pack_kernel(halves, lam_ref, own_ref, to_x_ref, to_y_ref, turned):
    y, x = lax.axis_index("rep") // 2, lax.axis_index("rep") % 2
    rows = turned.shape[2]
    for kind in range(2):
        block = jnp.concatenate([lam_ref[kind * halves + h] for h in range(halves)], axis=0)
        flipped = block.T
        for quarter in range(4):
            turned[kind, quarter] = flipped[quarter * rows : (quarter + 1) * rows]
    ny, nx = 1 - y, 1 - x
    own_ref[0, 0] = turned[0, ny * 2 + x]
    own_ref[0, 1] = turned[1, y * 2 + nx]
    own_ref[1, 0] = turned[0, y * 2 + x]
    own_ref[1, 1] = turned[1, y * 2 + x]
    to_x_ref[0] = turned[0, ny * 2 + nx]
    to_x_ref[1] = turned[0, y * 2 + nx]
    to_y_ref[0] = turned[1, ny * 2 + nx]
    to_y_ref[1] = turned[1, ny * 2 + x]


def product_kernel(
    mine_ref, sibling_ref, one_ref, two_ref, three_ref, three_sibling_ref,
    near_x_ref, near_y_ref, from_x_ref, from_y_ref, first_ref, last_ref, pieces,
):
    spot = lax.axis_index("loop")
    z, core = spot // 2, spot % 2

    def block(back, of_core):
        return lax.rem(z - back + CHIPS, CHIPS) * 2 + of_core

    pieces[block(0, core)] = mine_ref[...]
    pieces[block(0, 1 - core)] = sibling_ref[...]
    pieces[block(3, core)] = three_ref[...]
    pieces[block(3, 1 - core)] = three_sibling_ref[...]
    held, other = 1 + core, 2 - core
    pieces[block(held, core)] = one_ref[0]
    pieces[block(held, 1 - core)] = one_ref[1]
    pieces[block(other, 1 - core)] = two_ref[0]
    pieces[block(other, core)] = two_ref[1]
    halves = from_x_ref.shape[0]
    depth = pieces.shape[3] // halves
    for kind, near_ref, far_ref, out_ref in ((0, near_x_ref, from_x_ref, first_ref), (1, near_y_ref, from_y_ref, last_ref)):
        near = [pieces[s, kind] for s in range(2 * CHIPS)]
        far = [pieces[s, 2 + kind] for s in range(2 * CHIPS)]
        for h in range(halves):
            cut = slice(h * depth, (h + 1) * depth)
            near_lam = jnp.concatenate([p[:, cut] for p in near], axis=1)
            far_lam = jnp.concatenate([p[:, cut] for p in far], axis=1)
            out_ref[h] = jnp.dot(near_lam, near_ref[h], preferred_element_type=jnp.float32) + jnp.dot(
                far_lam, far_ref[h], preferred_element_type=jnp.float32
            )


def total_kernel(first_ref, last_ref, sum_y_ref, sum_x_ref, out_ref):
    halves = first_ref.shape[0]
    out_ref[:halves] = (first_ref[...] + sum_y_ref[...]).astype(out_ref.dtype)
    out_ref[halves:] = (last_ref[...] + sum_x_ref[...]).astype(out_ref.dtype)


def square(lam, integrals, block_mask):
    irreps, occ, depth = lam.shape
    halves = irreps // 2
    rows = occ // 4
    columns = integrals.shape[2]
    loops = 2 * CHIPS
    over_x = [(r, r ^ 1) for r in range(4)]
    over_y = [(r, r ^ 2) for r in range(4)]
    over_core = [(s, s ^ 1) for s in range(loops)]
    by_three = [(s, (s + 6) % loops) for s in range(loops)]
    by_core = [(s, (s + 2 + 2 * (s % 2)) % loops) for s in range(loops)]
    bf16, f32 = jnp.bfloat16, jnp.float32
    lanes = halves * depth
    sums = jax.ShapeDtypeStruct((halves, rows, columns), f32)
    in_vmem = pl.BlockSpec(memory_space=VMEM)

    live = lax.dynamic_slice_in_dim(block_mask, lax.axis_index("loop"), 1, 1)[:, :, None] == 1
    masked = jnp.where(live, lam.transpose(0, 2, 1), jnp.zeros((), bf16))
    own, to_x, to_y = pl.pallas_call(
        functools.partial(pack_kernel, halves),
        out_shape=(
            jax.ShapeDtypeStruct((2, 2, rows, lanes), bf16),
            jax.ShapeDtypeStruct((2, rows, lanes), bf16),
            jax.ShapeDtypeStruct((2, rows, lanes), bf16),
        ),
        in_specs=[in_vmem],
        out_specs=[in_vmem] * 3,
        scratch_shapes=[VMEM((2, 4, rows, lanes), bf16)],
        compiler_params=PARAMS,
    )(masked)

    lam_x = lax.ppermute(to_x, "rep", over_x)
    lam_y = lax.ppermute(to_y, "rep", over_y)
    near_x, near_y = integrals[:halves], integrals[halves:]
    far_x = lax.ppermute(near_x, "rep", over_x)
    far_y = lax.ppermute(near_y, "rep", over_y)

    def product(parts, cost):
        return pl.pallas_call(
            product_kernel,
            out_shape=(sums, sums),
            in_specs=[in_vmem] * 10,
            out_specs=[in_vmem] * 2,
            scratch_shapes=[VMEM((loops, 4, rows, lanes), bf16)],
            cost_estimate=pl.CostEstimate(flops=cost, bytes_accessed=0, transcendentals=0),
            compiler_params=PARAMS,
        )(*parts, near_x, near_y, far_x, far_y)

    def gathered(mine):
        sibling = lax.ppermute(mine, "loop", over_core)
        three = lax.ppermute(mine, "loop", by_three)
        one = lax.ppermute(jnp.stack([mine, sibling]), "loop", by_core)
        return [mine, sibling, one, lax.ppermute(one, "loop", over_core), three, lax.ppermute(three, "loop", over_core)]

    sent = jnp.concatenate([own[0], lam_x[0][None], lam_y[0][None]], axis=0)
    kept = jnp.concatenate([own[1], lam_x[1][None], lam_y[1][None]], axis=0)
    sent_parts = gathered(sent)
    kept, sent_parts[SENT_FIRST] = lax.optimization_barrier((kept, sent_parts[SENT_FIRST]))
    kept_parts = gathered(kept)
    partial_y, partial_x = product(sent_parts, COST_SENT)
    sum_y = lax.ppermute(partial_y, "rep", over_y)
    sum_x = lax.ppermute(partial_x, "rep", over_x)
    kept_parts, partial_y = lax.optimization_barrier((kept_parts, partial_y))
    own_y, own_x = product(kept_parts, COST_KEPT)
    return pl.pallas_call(
        total_kernel,
        out_shape=jax.ShapeDtypeStruct((irreps, rows, columns), bf16),
        in_specs=[in_vmem] * 4,
        out_specs=in_vmem,
        compiler_params=PARAMS,
    )(own_y, own_x, sum_y, sum_x)


def general(lam, integrals, block_mask):
    live = jnp.repeat(block_mask, lam.shape[2], axis=1) == 1
    kept = jnp.where(live[:, :, None], integrals, jnp.zeros_like(integrals))
    layer_lam = lax.all_gather(lam, "loop", axis=2, tiled=True)
    partial_sum = jnp.einsum("hpk,hka->hpa", layer_lam, kept, preferred_element_type=jnp.float32)
    return lax.psum_scatter(partial_sum, "rep", scatter_dimension=1, tiled=True).astype(jnp.bfloat16)


SENT_FIRST, COST_SENT, COST_KEPT = 4, 0, 0


def solution(mesh):
    return jax.shard_map(
        square if (mesh.shape["rep"], mesh.shape["loop"]) == (4, 2 * CHIPS) else general,
        mesh=mesh,
        in_specs=(P(None, None, ("rep", "loop")), P(None, "rep", "loop"), P(None, "rep")),
        out_specs=P(None, "rep", "loop"),
        check_vma=False,
    )
```

time: 56.5 us -> 40.6 us (0.72)
  waiting for transfers between devices: 26.5 us -> 14.4 us
  Pallas kernels: 8.73 us -> 2.68 us
  starting transfers between devices: 16.1 us -> 21.1 us
  local copies, waits for them, and re-layouts: 4.65 us -> 0.09 us
  other arithmetic: 0.14 us -> 2.05 us
    ppermute x1, waiting for transfers between devices: 9.61 us -> 1.77 us  [square(): sum_y = lax.ppermute(partial_y, 'rep', over_y)]
    ppermute x10 -> x12, starting transfers between devices: 9.59 us -> 14.5 us  [the longest x2 5.17 us: gathered(): three = lax.ppermute(mine, 'loop', by_three)]
    pallas_call x2 -> x3, Pallas kernels: 7 us -> 2.57 us  [the longest x2 1.75 us: product(): pl.pallas_call(product_kernel, out_shape=(sums, sums), in_specs=[in_vmem]...]
    ppermute x10 -> x12, waiting for transfers between devices: 13.7 us -> 9.75 us  [the longest x2 6.35 us: gathered(): three = lax.ppermute(mine, 'loop', by_three)]
    unnamed x16 -> x2, local copies, waits for them, and re-layouts: 2.54 us -> 0.01 us
    pallas_call x1, Pallas kernels: 1.73 us -> 0.12 us  [square(): pl.pallas_call(functools.partial(pack_kernel, halves), out_shape=(jax.Sha...]
    slice x3, local copies, waits for them, and re-layouts: 1.28 us -> 0.08 us  [the longest x1 0.07 us: square(): near_x, near_y = (integrals[:halves], integrals[halves:])]
    select_n x0 -> x1, other arithmetic: none -> 1.02 us  [square(): masked = jnp.where(live, lam.transpose(0, 2, 1), jnp.zeros((), bf16))]
  transfers between devices with their start and end apart: 14 -> 16, of which waited for: 8 -> 9; matrix products, arithmetic and copies ran while one was open for 4% -> 0% of each run, Pallas kernels for 6% -> 4%
where the time goes in v2:
time: 40.6 us; the launch traced here: 40.4 us
  starting transfers between devices  21.1 us (52%)
  waiting for transfers between devices  14.4 us (35%)
  Pallas kernels  2.68 us (7%)
  other arithmetic  2.05 us (5%)
    ppermute x2, waiting for transfers between devices, gathered(): three = lax.ppermute(mine, 'loop', by_three)  6.35 us
    ppermute x2, starting transfers between devices, gathered(): three = lax.ppermute(mine, 'loop', by_three)  5.17 us
    ppermute x2, starting transfers between devices, gathered(): one = lax.ppermute(jnp.stack([mine, sibling]), 'loop', by_core)  4.66 us
    ppermute x1, starting transfers between devices, square(): lam_x = lax.ppermute(to_x, 'rep', over_x)  3 us
    ppermute x2, starting transfers between devices, gathered(): lax.ppermute(one, 'loop', over_core)  2.44 us
    ppermute x2, waiting for transfers between devices, gathered(): one = lax.ppermute(jnp.stack([mine, sibling]), 'loop', by_core)  2.09 us
    ppermute x1, waiting for transfers between devices, square(): lam_y = lax.ppermute(to_y, 'rep', over_y)  2.02 us
    ppermute x1, waiting for transfers between devices, square(): sum_y = lax.ppermute(partial_y, 'rep', over_y)  1.77 us
  transfers between devices with their start and end apart: 16, of which 9 were waited for; matrix products, arithmetic and copies ran while one was open for 0% of the time, Pallas kernels for 4%

profile of v2, /device:TPU:0, one launch (start us, length us, event | category | flops | bytes accessed | tf_op | source)
XLA Modules:
  0.0 40.4 jit_solution(7390835959243833137)
XLA Ops:
  0.0 0.0 copy-start
  0.0 1.0 %fusion = pred[8]{0:T(512)(128)(4,1)S(1)} fusion(s32[8,8]{1,0:T(8,128)} %param.5, s32[]{:T(128)S(6)} %select_n.9), kind=kLoop, calls=%fused_computation.8 | loop fusion | flops 8 | bytes 44 | tf_op jit(solution)/shard_map/eq | solution.py:89
  1.0 1.0 %select_bitcast_fusion.lam_ref = bf16[8,32,384]{2,1,0:T(8,128)(2,1)S(1)} fusion(bf16[8,384,32]{1,2,0:T(8,128)(2,1)} %param.3, pred[8]{0:T(512)(128)(4,1)S(1)} %fusion), kind=kLoop, calls=%fused_computation.2 | loop fusion | flops 98304 | bytes 393224 | tf_op jit(solution)/shard_map/jit(_where)/select_n | solution.py:90
  2.0 0.1 shard_map.37
  2.1 3.0 %collective-permute-start = (bf16[2,96,128]{2,1,0:T(8,128)(2,1)S(1)}, bf16[2,96,128]{2,1,0:T(8,128)(2,1)S(1)}, u32[]{:S(2)}, u32[]{:S(2)}) collective-permute-start(bf16[2,96,128]{2,1,0:T(8,128)(2,1)S(1)} %get-tuple-element.21), channel_id=1, source_target_pairs={{0,1},{1,0},{2,3},{3,2},{4,5},{5,4},{6,7},{7,6},{8,9},{9,8},{10,11... | collective-permute-start | bytes 147464 | tf_op jit(solution)/shard_map/ppermute | solution.py:104
  5.1 1.5 %collective-permute-start.1 = (bf16[2,96,128]{2,1,0:T(8,128)(2,1)S(1)}, bf16[2,96,128]{2,1,0:T(8,128)(2,1)S(1)}, u32[]{:S(2)}, u32[]{:S(2)}) collective-permute-start(bf16[2,96,128]{2,1,0:T(8,128)(2,1)S(1)} %get-tuple-element.22), channel_id=1, source_target_pairs={{0,2},{1,3},{2,0},{3,1},{4,6},{5,7},{6,4},{7,5},{8,10},{9,11},{10,... | collective-permute-start | bytes 147464 | tf_op jit(solution)/shard_map/ppermute | solution.py:105
  6.6 0.5 %collective-permute-done = bf16[2,96,128]{2,1,0:T(8,128)(2,1)S(1)} collective-permute-done((bf16[2,96,128]{2,1,0:T(8,128)(2,1)S(1)}, bf16[2,96,128]{2,1,0:T(8,128)(2,1)S(1)}, u32[]{:S(2)}, u32[]{:S(2)}) %collective-permute-start) | collective-permute-done | bytes 49184 | tf_op jit(solution)/shard_map/ppermute | solution.py:104
  7.2 2.0 %collective-permute-done.1 = bf16[2,96,128]{2,1,0:T(8,128)(2,1)S(1)} collective-permute-done((bf16[2,96,128]{2,1,0:T(8,128)(2,1)S(1)}, bf16[2,96,128]{2,1,0:T(8,128)(2,1)S(1)}, u32[]{:S(2)}, u32[]{:S(2)}) %collective-permute-start.1) | collective-permute-done | bytes 49184 | tf_op jit(solution)/shard_map/ppermute | solution.py:105
  9.2 0.1 collective-permute-start.8
  9.3 0.0 copy-done
  9.3 0.1 fusion.2
  9.4 1.6 %collective-permute-start.13 = (bf16[4,256,256]{2,1,0:T(8,128)(2,1)S(1)}, bf16[4,256,256]{2,1,0:T(8,128)(2,1)S(1)}, u32[]{:S(2)}, u32[]{:S(2)}) collective-permute-start(bf16[4,256,256]{2,1,0:T(8,128)(2,1)S(1)} %get-tuple-element.35.near_y_ref), channel_id=1, source_target_pairs={{0,2},{1,3},{2,0},{3,1},{4,6},{5,7},{6,4},{7,5},{8,10},{9,11},{10,... | collective-permute-start | bytes 1572872 | tf_op jit(solution)/shard_map/ppermute | solution.py:108
  11.0 0.5 %collective-permute-start.12 = (bf16[4,256,256]{2,1,0:T(8,128)(2,1)S(1)}, bf16[4,256,256]{2,1,0:T(8,128)(2,1)S(1)}, u32[]{:S(2)}, u32[]{:S(2)}) collective-permute-start(bf16[4,256,256]{2,1,0:T(8,128)(2,1)S(1)} %get-tuple-element.36.near_x_ref), channel_id=1, source_target_pairs={{0,1},{1,0},{2,3},{3,2},{4,5},{5,4},{6,7},{7,6},{8,9},{9,8},{10,11... | collective-permute-start | bytes 1572872 | tf_op jit(solution)/shard_map/ppermute | solution.py:107
  11.5 0.0 collective-permute-done.8.sibling_ref
  11.6 1.6 %collective-permute-start.9 = (bf16[2,4,96,128]{3,2,1,0:T(8,128)(2,1)S(1)}, bf16[2,4,96,128]{3,2,1,0:T(8,128)(2,1)S(1)}, u32[]{:S(2)}, u32[]{:S(2)}) collective-permute-start(bf16[2,4,96,128]{3,2,1,0:T(8,128)(2,1)S(1)} %pad_maximum_fusion.1), channel_id=1, source_target_pairs={{0,8},{4,20},{8,16},{12,28},{16,24},{20,4},{24,0},{28,12},{1,9},{5... | collective-permute-start | bytes 589832 | tf_op jit(solution)/shard_map/ppermute | solution.py:124
  13.2 2.2 %collective-permute-start.2 = (bf16[4,96,128]{2,1,0:T(8,128)(2,1)S(1)}, bf16[4,96,128]{2,1,0:T(8,128)(2,1)S(1)}, u32[]{:S(2)}, u32[]{:S(2)}) collective-permute-start(bf16[4,96,128]{2,1,0:T(8,128)(2,1)S(1)} %get-tuple-element.38.mine_ref), channel_id=1, source_target_pairs={{0,24},{4,28},{8,0},{12,4},{16,8},{20,12},{24,16},{28,20},{1,25},{... | collective-permute-start | bytes 294920 | tf_op jit(solution)/shard_map/ppermute | solution.py:123
  15.4 5.3 %collective-permute-done.2.three_ref = bf16[4,96,128]{2,1,0:T(8,128)(2,1)S(1)} collective-permute-done((bf16[4,96,128]{2,1,0:T(8,128)(2,1)S(1)}, bf16[4,96,128]{2,1,0:T(8,128)(2,1)S(1)}, u32[]{:S(2)}, u32[]{:S(2)}) %collective-permute-start.2) | collective-permute-done | bytes 98336 | tf_op jit(solution)/shard_map/ppermute | solution.py:123
  20.8 0.0 collective-permute-start.3
  20.8 0.4 %collective-permute-done.9.one_ref = bf16[2,4,96,128]{3,2,1,0:T(8,128)(2,1)S(1)} collective-permute-done((bf16[2,4,96,128]{3,2,1,0:T(8,128)(2,1)S(1)}, bf16[2,4,96,128]{3,2,1,0:T(8,128)(2,1)S(1)}, u32[]{:S(2)}, u32[]{:S(2)}) %collective-permute-start.9) | collective-permute-done | bytes 196640 | tf_op jit(solution)/shard_map/ppermute | solution.py:124
  21.2 0.9 %collective-permute-start.10 = (bf16[2,4,96,128]{3,2,1,0:T(8,128)(2,1)S(1)}, bf16[2,4,96,128]{3,2,1,0:T(8,128)(2,1)S(1)}, u32[]{:S(2)}, u32[]{:S(2)}) collective-permute-start(bf16[2,4,96,128]{3,2,1,0:T(8,128)(2,1)S(1)} %collective-permute-done.9.one_ref), channel_id=1, source_target_pairs={{0,4},{4,0},{8,12},{12,8},{16,20},{20,16},{24,28},{28,24},{1,5},{5... | collective-permute-start | bytes 589832 | tf_op jit(solution)/shard_map/ppermute | solution.py:125
  22.1 0.0 collective-permute-start.11
  22.1 0.0 collective-permute-done.3.sibling_ref
  22.1 3.0 %collective-permute-start.4 = (bf16[2,4,96,128]{3,2,1,0:T(8,128)(2,1)S(1)}, bf16[2,4,96,128]{3,2,1,0:T(8,128)(2,1)S(1)}, u32[]{:S(2)}, u32[]{:S(2)}) collective-permute-start(bf16[2,4,96,128]{3,2,1,0:T(8,128)(2,1)S(1)} %pad_maximum_fusion), channel_id=1, source_target_pairs={{0,8},{4,20},{8,16},{12,28},{16,24},{20,4},{24,0},{28,12},{1,9},{5... | collective-permute-start | bytes 589832 | tf_op jit(solution)/shard_map/ppermute | solution.py:124
  25.1 0.0 collective-permute-done.11.three_sibling_ref
  25.2 0.0 collective-permute-done.13.from_y_ref
  25.2 0.0 collective-permute-done.12.from_x_ref
  25.2 0.0 collective-permute-done.10.two_ref
  25.2 0.9 %shard_map.38 = (f32[4,96,256]{2,1,0:T(8,128)S(1)}, f32[4,96,256]{2,1,0:T(8,128)S(1)}) custom-call(bf16[4,96,128]{2,1,0:T(8,128)(2,1)S(1)} %get-tuple-element.38.mine_ref, bf16[4,96,128]{2,1,0:T(8,128)(2,1)S(1)} %collective-permute-done.8.sibling_ref, bf16[2,4,96,128]{3,2,1,0:T(8,128)(2,1)S(1)} %collective-permute-done.9.one_ref, ...), custom_call_target="tpu_custom_call" | custom-call | tf_op jit(solution)/shard_map/pallas_call | solution.py:111
  26.1 1.5 %collective-permute-start.15 = (f32[4,96,256]{2,1,0:T(8,128)S(1)}, f32[4,96,256]{2,1,0:T(8,128)S(1)}, u32[]{:S(2)}, u32[]{:S(2)}) collective-permute-start(f32[4,96,256]{2,1,0:T(8,128)S(1)} %get-tuple-element.34), channel_id=1, source_target_pairs={{0,1},{1,0},{2,3},{3,2},{4,5},{5,4},{6,7},{7,6},{8,9},{9,8},{10,11... | collective-permute-start | bytes 1179656 | tf_op jit(solution)/shard_map/ppermute | solution.py:134
  27.6 0.5 %collective-permute-start.14 = (f32[4,96,256]{2,1,0:T(8,128)S(1)}, f32[4,96,256]{2,1,0:T(8,128)S(1)}, u32[]{:S(2)}, u32[]{:S(2)}) collective-permute-start(f32[4,96,256]{2,1,0:T(8,128)S(1)} %get-tuple-element.25), channel_id=1, source_target_pairs={{0,2},{1,3},{2,0},{3,1},{4,6},{5,7},{6,4},{7,5},{8,10},{9,11},{10,... | collective-permute-start | bytes 1179656 | tf_op jit(solution)/shard_map/ppermute | solution.py:133
  28.1 2.9 %collective-permute-start.6 = (bf16[4,96,128]{2,1,0:T(8,128)(2,1)S(1)}, bf16[4,96,128]{2,1,0:T(8,128)(2,1)S(1)}, u32[]{:S(2)}, u32[]{:S(2)}) collective-permute-start(bf16[4,96,128]{2,1,0:T(8,128)(2,1)S(1)} %pad_maximum_fusion.2.mine_ref), channel_id=1, source_target_pairs={{0,24},{4,28},{8,0},{12,4},{16,8},{20,12},{24,16},{28,20},{1,25},{... | collective-permute-start | bytes 294920 | tf_op jit(solution)/shard_map/ppermute | solution.py:123
  31.0 1.7 %collective-permute-done.4.one_ref = bf16[2,4,96,128]{3,2,1,0:T(8,128)(2,1)S(1)} collective-permute-done((bf16[2,4,96,128]{3,2,1,0:T(8,128)(2,1)S(1)}, bf16[2,4,96,128]{3,2,1,0:T(8,128)(2,1)S(1)}, u32[]{:S(2)}, u32[]{:S(2)}) %collective-permute-start.4) | collective-permute-done | bytes 196640 | tf_op jit(solution)/shard_map/ppermute | solution.py:124
  32.7 1.6 %collective-permute-start.5 = (bf16[2,4,96,128]{3,2,1,0:T(8,128)(2,1)S(1)}, bf16[2,4,96,128]{3,2,1,0:T(8,128)(2,1)S(1)}, u32[]{:S(2)}, u32[]{:S(2)}) collective-permute-start(bf16[2,4,96,128]{3,2,1,0:T(8,128)(2,1)S(1)} %collective-permute-done.4.one_ref), channel_id=1, source_target_pairs={{0,4},{4,0},{8,12},{12,8},{16,20},{20,16},{24,28},{28,24},{1,5},{5... | collective-permute-start | bytes 589832 | tf_op jit(solution)/shard_map/ppermute | solution.py:125
  34.3 1.0 %collective-permute-done.6.three_ref = bf16[4,96,128]{2,1,0:T(8,128)(2,1)S(1)} collective-permute-done((bf16[4,96,128]{2,1,0:T(8,128)(2,1)S(1)}, bf16[4,96,128]{2,1,0:T(8,128)(2,1)S(1)}, u32[]{:S(2)}, u32[]{:S(2)}) %collective-permute-start.6) | collective-permute-done | bytes 98336 | tf_op jit(solution)/shard_map/ppermute | solution.py:123
  35.3 0.0 collective-permute-start.7
  35.3 1.3 %collective-permute-done.7.three_sibling_ref = bf16[4,96,128]{2,1,0:T(8,128)(2,1)S(1)} collective-permute-done((bf16[4,96,128]{2,1,0:T(8,128)(2,1)S(1)}, bf16[4,96,128]{2,1,0:T(8,128)(2,1)S(1)}, u32[]{:S(2)}, u32[]{:S(2)}) %collective-permute-start.7) | collective-permute-done | bytes 98336 | tf_op jit(solution)/shard_map/ppermute | solution.py:125
  36.6 0.0 collective-permute-done.5.two_ref
  36.6 0.9 %shard_map.39 = (f32[4,96,256]{2,1,0:T(8,128)S(1)}, f32[4,96,256]{2,1,0:T(8,128)S(1)}) custom-call(bf16[4,96,128]{2,1,0:T(8,128)(2,1)S(1)} %pad_maximum_fusion.2.mine_ref, bf16[4,96,128]{2,1,0:T(8,128)(2,1)S(1)} %collective-permute-done.3.sibling_ref, bf16[2,4,96,128]{3,2,1,0:T(8,128)(2,1)S(1)} %collective-permute-done.4.one_ref, ...), custom_call_target="tpu_custom_call" | custom-call | tf_op jit(solution)/shard_map/pallas_call | solution.py:111
  37.5 0.4 collective-permute-done.15.sum_x_ref
  37.8 1.8 %collective-permute-done.14.sum_y_ref = f32[4,96,256]{2,1,0:T(8,128)S(1)} collective-permute-done((f32[4,96,256]{2,1,0:T(8,128)S(1)}, f32[4,96,256]{2,1,0:T(8,128)S(1)}, u32[]{:S(2)}, u32[]{:S(2)}) %collective-permute-start.14) | collective-permute-done | bytes 393248 | tf_op jit(solution)/shard_map/ppermute | solution.py:133
  39.6 0.8 %shard_map.40 = bf16[8,96,256]{2,1,0:T(8,128)(2,1)} custom-call(f32[4,96,256]{2,1,0:T(8,128)S(1)} %get-tuple-element.32.first_ref, f32[4,96,256]{2,1,0:T(8,128)S(1)} %get-tuple-element.33.last_ref, f32[4,96,256]{2,1,0:T(8,128)S(1)} %collective-permute-done.14.sum_y_ref, f32[4,96,256]{2,1,0:T(8,128)S(1)} %collective-permute-done.15.sum_x_ref), custom_call_target="tpu_custom_call" | custom-call | tf_op jit(solution)/shard_map/pallas_call | solution.py:137
  (7 shorter events, 0.1 us)
Async XLA Ops:
  0.0 9.3 %copy-start = (bf16[8,256,256]{2,1,0:T(8,128)(2,1)S(1)}, bf16[8,256,256]{2,1,0:T(8,128)(2,1)}, u32[]{:S(2)}) copy-start(bf16[8,256,256]{2,1,0:T(8,128)(2,1)} %param.4) | copy-start | bytes 3145732
  2.1 5.1 %collective-permute-start = (bf16[2,96,128]{2,1,0:T(8,128)(2,1)S(1)}, bf16[2,96,128]{2,1,0:T(8,128)(2,1)S(1)}, u32[]{:S(2)}, u32[]{:S(2)}) collective-permute-start(bf16[2,96,128]{2,1,0:T(8,128)(2,1)S(1)} %get-tuple-element.21), channel_id=1, source_target_pairs={{0,1},{1,0},{2,3},{3,2},{4,5},{5,4},{6,7},{7,6},{8,9},{9,8},{10,11... | collective-permute-start | bytes 147464 | tf_op jit(solution)/shard_map/ppermute | solution.py:104
  5.1 4.1 %collective-permute-start.1 = (bf16[2,96,128]{2,1,0:T(8,128)(2,1)S(1)}, bf16[2,96,128]{2,1,0:T(8,128)(2,1)S(1)}, u32[]{:S(2)}, u32[]{:S(2)}) collective-permute-start(bf16[2,96,128]{2,1,0:T(8,128)(2,1)S(1)} %get-tuple-element.22), channel_id=1, source_target_pairs={{0,2},{1,3},{2,0},{3,1},{4,6},{5,7},{6,4},{7,5},{8,10},{9,11},{10,... | collective-permute-start | bytes 147464 | tf_op jit(solution)/shard_map/ppermute | solution.py:105
  9.2 2.3 %collective-permute-start.8 = (bf16[4,96,128]{2,1,0:T(8,128)(2,1)S(1)}, bf16[4,96,128]{2,1,0:T(8,128)(2,1)S(1)}, u32[]{:S(2)}, u32[]{:S(2)}) collective-permute-start(bf16[4,96,128]{2,1,0:T(8,128)(2,1)S(1)} %get-tuple-element.38.mine_ref), channel_id=1, source_target_pairs={{0,4},{4,0},{8,12},{12,8},{16,20},{20,16},{24,28},{28,24},{1,5},{5... | collective-permute-start | bytes 294920 | tf_op jit(solution)/shard_map/ppermute | solution.py:122
  9.4 15.8 %collective-permute-start.13 = (bf16[4,256,256]{2,1,0:T(8,128)(2,1)S(1)}, bf16[4,256,256]{2,1,0:T(8,128)(2,1)S(1)}, u32[]{:S(2)}, u32[]{:S(2)}) collective-permute-start(bf16[4,256,256]{2,1,0:T(8,128)(2,1)S(1)} %get-tuple-element.35.near_y_ref), channel_id=1, source_target_pairs={{0,2},{1,3},{2,0},{3,1},{4,6},{5,7},{6,4},{7,5},{8,10},{9,11},{10,... | collective-permute-start | bytes 1572872 | tf_op jit(solution)/shard_map/ppermute | solution.py:108
  11.0 14.2 %collective-permute-start.12 = (bf16[4,256,256]{2,1,0:T(8,128)(2,1)S(1)}, bf16[4,256,256]{2,1,0:T(8,128)(2,1)S(1)}, u32[]{:S(2)}, u32[]{:S(2)}) collective-permute-start(bf16[4,256,256]{2,1,0:T(8,128)(2,1)S(1)} %get-tuple-element.36.near_x_ref), channel_id=1, source_target_pairs={{0,1},{1,0},{2,3},{3,2},{4,5},{5,4},{6,7},{7,6},{8,9},{9,8},{10,11... | collective-permute-start | bytes 1572872 | tf_op jit(solution)/shard_map/ppermute | solution.py:107
  11.6 9.7 %collective-permute-start.9 = (bf16[2,4,96,128]{3,2,1,0:T(8,128)(2,1)S(1)}, bf16[2,4,96,128]{3,2,1,0:T(8,128)(2,1)S(1)}, u32[]{:S(2)}, u32[]{:S(2)}) collective-permute-start(bf16[2,4,96,128]{3,2,1,0:T(8,128)(2,1)S(1)} %pad_maximum_fusion.1), channel_id=1, source_target_pairs={{0,8},{4,20},{8,16},{12,28},{16,24},{20,4},{24,0},{28,12},{1,9},{5... | collective-permute-start | bytes 589832 | tf_op jit(solution)/shard_map/ppermute | solution.py:124
  13.2 7.6 %collective-permute-start.2 = (bf16[4,96,128]{2,1,0:T(8,128)(2,1)S(1)}, bf16[4,96,128]{2,1,0:T(8,128)(2,1)S(1)}, u32[]{:S(2)}, u32[]{:S(2)}) collective-permute-start(bf16[4,96,128]{2,1,0:T(8,128)(2,1)S(1)} %get-tuple-element.38.mine_ref), channel_id=1, source_target_pairs={{0,24},{4,28},{8,0},{12,4},{16,8},{20,12},{24,16},{28,20},{1,25},{... | collective-permute-start | bytes 294920 | tf_op jit(solution)/shard_map/ppermute | solution.py:123
  20.8 1.3 %collective-permute-start.3 = (bf16[4,96,128]{2,1,0:T(8,128)(2,1)S(1)}, bf16[4,96,128]{2,1,0:T(8,128)(2,1)S(1)}, u32[]{:S(2)}, u32[]{:S(2)}) collective-permute-start(bf16[4,96,128]{2,1,0:T(8,128)(2,1)S(1)} %pad_maximum_fusion.2.mine_ref), channel_id=1, source_target_pairs={{0,4},{4,0},{8,12},{12,8},{16,20},{20,16},{24,28},{28,24},{1,5},{5... | collective-permute-start | bytes 294920 | tf_op jit(solution)/shard_map/ppermute | solution.py:122
  21.2 4.0 %collective-permute-start.10 = (bf16[2,4,96,128]{3,2,1,0:T(8,128)(2,1)S(1)}, bf16[2,4,96,128]{3,2,1,0:T(8,128)(2,1)S(1)}, u32[]{:S(2)}, u32[]{:S(2)}) collective-permute-start(bf16[2,4,96,128]{3,2,1,0:T(8,128)(2,1)S(1)} %collective-permute-done.9.one_ref), channel_id=1, source_target_pairs={{0,4},{4,0},{8,12},{12,8},{16,20},{20,16},{24,28},{28,24},{1,5},{5... | collective-permute-start | bytes 589832 | tf_op jit(solution)/shard_map/ppermute | solution.py:125
  22.1 3.1 %collective-permute-start.11 = (bf16[4,96,128]{2,1,0:T(8,128)(2,1)S(1)}, bf16[4,96,128]{2,1,0:T(8,128)(2,1)S(1)}, u32[]{:S(2)}, u32[]{:S(2)}) collective-permute-start(bf16[4,96,128]{2,1,0:T(8,128)(2,1)S(1)} %collective-permute-done.2.three_ref), channel_id=1, source_target_pairs={{0,4},{4,0},{8,12},{12,8},{16,20},{20,16},{24,28},{28,24},{1,5},{5... | collective-permute-start | bytes 294920 | tf_op jit(solution)/shard_map/ppermute | solution.py:125
  22.1 10.6 %collective-permute-start.4 = (bf16[2,4,96,128]{3,2,1,0:T(8,128)(2,1)S(1)}, bf16[2,4,96,128]{3,2,1,0:T(8,128)(2,1)S(1)}, u32[]{:S(2)}, u32[]{:S(2)}) collective-permute-start(bf16[2,4,96,128]{3,2,1,0:T(8,128)(2,1)S(1)} %pad_maximum_fusion), channel_id=1, source_target_pairs={{0,8},{4,20},{8,16},{12,28},{16,24},{20,4},{24,0},{28,12},{1,9},{5... | collective-permute-start | bytes 589832 | tf_op jit(solution)/shard_map/ppermute | solution.py:124
  26.1 11.8 %collective-permute-start.15 = (f32[4,96,256]{2,1,0:T(8,128)S(1)}, f32[4,96,256]{2,1,0:T(8,128)S(1)}, u32[]{:S(2)}, u32[]{:S(2)}) collective-permute-start(f32[4,96,256]{2,1,0:T(8,128)S(1)} %get-tuple-element.34), channel_id=1, source_target_pairs={{0,1},{1,0},{2,3},{3,2},{4,5},{5,4},{6,7},{7,6},{8,9},{9,8},{10,11... | collective-permute-start | bytes 1179656 | tf_op jit(solution)/shard_map/ppermute | solution.py:134
  27.6 12.0 %collective-permute-start.14 = (f32[4,96,256]{2,1,0:T(8,128)S(1)}, f32[4,96,256]{2,1,0:T(8,128)S(1)}, u32[]{:S(2)}, u32[]{:S(2)}) collective-permute-start(f32[4,96,256]{2,1,0:T(8,128)S(1)} %get-tuple-element.25), channel_id=1, source_target_pairs={{0,2},{1,3},{2,0},{3,1},{4,6},{5,7},{6,4},{7,5},{8,10},{9,11},{10,... | collective-permute-start | bytes 1179656 | tf_op jit(solution)/shard_map/ppermute | solution.py:133
  28.1 7.2 %collective-permute-start.6 = (bf16[4,96,128]{2,1,0:T(8,128)(2,1)S(1)}, bf16[4,96,128]{2,1,0:T(8,128)(2,1)S(1)}, u32[]{:S(2)}, u32[]{:S(2)}) collective-permute-start(bf16[4,96,128]{2,1,0:T(8,128)(2,1)S(1)} %pad_maximum_fusion.2.mine_ref), channel_id=1, source_target_pairs={{0,24},{4,28},{8,0},{12,4},{16,8},{20,12},{24,16},{28,20},{1,25},{... | collective-permute-start | bytes 294920 | tf_op jit(solution)/shard_map/ppermute | solution.py:123
  32.7 3.9 %collective-permute-start.5 = (bf16[2,4,96,128]{3,2,1,0:T(8,128)(2,1)S(1)}, bf16[2,4,96,128]{3,2,1,0:T(8,128)(2,1)S(1)}, u32[]{:S(2)}, u32[]{:S(2)}) collective-permute-start(bf16[2,4,96,128]{3,2,1,0:T(8,128)(2,1)S(1)} %collective-permute-done.4.one_ref), channel_id=1, source_target_pairs={{0,4},{4,0},{8,12},{12,8},{16,20},{20,16},{24,28},{28,24},{1,5},{5... | collective-permute-start | bytes 589832 | tf_op jit(solution)/shard_map/ppermute | solution.py:125
  35.3 1.3 %collective-permute-start.7 = (bf16[4,96,128]{2,1,0:T(8,128)(2,1)S(1)}, bf16[4,96,128]{2,1,0:T(8,128)(2,1)S(1)}, u32[]{:S(2)}, u32[]{:S(2)}) collective-permute-start(bf16[4,96,128]{2,1,0:T(8,128)(2,1)S(1)} %collective-permute-done.6.three_ref), channel_id=1, source_target_pairs={{0,4},{4,0},{8,12},{12,8},{16,20},{20,16},{24,28},{28,24},{1,5},{5... | collective-permute-start | bytes 294920 | tf_op jit(solution)/shard_map/ppermute | solution.py:125

commit v3 on v0

v3 whole, which is shorter than its diff:
```python
import functools

import jax
import jax.numpy as jnp
from jax import lax
from jax.experimental import pallas as pl
from jax.experimental.pallas import tpu as pltpu
from jax.sharding import PartitionSpec as P

VMEM = pltpu.VMEM
ALONE, BY_CORE = 3, (1, 2)
PARAMS = pltpu.CompilerParams(vmem_limit_bytes=16 << 20)
CHIPS = 4
COST_PACK, COST_JOIN, COST_SENT, COST_KEPT, TIES, CUT_SENT, CUT_KEPT, KTIE, OTIE = 2 * 10**9, 2 * 10**9, 0, 0, 2, 1, 1, 0, 1


def cost(flops):
    return pl.CostEstimate(flops=flops, bytes_accessed=0, transcendentals=0)


def swap(array, pairs, scope):
    with jax.named_scope(scope):
        return lax.ppermute(array, ("loop", "rep"), pairs)


def position():
    rep, spot = lax.axis_index("rep"), lax.axis_index("loop")
    return rep // 2, rep % 2, spot // 2, spot % 2


def pack_kernel(halves, lam_ref, mine_ref, other_ref, to_mine_ref, to_other_ref, turned):
    y, x, _, core = position()
    rows = turned.shape[2]
    for kind in range(2):
        block = jnp.concatenate([lam_ref[kind * halves + h] for h in range(halves)], axis=0)
        flipped = block.T
        for quarter in range(4):
            turned[kind, quarter] = flipped[quarter * rows : (quarter + 1) * rows]
    kept, over_x, over_y, over_both = y * 2 + x, y * 2 + 1 - x, (1 - y) * 2 + x, (1 - y) * 2 + 1 - x
    for kind, own_ref, to_ref in ((core, mine_ref, to_mine_ref), (1 - core, other_ref, to_other_ref)):
        summed, fetched = jnp.where(kind == 0, over_y, over_x), jnp.where(kind == 0, over_x, over_y)
        own_ref[0] = turned[kind, summed]
        own_ref[1] = turned[kind, kept]
        to_ref[0] = turned[kind, over_both]
        to_ref[1] = turned[kind, fetched]


def split_kernel(mask_ref, integrals_ref, _, mine_ref, other_ref):
    irreps, blocks = mask_ref.shape
    halves = irreps // 2
    rows = integrals_ref.shape[1] // blocks
    core = position()[3]
    for kind, out_ref in ((core, mine_ref), (1 - core, other_ref)):
        for h in range(halves):
            for b in range(blocks):
                part = integrals_ref[kind * halves + h, b * rows : (b + 1) * rows]
                live = mask_ref[kind * halves + h, b] == 1
                out_ref[h, b * rows : (b + 1) * rows] = jnp.where(live, part, jnp.zeros_like(part))


def join_kernel(mine_ref, other_ref, far_mine_ref, far_other_ref, sent_ref, kept_ref):
    for which, out_ref in enumerate((sent_ref, kept_ref)):
        for slot, ref in enumerate((mine_ref, other_ref, far_mine_ref, far_other_ref)):
            out_ref[slot] = ref[which]


def product_kernel(
    own_ref, sibling_ref, one_ref, two_ref, alone_ref, alone_sibling_ref,
    near_ref, near_other_ref, far_ref, far_other_ref, out_ref, out_other_ref, pieces,
):
    _, _, z, core = position()

    def place(message, back, from_sibling):
        block = (z ^ back) * 2 + (1 - core if from_sibling else core)
        for layer in range(2):
            for kind in range(2):
                pieces[layer, kind, block] = message[2 * layer + (1 - kind if from_sibling else kind)]

    held = jnp.where(core == 0, BY_CORE[0], BY_CORE[1])
    passed = jnp.where(core == 0, BY_CORE[1], BY_CORE[0])
    place(own_ref[...], 0, False)
    place(sibling_ref[...], 0, True)
    place(alone_ref[...], ALONE, False)
    place(alone_sibling_ref[...], ALONE, True)
    place(one_ref[0], held, False)
    place(one_ref[1], held, True)
    place(two_ref[0], passed, True)
    place(two_ref[1], passed, False)
    halves = near_ref.shape[0]
    depth = pieces.shape[4] // halves
    for kind, (near, far, out) in enumerate(((near_ref, far_ref, out_ref), (near_other_ref, far_other_ref, out_other_ref))):
        parts = [[pieces[layer, kind, s] for s in range(2 * CHIPS)] for layer in range(2)]
        for h in range(halves):
            cut = slice(h * depth, (h + 1) * depth)
            near_lam, far_lam = (jnp.concatenate([p[:, cut] for p in parts[layer]], axis=1) for layer in range(2))
            out[h] = jnp.dot(near_lam, near[h], preferred_element_type=jnp.float32) + jnp.dot(
                far_lam, far[h], preferred_element_type=jnp.float32
            )


def total_kernel(mine_ref, other_ref, sum_mine_ref, sum_other_ref, out_ref):
    halves = mine_ref.shape[0]
    core = position()[3]
    out_ref[pl.ds(core * halves, halves)] = (mine_ref[...] + sum_mine_ref[...]).astype(out_ref.dtype)
    out_ref[pl.ds((1 - core) * halves, halves)] = (other_ref[...] + sum_other_ref[...]).astype(out_ref.dtype)


def square(lam, integrals, block_mask):
    irreps, occ, depth = lam.shape
    halves = irreps // 2
    rows = occ // 4
    columns = integrals.shape[2]
    loops = 2 * CHIPS
    bf16, f32 = jnp.bfloat16, jnp.float32
    lanes = halves * depth
    in_vmem = pl.BlockSpec(memory_space=VMEM)
    quarters = jax.ShapeDtypeStruct((2, rows, lanes), bf16)
    half = jax.ShapeDtypeStruct((halves,) + integrals.shape[1:], bf16)
    sums = jax.ShapeDtypeStruct((halves, rows, columns), f32)

    def pairs(aim):
        places = [(s, r) for s in range(loops) for r in range(4)]
        return [(at, places.index(aim(s, r, s % 2))) for at, (s, r) in enumerate(places)]

    over_core = pairs(lambda s, r, core: (s ^ 1, r))
    fetch = pairs(lambda s, r, core: (s, r ^ (1 + core)))
    reduce = pairs(lambda s, r, core: (s, r ^ (2 - core)))
    by_three = pairs(lambda s, r, core: (s ^ (2 * ALONE), r))
    by_core = pairs(lambda s, r, core: (s ^ (2 * BY_CORE[core]), r))

    mine, other, to_mine, to_other = pl.pallas_call(
        functools.partial(pack_kernel, halves),
        out_shape=[quarters] * 4,
        in_specs=[in_vmem],
        out_specs=[in_vmem] * 4,
        scratch_shapes=[VMEM((2, 4, rows, lanes), bf16)],
        cost_estimate=cost(COST_PACK),
        compiler_params=PARAMS,
    )(lam.transpose(0, 2, 1))
    far_mine = swap(to_mine, fetch, "lam_mine")
    far_other = swap(to_other, reduce, "lam_other")

    near, near_other = pl.pallas_call(
        split_kernel,
        out_shape=[half] * 2,
        in_specs=[pl.BlockSpec(memory_space=pltpu.SMEM), in_vmem, pl.BlockSpec(memory_space=pl.ANY)],
        out_specs=[in_vmem] * 2,
        compiler_params=PARAMS,
    )(block_mask, integrals, to_mine)
    far = swap(near, fetch, "integrals_mine")
    far_other_integrals = swap(near_other, reduce, "integrals_other")

    starts = pl.pallas_call(
        join_kernel,
        out_shape=[jax.ShapeDtypeStruct((4, rows, lanes), bf16)] * 2,
        in_specs=[in_vmem] * 4,
        out_specs=[in_vmem] * 2,
        cost_estimate=cost(COST_JOIN),
        compiler_params=PARAMS,
    )(mine, other, far_mine, far_other)

    def gathered(which, name):
        own = starts[which]
        sibling = swap(own, over_core, name + "_own_over_core")
        return own, sibling, swap(own, by_three, name + "_by_three")

    def with_core(parts, name):
        own, sibling, three = parts
        return [own, sibling, swap(jnp.stack([own, sibling]), by_core, name + "_by_core"), three]

    def exchanged(parts, name):
        own, sibling, one, three = parts
        three_sibling = swap(three, over_core, name + "_three_over_core")
        if name == "sent":
            one, three_sibling = lax.optimization_barrier((one, three_sibling))
        cut = CUT_SENT if name == "sent" else CUT_KEPT
        two = jnp.concatenate([swap(part, over_core, name + "_one_over_core") for part in jnp.split(one, cut, axis=1)], axis=1)
        return [own, sibling, one, two, three, three_sibling]

    def product(parts, flops):
        return pl.pallas_call(
            product_kernel,
            out_shape=[sums] * 2,
            in_specs=[in_vmem] * 10,
            out_specs=[in_vmem] * 2,
            scratch_shapes=[VMEM((2, 2, loops, rows, lanes), bf16)],
            cost_estimate=cost(flops),
            compiler_params=PARAMS,
        )(*parts, near, near_other, far, far_other_integrals)

    sent_parts = gathered(0, "sent")
    kept_own, kept_sibling, kept_three = gathered(1, "kept")
    sent_parts = with_core(sent_parts, "sent")
    if OTIE == 1:
        sent_parts[3], kept_sibling = lax.optimization_barrier((sent_parts[3], kept_sibling))
    if KTIE == 1:
        sent_parts[2], kept_three = lax.optimization_barrier((sent_parts[2], kept_three))
    kept_parts = with_core((kept_own, kept_sibling, kept_three), "kept")
    if TIES == 1:
        sent_parts[2], far, far_other_integrals = lax.optimization_barrier((sent_parts[2], far, far_other_integrals))
    if TIES == 2:
        sent_parts[3], far, far_other_integrals = lax.optimization_barrier((sent_parts[3], far, far_other_integrals))
    sent, sent_other = product(exchanged(sent_parts, "sent"), COST_SENT)
    sum_mine = swap(sent, reduce, "sums_mine")
    sum_other = swap(sent_other, fetch, "sums_other")
    kept_parts, sent = lax.optimization_barrier((kept_parts, sent))
    kept, kept_other = product(exchanged(kept_parts, "kept"), COST_KEPT)
    return pl.pallas_call(
        total_kernel,
        out_shape=jax.ShapeDtypeStruct((irreps, rows, columns), bf16),
        in_specs=[in_vmem] * 4,
        out_specs=in_vmem,
        compiler_params=PARAMS,
    )(kept, kept_other, sum_mine, sum_other)


def general(lam, integrals, block_mask):
    live = jnp.repeat(block_mask, lam.shape[2], axis=1) == 1
    kept = jnp.where(live[:, :, None], integrals, jnp.zeros_like(integrals))
    layer_lam = lax.all_gather(lam, "loop", axis=2, tiled=True)
    partial_sum = jnp.einsum("hpk,hka->hpa", layer_lam, kept, preferred_element_type=jnp.float32)
    return lax.psum_scatter(partial_sum, "rep", scatter_dimension=1, tiled=True).astype(jnp.bfloat16)


def solution(mesh):
    return jax.shard_map(
        square if (mesh.shape["rep"], mesh.shape["loop"]) == (4, 2 * CHIPS) else general,
        mesh=mesh,
        in_specs=(P(None, None, ("rep", "loop")), P(None, "rep", "loop"), P(None, "rep")),
        out_specs=P(None, "rep", "loop"),
        check_vma=False,
    )
```

time: 159 us -> 36.9 us (0.23)
  blocking collectives: 111 us -> 0 us
  starting transfers between devices: 0.01 us -> 17.2 us
  waiting for transfers between devices: 29.3 us -> 15 us
  between operations: 13.4 us -> 0.07 us
  Pallas kernels: 0 us -> 3.45 us
  matrix products: 2.67 us -> 0 us
    psum x1 -> x0, blocking collectives: 111 us -> none  [per_device(): summed = lax.psum(partial_sum, 'rep')]
    all_gather x1 -> x0, waiting for transfers between devices: 28.6 us -> none  [per_device(): layer_lam = lax.all_gather(lam, 'loop', axis=2, tiled=True)]
    ppermute x0 -> x16, starting transfers between devices: none -> 17.2 us  [swap(): return lax.ppermute(array, ('loop', 'rep'), pairs)]
    ppermute x0 -> x16, waiting for transfers between devices: none -> 15 us  [swap(): return lax.ppermute(array, ('loop', 'rep'), pairs)]
    pallas_call x0 -> x6, Pallas kernels: none -> 3.45 us  [the longest x2 1.75 us: product(): pl.pallas_call(product_kernel, out_shape=[sums] * 2, in_specs=[in_vmem] *...]
    dot_general x1 -> x0, matrix products: 2.67 us -> none  [per_device(): jnp.einsum('hpk,hka->hpa', layer_lam, kept, preferred_element_type=jnp.fl...]
    convert_element_type x1 -> x0, local copies, waits for them, and re-layouts: 1.77 us -> none  [per_device(): return result.astype(jnp.bfloat16)]
  transfers between devices with their start and end apart: 1 -> 16, of which waited for: 1 -> 8; matrix products, arithmetic and copies ran while one was open for 1% -> 0% of each run, Pallas kernels for 0% -> 7%
where the time goes in v3:
time: 36.9 us; the launch traced here: 36.7 us
  starting transfers between devices  17.2 us (47%)
  waiting for transfers between devices  15 us (41%)
  Pallas kernels  3.45 us (9%)
  local copies, waits for them, and re-layouts  0.93 us (3%)
    ppermute x16, starting transfers between devices, swap(): return lax.ppermute(array, ('loop', 'rep'), pairs)  17.2 us
    ppermute x16, waiting for transfers between devices, swap(): return lax.ppermute(array, ('loop', 'rep'), pairs)  15 us
    pallas_call x2, Pallas kernels, product(): pl.pallas_call(product_kernel, out_shape=[sums] * 2, in_specs=[in_vmem] *...  1.75 us
    unnamed x6, local copies, waits for them, and re-layouts  0.93 us
    pallas_call x1, Pallas kernels, square(): pl.pallas_call(total_kernel, out_shape=jax.ShapeDtypeStruct((irreps, rows...  0.82 us
    pallas_call x1, Pallas kernels, square(): pl.pallas_call(split_kernel, out_shape=[half] * 2, in_specs=[pl.BlockSpec...  0.75 us
  transfers between devices with their start and end apart: 16, of which 8 were waited for; matrix products, arithmetic and copies ran while one was open for 0% of the time, Pallas kernels for 7%

profile of v3, /device:TPU:0, one launch (start us, length us, event | category | flops | bytes accessed | tf_op | source)
XLA Modules:
  0.0 36.7 jit_solution(9355097184787207715)
XLA Ops:
  0.0 0.0 copy-start.2
  0.0 0.9 %copy-done.2 = bf16[8,384,32]{1,2,0:T(8,128)(2,1)S(1)} copy-done((bf16[8,384,32]{1,2,0:T(8,128)(2,1)S(1)}, bf16[8,384,32]{1,2,0:T(8,128)(2,1)}, u32[]{:S(2)}) %copy-start.2) | copy-done | bytes 196632
  0.9 0.0 copy-start
  0.9 0.0 copy-start.1
  0.9 0.1 shard_map.37
  1.1 3.0 %collective-permute-start.1 = (bf16[2,96,128]{2,1,0:T(8,128)(2,1)S(1)}, bf16[2,96,128]{2,1,0:T(8,128)(2,1)S(1)}, u32[]{:S(2)}, u32[]{:S(2)}) collective-permute-start(bf16[2,96,128]{2,1,0:T(8,128)(2,1)S(1)} %get-tuple-element.31), channel_id=1, source_target_pairs={{0,2},{1,3},{2,0},{3,1},{4,5},{5,4},{6,7},{7,6},{8,10},{9,11},{10,... | collective-permute-start | bytes 147464 | tf_op jit(solution)/shard_map/lam_other/ppermute | solution.py:23
  4.1 1.5 %collective-permute-start = (bf16[2,96,128]{2,1,0:T(8,128)(2,1)S(1)}, bf16[2,96,128]{2,1,0:T(8,128)(2,1)S(1)}, u32[]{:S(2)}, u32[]{:S(2)}) collective-permute-start(bf16[2,96,128]{2,1,0:T(8,128)(2,1)S(1)} %get-tuple-element.30._), channel_id=1, source_target_pairs={{0,1},{1,0},{2,3},{3,2},{4,6},{5,7},{6,4},{7,5},{8,9},{9,8},{10,11... | collective-permute-start | bytes 147464 | tf_op jit(solution)/shard_map/lam_mine/ppermute | solution.py:23
  5.6 0.0 copy-done
  5.6 0.0 copy-done.1
  5.6 0.8 %shard_map.39 = (bf16[4,256,256]{2,1,0:T(8,128)(2,1)S(1)}, bf16[4,256,256]{2,1,0:T(8,128)(2,1)S(1)}) custom-call(s32[8,8]{1,0:T(8,128)S(1)} %copy-done.1, bf16[8,256,256]{2,1,0:T(8,128)(2,1)S(1)} %copy-done, bf16[2,96,128]{2,1,0:T(8,128)(2,1)S(1)} %get-tuple-element.30._), custom_call_target="tpu_custom_call" | custom-call | tf_op jit(solution)/shard_map/pallas_call | solution.py:143
  6.3 0.6 %collective-permute-start.8 = (bf16[4,256,256]{2,1,0:T(8,128)(2,1)S(1)}, bf16[4,256,256]{2,1,0:T(8,128)(2,1)S(1)}, u32[]{:S(2)}, u32[]{:S(2)}) collective-permute-start(bf16[4,256,256]{2,1,0:T(8,128)(2,1)S(1)} %get-tuple-element.36.near_ref), channel_id=1, source_target_pairs={{0,1},{1,0},{2,3},{3,2},{4,6},{5,7},{6,4},{7,5},{8,9},{9,8},{10,11... | collective-permute-start | bytes 1572872 | tf_op jit(solution)/shard_map/integrals_mine/ppermute | solution.py:23
  6.9 0.5 %collective-permute-start.9 = (bf16[4,256,256]{2,1,0:T(8,128)(2,1)S(1)}, bf16[4,256,256]{2,1,0:T(8,128)(2,1)S(1)}, u32[]{:S(2)}, u32[]{:S(2)}) collective-permute-start(bf16[4,256,256]{2,1,0:T(8,128)(2,1)S(1)} %get-tuple-element.37.near_other_ref), channel_id=1, source_target_pairs={{0,2},{1,3},{2,0},{3,1},{4,5},{5,4},{6,7},{7,6},{8,10},{9,11},{10,... | collective-permute-start | bytes 1572872 | tf_op jit(solution)/shard_map/integrals_other/ppermute | solution.py:23
  7.4 0.0 collective-permute-done.1.far_other_ref
  7.4 0.7 %collective-permute-done.far_mine_ref = bf16[2,96,128]{2,1,0:T(8,128)(2,1)S(1)} collective-permute-done((bf16[2,96,128]{2,1,0:T(8,128)(2,1)S(1)}, bf16[2,96,128]{2,1,0:T(8,128)(2,1)S(1)}, u32[]{:S(2)}, u32[]{:S(2)}) %collective-permute-start) | collective-permute-done | bytes 49184 | tf_op jit(solution)/shard_map/lam_mine/ppermute | solution.py:23
  8.2 0.1 collective-permute-start.6
  8.3 3.7 %collective-permute-start.2 = (bf16[4,96,128]{2,1,0:T(8,128)(2,1)S(1)}, bf16[4,96,128]{2,1,0:T(8,128)(2,1)S(1)}, u32[]{:S(2)}, u32[]{:S(2)}) collective-permute-start(bf16[4,96,128]{2,1,0:T(8,128)(2,1)S(1)} %get-tuple-element.33.own_ref), channel_id=1, source_target_pairs={{0,24},{1,25},{2,26},{3,27},{4,28},{5,29},{6,30},{7,31},{8,16},{9,... | collective-permute-start | bytes 294920 | tf_op jit(solution)/shard_map/sent_by_three/ppermute | solution.py:23
  11.9 0.2 collective-permute-start.3
  12.1 0.0 collective-permute-done.6.sibling_ref
  12.1 0.1 collective-permute-start.7
  12.2 1.0 %collective-permute-done.3.sibling_ref = bf16[4,96,128]{2,1,0:T(8,128)(2,1)S(1)} collective-permute-done((bf16[4,96,128]{2,1,0:T(8,128)(2,1)S(1)}, bf16[4,96,128]{2,1,0:T(8,128)(2,1)S(1)}, u32[]{:S(2)}, u32[]{:S(2)}) %collective-permute-start.3) | collective-permute-done | bytes 98336 | tf_op jit(solution)/shard_map/kept_own_over_core/ppermute | solution.py:23
  13.2 2.5 %collective-permute-done.2.alone_ref = bf16[4,96,128]{2,1,0:T(8,128)(2,1)S(1)} collective-permute-done((bf16[4,96,128]{2,1,0:T(8,128)(2,1)S(1)}, bf16[4,96,128]{2,1,0:T(8,128)(2,1)S(1)}, u32[]{:S(2)}, u32[]{:S(2)}) %collective-permute-start.2) | collective-permute-done | bytes 98336 | tf_op jit(solution)/shard_map/sent_by_three/ppermute | solution.py:23
  15.7 4.0 %collective-permute-done.8.far_ref = bf16[4,256,256]{2,1,0:T(8,128)(2,1)S(1)} collective-permute-done((bf16[4,256,256]{2,1,0:T(8,128)(2,1)S(1)}, bf16[4,256,256]{2,1,0:T(8,128)(2,1)S(1)}, u32[]{:S(2)}, u32[]{:S(2)}) %collective-permute-start.8) | collective-permute-done | bytes 524320 | tf_op jit(solution)/shard_map/integrals_mine/ppermute | solution.py:23
  19.7 0.0 collective-permute-done.9.far_other_ref
  19.7 0.0 collective-permute-start.10
  19.7 0.0 collective-permute-done.7.one_ref
  19.8 1.3 %collective-permute-done.10.alone_sibling_ref = bf16[4,96,128]{2,1,0:T(8,128)(2,1)S(1)} collective-permute-done((bf16[4,96,128]{2,1,0:T(8,128)(2,1)S(1)}, bf16[4,96,128]{2,1,0:T(8,128)(2,1)S(1)}, u32[]{:S(2)}, u32[]{:S(2)}) %collective-permute-start.10) | collective-permute-done | bytes 98336 | tf_op jit(solution)/shard_map/sent_three_over_core/ppermute | solution.py:23
  21.0 0.2 collective-permute-start.11
  21.2 1.6 %collective-permute-start.4 = (bf16[2,4,96,128]{3,2,1,0:T(8,128)(2,1)S(1)}, bf16[2,4,96,128]{3,2,1,0:T(8,128)(2,1)S(1)}, u32[]{:S(2)}, u32[]{:S(2)}) collective-permute-start(bf16[2,4,96,128]{3,2,1,0:T(8,128)(2,1)S(1)} %pad_maximum_fusion), channel_id=1, source_target_pairs={{0,8},{1,9},{2,10},{3,11},{4,20},{5,21},{6,22},{7,23},{8,0},{9,1},... | collective-permute-start | bytes 589832 | tf_op jit(solution)/shard_map/kept_by_core/ppermute | solution.py:23
  22.9 0.0 collective-permute-done.11.two_ref
  22.9 0.9 %shard_map.40 = (f32[4,96,256]{2,1,0:T(8,128)S(1)}, f32[4,96,256]{2,1,0:T(8,128)S(1)}) custom-call(bf16[4,96,128]{2,1,0:T(8,128)(2,1)S(1)} %get-tuple-element.33.own_ref, bf16[4,96,128]{2,1,0:T(8,128)(2,1)S(1)} %collective-permute-done.6.sibling_ref, bf16[2,4,96,128]{3,2,1,0:T(8,128)(2,1)S(1)} %collective-permute-done.7.one_ref, ...), custom_call_target="tpu_custom_call" | custom-call | tf_op jit(solution)/shard_map/pallas_call | solution.py:181
  23.7 1.2 %collective-permute-start.15 = (f32[4,96,256]{2,1,0:T(8,128)S(1)}, f32[4,96,256]{2,1,0:T(8,128)S(1)}, u32[]{:S(2)}, u32[]{:S(2)}) collective-permute-start(f32[4,96,256]{2,1,0:T(8,128)S(1)} %get-tuple-element.50), channel_id=1, source_target_pairs={{0,1},{1,0},{2,3},{3,2},{4,6},{5,7},{6,4},{7,5},{8,9},{9,8},{10,11... | collective-permute-start | bytes 1179656 | tf_op jit(solution)/shard_map/sums_other/ppermute | solution.py:23
  25.0 0.9 %collective-permute-start.14 = (f32[4,96,256]{2,1,0:T(8,128)S(1)}, f32[4,96,256]{2,1,0:T(8,128)S(1)}, u32[]{:S(2)}, u32[]{:S(2)}) collective-permute-start(f32[4,96,256]{2,1,0:T(8,128)S(1)} %get-tuple-element.43), channel_id=1, source_target_pairs={{0,2},{1,3},{2,0},{3,1},{4,5},{5,4},{6,7},{7,6},{8,10},{9,11},{10,... | collective-permute-start | bytes 1179656 | tf_op jit(solution)/shard_map/sums_mine/ppermute | solution.py:23
  25.9 3.2 %collective-permute-start.5 = (bf16[4,96,128]{2,1,0:T(8,128)(2,1)S(1)}, bf16[4,96,128]{2,1,0:T(8,128)(2,1)S(1)}, u32[]{:S(2)}, u32[]{:S(2)}) collective-permute-start(bf16[4,96,128]{2,1,0:T(8,128)(2,1)S(1)} %get-tuple-element.44.own_ref), channel_id=1, source_target_pairs={{0,24},{1,25},{2,26},{3,27},{4,28},{5,29},{6,30},{7,31},{8,16},{9,... | collective-permute-start | bytes 294920 | tf_op jit(solution)/shard_map/kept_by_three/ppermute | solution.py:23
  29.1 3.9 %collective-permute-done.5.alone_ref = bf16[4,96,128]{2,1,0:T(8,128)(2,1)S(1)} collective-permute-done((bf16[4,96,128]{2,1,0:T(8,128)(2,1)S(1)}, bf16[4,96,128]{2,1,0:T(8,128)(2,1)S(1)}, u32[]{:S(2)}, u32[]{:S(2)}) %collective-permute-start.5) | collective-permute-done | bytes 98336 | tf_op jit(solution)/shard_map/kept_by_three/ppermute | solution.py:23
  33.0 0.0 collective-permute-done.4.one_ref
  33.0 0.0 collective-permute-start.12
  33.0 0.5 %collective-permute-start.13 = (bf16[4,96,128]{2,1,0:T(8,128)(2,1)S(1)}, bf16[4,96,128]{2,1,0:T(8,128)(2,1)S(1)}, u32[]{:S(2)}, u32[]{:S(2)}) collective-permute-start(bf16[4,96,128]{2,1,0:T(8,128)(2,1)S(1)} %collective-permute-done.5.alone_ref), channel_id=1, source_target_pairs={{0,4},{1,5},{2,6},{3,7},{4,0},{5,1},{6,2},{7,3},{8,12},{9,13},{10,... | collective-permute-start | bytes 294920 | tf_op jit(solution)/shard_map/kept_three_over_core/ppermute | solution.py:23
  33.5 1.1 %collective-permute-done.13.alone_sibling_ref = bf16[4,96,128]{2,1,0:T(8,128)(2,1)S(1)} collective-permute-done((bf16[4,96,128]{2,1,0:T(8,128)(2,1)S(1)}, bf16[4,96,128]{2,1,0:T(8,128)(2,1)S(1)}, u32[]{:S(2)}, u32[]{:S(2)}) %collective-permute-start.13) | collective-permute-done | bytes 98336 | tf_op jit(solution)/shard_map/kept_three_over_core/ppermute | solution.py:23
  34.6 0.0 collective-permute-done.12.two_ref
  34.6 0.9 %shard_map.41 = (f32[4,96,256]{2,1,0:T(8,128)S(1)}, f32[4,96,256]{2,1,0:T(8,128)S(1)}) custom-call(bf16[4,96,128]{2,1,0:T(8,128)(2,1)S(1)} %get-tuple-element.44.own_ref, bf16[4,96,128]{2,1,0:T(8,128)(2,1)S(1)} %collective-permute-done.3.sibling_ref, bf16[2,4,96,128]{3,2,1,0:T(8,128)(2,1)S(1)} %collective-permute-done.4.one_ref, ...), custom_call_target="tpu_custom_call" | custom-call | tf_op jit(solution)/shard_map/pallas_call | solution.py:181
  35.5 0.0 collective-permute-done.15.sum_other_ref
  35.5 0.4 %collective-permute-done.14.sum_mine_ref = f32[4,96,256]{2,1,0:T(8,128)S(1)} collective-permute-done((f32[4,96,256]{2,1,0:T(8,128)S(1)}, f32[4,96,256]{2,1,0:T(8,128)S(1)}, u32[]{:S(2)}, u32[]{:S(2)}) %collective-permute-start.14) | collective-permute-done | bytes 393248 | tf_op jit(solution)/shard_map/sums_mine/ppermute | solution.py:23
  35.9 0.8 %shard_map.42 = bf16[8,96,256]{2,1,0:T(8,128)(2,1)} custom-call(f32[4,96,256]{2,1,0:T(8,128)S(1)} %get-tuple-element.48.mine_ref, f32[4,96,256]{2,1,0:T(8,128)S(1)} %get-tuple-element.49.other_ref, f32[4,96,256]{2,1,0:T(8,128)S(1)} %collective-permute-done.14.sum_mine_ref, f32[4,96,256]{2,1,0:T(8,128)S(1)} %collective-permute-done.15.sum_other_ref), custom_call_target="tpu_custom_call" | custom-call | tf_op jit(solution)/shard_map/pallas_call | solution.py:208
  (3 shorter events, 0.1 us)
Async XLA Ops:
  0.0 0.9 %copy-start.2 = (bf16[8,384,32]{1,2,0:T(8,128)(2,1)S(1)}, bf16[8,384,32]{1,2,0:T(8,128)(2,1)}, u32[]{:S(2)}) copy-start(bf16[8,384,32]{1,2,0:T(8,128)(2,1)} %param.3) | copy-start | bytes 589828
  0.9 4.7 %copy-start = (bf16[8,256,256]{2,1,0:T(8,128)(2,1)S(1)}, bf16[8,256,256]{2,1,0:T(8,128)(2,1)}, u32[]{:S(2)}) copy-start(bf16[8,256,256]{2,1,0:T(8,128)(2,1)} %integrals_ref.1) | copy-start | bytes 3145732
  0.9 4.7 %copy-start.1 = (s32[8,8]{1,0:T(8,128)S(1)}, s32[8,8]{1,0:T(8,128)}, u32[]{:S(2)}) copy-start(s32[8,8]{1,0:T(8,128)} %mask_ref.1) | copy-start | bytes 772
  1.1 6.4 %collective-permute-start.1 = (bf16[2,96,128]{2,1,0:T(8,128)(2,1)S(1)}, bf16[2,96,128]{2,1,0:T(8,128)(2,1)S(1)}, u32[]{:S(2)}, u32[]{:S(2)}) collective-permute-start(bf16[2,96,128]{2,1,0:T(8,128)(2,1)S(1)} %get-tuple-element.31), channel_id=1, source_target_pairs={{0,2},{1,3},{2,0},{3,1},{4,5},{5,4},{6,7},{7,6},{8,10},{9,11},{10,... | collective-permute-start | bytes 147464 | tf_op jit(solution)/shard_map/lam_other/ppermute | solution.py:23
  4.1 4.1 %collective-permute-start = (bf16[2,96,128]{2,1,0:T(8,128)(2,1)S(1)}, bf16[2,96,128]{2,1,0:T(8,128)(2,1)S(1)}, u32[]{:S(2)}, u32[]{:S(2)}) collective-permute-start(bf16[2,96,128]{2,1,0:T(8,128)(2,1)S(1)} %get-tuple-element.30._), channel_id=1, source_target_pairs={{0,1},{1,0},{2,3},{3,2},{4,6},{5,7},{6,4},{7,5},{8,9},{9,8},{10,11... | collective-permute-start | bytes 147464 | tf_op jit(solution)/shard_map/lam_mine/ppermute | solution.py:23
  6.3 13.4 %collective-permute-start.8 = (bf16[4,256,256]{2,1,0:T(8,128)(2,1)S(1)}, bf16[4,256,256]{2,1,0:T(8,128)(2,1)S(1)}, u32[]{:S(2)}, u32[]{:S(2)}) collective-permute-start(bf16[4,256,256]{2,1,0:T(8,128)(2,1)S(1)} %get-tuple-element.36.near_ref), channel_id=1, source_target_pairs={{0,1},{1,0},{2,3},{3,2},{4,6},{5,7},{6,4},{7,5},{8,9},{9,8},{10,11... | collective-permute-start | bytes 1572872 | tf_op jit(solution)/shard_map/integrals_mine/ppermute | solution.py:23
  6.9 12.8 %collective-permute-start.9 = (bf16[4,256,256]{2,1,0:T(8,128)(2,1)S(1)}, bf16[4,256,256]{2,1,0:T(8,128)(2,1)S(1)}, u32[]{:S(2)}, u32[]{:S(2)}) collective-permute-start(bf16[4,256,256]{2,1,0:T(8,128)(2,1)S(1)} %get-tuple-element.37.near_other_ref), channel_id=1, source_target_pairs={{0,2},{1,3},{2,0},{3,1},{4,5},{5,4},{6,7},{7,6},{8,10},{9,11},{10,... | collective-permute-start | bytes 1572872 | tf_op jit(solution)/shard_map/integrals_other/ppermute | solution.py:23
  8.2 3.9 %collective-permute-start.6 = (bf16[4,96,128]{2,1,0:T(8,128)(2,1)S(1)}, bf16[4,96,128]{2,1,0:T(8,128)(2,1)S(1)}, u32[]{:S(2)}, u32[]{:S(2)}) collective-permute-start(bf16[4,96,128]{2,1,0:T(8,128)(2,1)S(1)} %get-tuple-element.33.own_ref), channel_id=1, source_target_pairs={{0,4},{1,5},{2,6},{3,7},{4,0},{5,1},{6,2},{7,3},{8,12},{9,13},{10,... | collective-permute-start | bytes 294920 | tf_op jit(solution)/shard_map/sent_own_over_core/ppermute | solution.py:23
  8.3 7.5 %collective-permute-start.2 = (bf16[4,96,128]{2,1,0:T(8,128)(2,1)S(1)}, bf16[4,96,128]{2,1,0:T(8,128)(2,1)S(1)}, u32[]{:S(2)}, u32[]{:S(2)}) collective-permute-start(bf16[4,96,128]{2,1,0:T(8,128)(2,1)S(1)} %get-tuple-element.33.own_ref), channel_id=1, source_target_pairs={{0,24},{1,25},{2,26},{3,27},{4,28},{5,29},{6,30},{7,31},{8,16},{9,... | collective-permute-start | bytes 294920 | tf_op jit(solution)/shard_map/sent_by_three/ppermute | solution.py:23
  11.9 1.3 %collective-permute-start.3 = (bf16[4,96,128]{2,1,0:T(8,128)(2,1)S(1)}, bf16[4,96,128]{2,1,0:T(8,128)(2,1)S(1)}, u32[]{:S(2)}, u32[]{:S(2)}) collective-permute-start(bf16[4,96,128]{2,1,0:T(8,128)(2,1)S(1)} %get-tuple-element.44.own_ref), channel_id=1, source_target_pairs={{0,4},{1,5},{2,6},{3,7},{4,0},{5,1},{6,2},{7,3},{8,12},{9,13},{10,... | collective-permute-start | bytes 294920 | tf_op jit(solution)/shard_map/kept_own_over_core/ppermute | solution.py:23
  12.1 7.6 %collective-permute-start.7 = (bf16[2,4,96,128]{3,2,1,0:T(8,128)(2,1)S(1)}, bf16[2,4,96,128]{3,2,1,0:T(8,128)(2,1)S(1)}, u32[]{:S(2)}, u32[]{:S(2)}) collective-permute-start(bf16[2,4,96,128]{3,2,1,0:T(8,128)(2,1)S(1)} %pad_maximum_fusion.1), channel_id=1, source_target_pairs={{0,8},{1,9},{2,10},{3,11},{4,20},{5,21},{6,22},{7,23},{8,0},{9,1},... | collective-permute-start | bytes 589832 | tf_op jit(solution)/shard_map/sent_by_core/ppermute | solution.py:23
  19.7 1.3 %collective-permute-start.10 = (bf16[4,96,128]{2,1,0:T(8,128)(2,1)S(1)}, bf16[4,96,128]{2,1,0:T(8,128)(2,1)S(1)}, u32[]{:S(2)}, u32[]{:S(2)}) collective-permute-start(bf16[4,96,128]{2,1,0:T(8,128)(2,1)S(1)} %collective-permute-done.2.alone_ref), channel_id=1, source_target_pairs={{0,4},{1,5},{2,6},{3,7},{4,0},{5,1},{6,2},{7,3},{8,12},{9,13},{10,... | collective-permute-start | bytes 294920 | tf_op jit(solution)/shard_map/sent_three_over_core/ppermute | solution.py:23
  21.0 1.8 %collective-permute-start.11 = (bf16[2,4,96,128]{3,2,1,0:T(8,128)(2,1)S(1)}, bf16[2,4,96,128]{3,2,1,0:T(8,128)(2,1)S(1)}, u32[]{:S(2)}, u32[]{:S(2)}) collective-permute-start(bf16[2,4,96,128]{3,2,1,0:T(8,128)(2,1)S(1)} %collective-permute-done.7.one_ref), channel_id=1, source_target_pairs={{0,4},{1,5},{2,6},{3,7},{4,0},{5,1},{6,2},{7,3},{8,12},{9,13},{10,... | collective-permute-start | bytes 589832 | tf_op jit(solution)/shard_map/sent_one_over_core/ppermute | solution.py:23
  21.2 11.8 %collective-permute-start.4 = (bf16[2,4,96,128]{3,2,1,0:T(8,128)(2,1)S(1)}, bf16[2,4,96,128]{3,2,1,0:T(8,128)(2,1)S(1)}, u32[]{:S(2)}, u32[]{:S(2)}) collective-permute-start(bf16[2,4,96,128]{3,2,1,0:T(8,128)(2,1)S(1)} %pad_maximum_fusion), channel_id=1, source_target_pairs={{0,8},{1,9},{2,10},{3,11},{4,20},{5,21},{6,22},{7,23},{8,0},{9,1},... | collective-permute-start | bytes 589832 | tf_op jit(solution)/shard_map/kept_by_core/ppermute | solution.py:23
  23.7 11.7 %collective-permute-start.15 = (f32[4,96,256]{2,1,0:T(8,128)S(1)}, f32[4,96,256]{2,1,0:T(8,128)S(1)}, u32[]{:S(2)}, u32[]{:S(2)}) collective-permute-start(f32[4,96,256]{2,1,0:T(8,128)S(1)} %get-tuple-element.50), channel_id=1, source_target_pairs={{0,1},{1,0},{2,3},{3,2},{4,6},{5,7},{6,4},{7,5},{8,9},{9,8},{10,11... | collective-permute-start | bytes 1179656 | tf_op jit(solution)/shard_map/sums_other/ppermute | solution.py:23
  25.0 10.9 %collective-permute-start.14 = (f32[4,96,256]{2,1,0:T(8,128)S(1)}, f32[4,96,256]{2,1,0:T(8,128)S(1)}, u32[]{:S(2)}, u32[]{:S(2)}) collective-permute-start(f32[4,96,256]{2,1,0:T(8,128)S(1)} %get-tuple-element.43), channel_id=1, source_target_pairs={{0,2},{1,3},{2,0},{3,1},{4,5},{5,4},{6,7},{7,6},{8,10},{9,11},{10,... | collective-permute-start | bytes 1179656 | tf_op jit(solution)/shard_map/sums_mine/ppermute | solution.py:23
  25.9 7.1 %collective-permute-start.5 = (bf16[4,96,128]{2,1,0:T(8,128)(2,1)S(1)}, bf16[4,96,128]{2,1,0:T(8,128)(2,1)S(1)}, u32[]{:S(2)}, u32[]{:S(2)}) collective-permute-start(bf16[4,96,128]{2,1,0:T(8,128)(2,1)S(1)} %get-tuple-element.44.own_ref), channel_id=1, source_target_pairs={{0,24},{1,25},{2,26},{3,27},{4,28},{5,29},{6,30},{7,31},{8,16},{9,... | collective-permute-start | bytes 294920 | tf_op jit(solution)/shard_map/kept_by_three/ppermute | solution.py:23
  33.0 1.6 %collective-permute-start.12 = (bf16[2,4,96,128]{3,2,1,0:T(8,128)(2,1)S(1)}, bf16[2,4,96,128]{3,2,1,0:T(8,128)(2,1)S(1)}, u32[]{:S(2)}, u32[]{:S(2)}) collective-permute-start(bf16[2,4,96,128]{3,2,1,0:T(8,128)(2,1)S(1)} %collective-permute-done.4.one_ref), channel_id=1, source_target_pairs={{0,4},{1,5},{2,6},{3,7},{4,0},{5,1},{6,2},{7,3},{8,12},{9,13},{10,... | collective-permute-start | bytes 589832 | tf_op jit(solution)/shard_map/kept_one_over_core/ppermute | solution.py:23
  33.0 1.6 %collective-permute-start.13 = (bf16[4,96,128]{2,1,0:T(8,128)(2,1)S(1)}, bf16[4,96,128]{2,1,0:T(8,128)(2,1)S(1)}, u32[]{:S(2)}, u32[]{:S(2)}) collective-permute-start(bf16[4,96,128]{2,1,0:T(8,128)(2,1)S(1)} %collective-permute-done.5.alone_ref), channel_id=1, source_target_pairs={{0,4},{1,5},{2,6},{3,7},{4,0},{5,1},{6,2},{7,3},{8,12},{9,13},{10,... | collective-permute-start | bytes 294920 | tf_op jit(solution)/shard_map/kept_three_over_core/ppermute | solution.py:23

commit v4 on v3

v4 whole, which is shorter than its diff:
```python
import functools

import jax
import jax.numpy as jnp
from jax import lax
from jax.experimental import pallas as pl
from jax.experimental.pallas import tpu as pltpu
from jax.sharding import PartitionSpec as P

VMEM = pltpu.VMEM
SENT, KEPT = (3, 1, 2), (3, 1, 2)
PARAMS = pltpu.CompilerParams(vmem_limit_bytes=16 << 20)
CHIPS = 4
COST_PACK, COST_JOIN, COST_FAR = 2 * 10**9, 4 * 10**9, 4 * 10**9
COST_SENT, COST_OTHER, COST_KEPT, COST_SUM, HOLD, APART = 0, 0, 0, 2 * 10**9, 0, 1


def cost(flops):
    return pl.CostEstimate(flops=flops, bytes_accessed=0, transcendentals=0)


def swap(array, pairs, scope):
    with jax.named_scope(scope):
        return lax.ppermute(array, ("loop", "rep"), pairs)


def mark(flops, *arrays):
    return pl.pallas_call(
        lambda *refs: None,
        out_shape=[jax.ShapeDtypeStruct(array.shape, array.dtype) for array in arrays],
        in_specs=[pl.BlockSpec(memory_space=VMEM)] * len(arrays),
        out_specs=[pl.BlockSpec(memory_space=VMEM)] * len(arrays),
        input_output_aliases={i: i for i in range(len(arrays))},
        cost_estimate=cost(flops),
        compiler_params=PARAMS,
    )(*arrays)


def position():
    rep, spot = lax.axis_index("rep"), lax.axis_index("loop")
    return rep // 2, rep % 2, spot // 2, spot % 2


def pack_kernel(halves, lam_ref, mine_ref, other_ref, to_mine_ref, to_other_ref, turned):
    y, x, _, core = position()
    rows = turned.shape[2]
    for kind in range(2):
        block = jnp.concatenate([lam_ref[kind * halves + h] for h in range(halves)], axis=0)
        flipped = block.T
        for quarter in range(4):
            turned[kind, quarter] = flipped[quarter * rows : (quarter + 1) * rows]
    kept, over_x, over_y, over_both = y * 2 + x, y * 2 + 1 - x, (1 - y) * 2 + x, (1 - y) * 2 + 1 - x
    for kind, own_ref, to_ref in ((core, mine_ref, to_mine_ref), (1 - core, other_ref, to_other_ref)):
        summed, fetched = jnp.where(kind == 0, over_y, over_x), jnp.where(kind == 0, over_x, over_y)
        own_ref[0] = turned[kind, summed]
        own_ref[1] = turned[kind, kept]
        to_ref[0] = turned[kind, over_both]
        to_ref[1] = turned[kind, fetched]


def split_kernel(mask_ref, integrals_ref, _, mine_ref, other_ref):
    irreps, blocks = mask_ref.shape
    halves = irreps // 2
    _, depth, columns = integrals_ref.shape
    core = position()[3]
    for kind, out_ref in ((core, mine_ref), (1 - core, other_ref)):
        live = mask_ref[pl.ds(kind * halves, halves)].astype(jnp.float32)
        for h in range(halves):
            for b in range(blocks):
                rows = slice(b * depth // blocks, (b + 1) * depth // blocks)
                factor = jnp.broadcast_to(live[h : h + 1, b : b + 1], (depth // blocks, columns)).astype(jnp.bfloat16)
                out_ref[h, rows] = integrals_ref[kind * halves + h, rows] * factor


def join_kernel(mine_ref, other_ref, far_mine_ref, far_other_ref, sent_ref, kept_ref):
    for which, out_ref in enumerate((sent_ref, kept_ref)):
        for slot, ref in enumerate((mine_ref, other_ref, far_mine_ref, far_other_ref)):
            out_ref[slot] = ref[which]


def product_kernel(kinds, hops, *refs):
    own_ref, sibling_ref, one_ref, two_ref, alone_ref, alone_sibling_ref = refs[:6]
    integrals_refs, out_refs, pieces = refs[6 : 6 + 2 * len(kinds)], refs[6 + 2 * len(kinds) : -1], refs[-1]
    _, _, z, core = position()

    def place(message, back, from_sibling):
        block = (z ^ back) * 2 + (1 - core if from_sibling else core)
        for layer in range(2):
            for slot, kind in enumerate(kinds):
                pieces[layer, slot, block] = message[2 * layer + (1 - kind if from_sibling else kind)]

    held = jnp.where(core == 0, hops[1], hops[2])
    passed = jnp.where(core == 0, hops[2], hops[1])
    place(own_ref, 0, False)
    place(sibling_ref, 0, True)
    place(alone_ref, hops[0], False)
    place(alone_sibling_ref, hops[0], True)
    place(one_ref.at[0], held, False)
    place(one_ref.at[1], held, True)
    place(two_ref.at[0], passed, True)
    place(two_ref.at[1], passed, False)
    for slot, out in enumerate(out_refs):
        near, far = integrals_refs[2 * slot : 2 * slot + 2]
        halves = near.shape[0]
        depth = pieces.shape[4] // halves
        parts = [[pieces[layer, slot, s] for s in range(2 * CHIPS)] for layer in range(2)]
        for h in range(halves):
            cut = slice(h * depth, (h + 1) * depth)
            near_lam, far_lam = (jnp.concatenate([p[:, cut] for p in parts[layer]], axis=1) for layer in range(2))
            out[h] = jnp.dot(near_lam, near[h], preferred_element_type=jnp.float32) + jnp.dot(
                far_lam, far[h], preferred_element_type=jnp.float32
            )


def total_kernel(kept_ref, kept_other_ref, arrived_ref, arrived_other_ref, out_ref, rounded, done):
    core = position()[3]
    halves = kept_ref.shape[0]
    copies = []
    for kind, kept, arrived in ((0, kept_ref, arrived_ref), (1, kept_other_ref, arrived_other_ref)):
        at = (1 - core if kind else core) * halves
        for h in range(halves):
            step = kind * halves + h
            rounded[step] = (kept[h] + arrived[h]).astype(rounded.dtype)
            copies.append(pltpu.make_async_copy(rounded.at[step], out_ref.at[at + h], done.at[step]))
            copies[-1].start()
    for copy in copies:
        copy.wait()


def square(lam, integrals, block_mask):
    irreps, occ, depth = lam.shape
    halves = irreps // 2
    rows = occ // 4
    columns = integrals.shape[2]
    loops = 2 * CHIPS
    bf16, f32 = jnp.bfloat16, jnp.float32
    lanes = halves * depth
    in_vmem = pl.BlockSpec(memory_space=VMEM)
    quarters = jax.ShapeDtypeStruct((2, rows, lanes), bf16)
    half = jax.ShapeDtypeStruct((halves,) + integrals.shape[1:], bf16)
    sums = jax.ShapeDtypeStruct((halves, rows, columns), f32)

    def pairs(aim):
        places = [(s, r) for s in range(loops) for r in range(4)]
        return [(at, places.index(aim(s, r, s % 2))) for at, (s, r) in enumerate(places)]

    over_core = pairs(lambda s, r, core: (s ^ 1, r))
    fetch = pairs(lambda s, r, core: (s, r ^ (1 + core)))
    reduce = pairs(lambda s, r, core: (s, r ^ (2 - core)))
    alone = lambda hops: pairs(lambda s, r, core: (s ^ (2 * hops[0]), r))
    by_core = lambda hops: pairs(lambda s, r, core: (s ^ (2 * hops[1 + core]), r))

    mine, other, to_mine, to_other = pl.pallas_call(
        functools.partial(pack_kernel, halves),
        out_shape=[quarters] * 4,
        in_specs=[in_vmem],
        out_specs=[in_vmem] * 4,
        scratch_shapes=[VMEM((2, 4, rows, lanes), bf16)],
        cost_estimate=cost(COST_PACK),
        compiler_params=PARAMS,
    )(lam.transpose(0, 2, 1))
    far_mine = swap(to_mine, fetch, "lam_mine")
    far_other = swap(to_other, reduce, "lam_other")

    near, near_other = pl.pallas_call(
        split_kernel,
        out_shape=[half] * 2,
        in_specs=[in_vmem, in_vmem, pl.BlockSpec(memory_space=pl.ANY)],
        out_specs=[in_vmem] * 2,
        compiler_params=PARAMS,
    )(block_mask, integrals, to_mine)
    far = swap(near, fetch, "integrals_mine")
    far_other_integrals = swap(near_other, reduce, "integrals_other")

    starts = pl.pallas_call(
        join_kernel,
        out_shape=[jax.ShapeDtypeStruct((4, rows, lanes), bf16)] * 2,
        in_specs=[in_vmem] * 4,
        out_specs=[in_vmem] * 2,
        cost_estimate=cost(COST_JOIN),
        compiler_params=PARAMS,
    )(mine, other, far_mine, far_other)

    def gathered(which, hops, name):
        own = starts[which]
        sibling = swap(own, over_core, name + "_own_over_core")
        return own, sibling, swap(own, alone(hops), name + "_by_three")

    def with_core(parts, hops, name):
        own, sibling, three = parts
        return [own, sibling, swap(jnp.stack([own, sibling]), by_core(hops), name + "_by_core"), three]

    def exchanged(parts, name):
        own, sibling, one, three = parts
        three_sibling = swap(three, over_core, name + "_three_over_core")
        if name == "sent":
            one, three_sibling = lax.optimization_barrier((one, three_sibling))
        return [own, sibling, one, swap(one, over_core, name + "_one_over_core"), three, three_sibling]

    def product(parts, kinds, hops, flops):
        given = [(near, far), (near_other, far_other_integrals)]
        return pl.pallas_call(
            functools.partial(product_kernel, kinds, hops),
            out_shape=[sums] * len(kinds),
            in_specs=[in_vmem] * (6 + 2 * len(kinds)),
            out_specs=[in_vmem] * len(kinds),
            scratch_shapes=[VMEM((2, len(kinds), loops, rows, lanes), bf16)],
            cost_estimate=cost(flops),
            compiler_params=PARAMS,
        )(*parts, *(array for kind in kinds for array in given[kind]))

    sent_parts = with_core(gathered(0, SENT, "sent"), SENT, "sent")
    kept_own = starts[1]
    kept_sibling = swap(kept_own, over_core, "kept_own_over_core")
    sent_parts[3], kept_sibling = lax.optimization_barrier((sent_parts[3], kept_sibling))
    alone_own = kept_own
    if HOLD == 1:
        sent_parts[2], alone_own = lax.optimization_barrier((sent_parts[2], alone_own))
    if HOLD == 2:
        sent_parts[2], kept_sibling = lax.optimization_barrier((sent_parts[2], kept_sibling))
    far, far_other_integrals = mark(COST_FAR, far, far_other_integrals)
    if HOLD == 3:
        far, alone_own = lax.optimization_barrier((far, alone_own))
    kept_alone = swap(alone_own, alone(KEPT), "kept_by_three")
    kept_parts = with_core((kept_own, kept_sibling, kept_alone), KEPT, "kept")
    sent_parts = exchanged(sent_parts, "sent")
    if APART:
        (sent,) = product(sent_parts, (0,), SENT, COST_SENT)
        (sent_other,) = product(sent_parts, (1,), SENT, COST_OTHER)
    else:
        sent, sent_other = product(sent_parts, (0, 1), SENT, COST_SENT)
    sum_mine = swap(sent, reduce, "sums_mine")
    sum_other = swap(sent_other, fetch, "sums_other")
    if COST_SUM:
        (sum_mine,) = mark(COST_SUM, sum_mine)
    kept_parts, sent = lax.optimization_barrier((kept_parts, sent))
    kept, kept_other = product(exchanged(kept_parts, "kept"), (0, 1), KEPT, COST_KEPT)
    return pl.pallas_call(
        total_kernel,
        out_shape=jax.ShapeDtypeStruct((irreps, rows, columns), bf16),
        in_specs=[in_vmem] * 4,
        out_specs=pl.BlockSpec(memory_space=pl.ANY),
        scratch_shapes=[VMEM((irreps, rows, columns), bf16), pltpu.SemaphoreType.DMA((irreps,))],
        compiler_params=PARAMS,
    )(kept, kept_other, sum_mine, sum_other)


def general(lam, integrals, block_mask):
    live = jnp.repeat(block_mask, lam.shape[2], axis=1) == 1
    kept = jnp.where(live[:, :, None], integrals, jnp.zeros_like(integrals))
    layer_lam = lax.all_gather(lam, "loop", axis=2, tiled=True)
    partial_sum = jnp.einsum("hpk,hka->hpa", layer_lam, kept, preferred_element_type=jnp.float32)
    return lax.psum_scatter(partial_sum, "rep", scatter_dimension=1, tiled=True).astype(jnp.bfloat16)


def solution(mesh):
    return jax.shard_map(
        square if (mesh.shape["rep"], mesh.shape["loop"]) == (4, 2 * CHIPS) else general,
        mesh=mesh,
        in_specs=(P(None, None, ("rep", "loop")), P(None, "rep", "loop"), P(None, "rep")),
        out_specs=P(None, "rep", "loop"),
        check_vma=False,
    )
```

time: 36.9 us -> 34.9 us (0.946)
  waiting for transfers between devices: 15 us -> 11.1 us
  starting transfers between devices: 17.2 us -> 19.6 us
  Pallas kernels: 3.45 us -> 3.07 us
    ppermute x16, waiting for transfers between devices: 15 us -> 11.1 us  [swap(): return lax.ppermute(array, ('loop', 'rep'), pairs)]
    ppermute x16, starting transfers between devices: 17.2 us -> 19.6 us  [swap(): return lax.ppermute(array, ('loop', 'rep'), pairs)]
    pallas_call x3 -> x6, Pallas kernels: 2.5 us -> 2.13 us  [the longest x3 1.93 us: product(): pl.pallas_call(functools.partial(product_kernel, kinds, hops), out_shape=...]
  transfers between devices with their start and end apart: 16 -> 16, of which waited for: 8 -> 7; matrix products, arithmetic and copies ran while one was open for 0% -> 0% of each run, Pallas kernels for 7% -> 6%
where the time goes in v4:
time: 34.9 us; the launch traced here: 34.8 us
  starting transfers between devices  19.6 us (56%)
  waiting for transfers between devices  11.1 us (32%)
  Pallas kernels  3.07 us (9%)
  local copies, waits for them, and re-layouts  0.93 us (3%)
    ppermute x16, starting transfers between devices, swap(): return lax.ppermute(array, ('loop', 'rep'), pairs)  19.6 us
    ppermute x16, waiting for transfers between devices, swap(): return lax.ppermute(array, ('loop', 'rep'), pairs)  11.1 us
    pallas_call x3, Pallas kernels, product(): pl.pallas_call(functools.partial(product_kernel, kinds, hops), out_shape=...  1.93 us
    unnamed x6, local copies, waits for them, and re-layouts  0.93 us
    pallas_call x1, Pallas kernels, square(): pl.pallas_call(total_kernel, out_shape=jax.ShapeDtypeStruct((irreps, rows...  0.82 us
  transfers between devices with their start and end apart: 16, of which 7 were waited for; matrix products, arithmetic and copies ran while one was open for 0% of the time, Pallas kernels for 6%

profile of v4, /device:TPU:0, one launch (start us, length us, event | category | flops | bytes accessed | tf_op | source)
XLA Modules:
  0.0 34.8 jit_solution(8291758214004905743)
XLA Ops:
  0.0 0.0 copy-start.2
  0.0 0.9 %copy-done.2 = bf16[8,384,32]{1,2,0:T(8,128)(2,1)S(1)} copy-done((bf16[8,384,32]{1,2,0:T(8,128)(2,1)S(1)}, bf16[8,384,32]{1,2,0:T(8,128)(2,1)}, u32[]{:S(2)}) %copy-start.2) | copy-done | bytes 196632
  0.9 0.0 copy-start
  0.9 0.0 copy-start.1
  0.9 0.1 shard_map.37
  1.1 3.0 %collective-permute-start.1 = (bf16[2,96,128]{2,1,0:T(8,128)(2,1)S(1)}, bf16[2,96,128]{2,1,0:T(8,128)(2,1)S(1)}, u32[]{:S(2)}, u32[]{:S(2)}) collective-permute-start(bf16[2,96,128]{2,1,0:T(8,128)(2,1)S(1)} %get-tuple-element.28), channel_id=1, source_target_pairs={{0,2},{1,3},{2,0},{3,1},{4,5},{5,4},{6,7},{7,6},{8,10},{9,11},{10,... | collective-permute-start | bytes 147464 | tf_op jit(solution)/shard_map/lam_other/ppermute | solution.py:24
  4.1 1.5 %collective-permute-start = (bf16[2,96,128]{2,1,0:T(8,128)(2,1)S(1)}, bf16[2,96,128]{2,1,0:T(8,128)(2,1)S(1)}, u32[]{:S(2)}, u32[]{:S(2)}) collective-permute-start(bf16[2,96,128]{2,1,0:T(8,128)(2,1)S(1)} %get-tuple-element.27._), channel_id=1, source_target_pairs={{0,1},{1,0},{2,3},{3,2},{4,6},{5,7},{6,4},{7,5},{8,9},{9,8},{10,11... | collective-permute-start | bytes 147464 | tf_op jit(solution)/shard_map/lam_mine/ppermute | solution.py:24
  5.6 0.0 copy-done
  5.6 0.0 copy-done.1
  5.6 0.2 shard_map.39
  5.8 0.6 %collective-permute-start.10 = (bf16[4,256,256]{2,1,0:T(8,128)(2,1)S(1)}, bf16[4,256,256]{2,1,0:T(8,128)(2,1)S(1)}, u32[]{:S(2)}, u32[]{:S(2)}) collective-permute-start(bf16[4,256,256]{2,1,0:T(8,128)(2,1)S(1)} %get-tuple-element.35.refs_6_), channel_id=1, source_target_pairs={{0,1},{1,0},{2,3},{3,2},{4,6},{5,7},{6,4},{7,5},{8,9},{9,8},{10,11... | collective-permute-start | bytes 1572872 | tf_op jit(solution)/shard_map/integrals_mine/ppermute | solution.py:24
  6.4 0.5 %collective-permute-start.11 = (bf16[4,256,256]{2,1,0:T(8,128)(2,1)S(1)}, bf16[4,256,256]{2,1,0:T(8,128)(2,1)S(1)}, u32[]{:S(2)}, u32[]{:S(2)}) collective-permute-start(bf16[4,256,256]{2,1,0:T(8,128)(2,1)S(1)} %get-tuple-element.36.refs_8_.refs_6_), channel_id=1, source_target_pairs={{0,2},{1,3},{2,0},{3,1},{4,5},{5,4},{6,7},{7,6},{8,10},{9,11},{10,... | collective-permute-start | bytes 1572872 | tf_op jit(solution)/shard_map/integrals_other/ppermute | solution.py:24
  6.9 0.0 collective-permute-done.1.far_other_ref
  6.9 1.5 %collective-permute-done.far_mine_ref = bf16[2,96,128]{2,1,0:T(8,128)(2,1)S(1)} collective-permute-done((bf16[2,96,128]{2,1,0:T(8,128)(2,1)S(1)}, bf16[2,96,128]{2,1,0:T(8,128)(2,1)S(1)}, u32[]{:S(2)}, u32[]{:S(2)}) %collective-permute-start) | collective-permute-done | bytes 49184 | tf_op jit(solution)/shard_map/lam_mine/ppermute | solution.py:24
  8.4 0.1 collective-permute-start.6
  8.5 3.7 %collective-permute-start.2 = (bf16[4,96,128]{2,1,0:T(8,128)(2,1)S(1)}, bf16[4,96,128]{2,1,0:T(8,128)(2,1)S(1)}, u32[]{:S(2)}, u32[]{:S(2)}) collective-permute-start(bf16[4,96,128]{2,1,0:T(8,128)(2,1)S(1)} %get-tuple-element.30.refs_0_), channel_id=1, source_target_pairs={{0,24},{1,25},{2,26},{3,27},{4,28},{5,29},{6,30},{7,31},{8,16},{9,... | collective-permute-start | bytes 294920 | tf_op jit(solution)/shard_map/sent_by_three/ppermute | solution.py:24
  12.2 0.2 collective-permute-start.3
  12.3 0.0 collective-permute-done.6.refs_1_
  12.4 0.1 collective-permute-start.7
  12.4 1.0 %collective-permute-done.3.refs_1_ = bf16[4,96,128]{2,1,0:T(8,128)(2,1)S(1)} collective-permute-done((bf16[4,96,128]{2,1,0:T(8,128)(2,1)S(1)}, bf16[4,96,128]{2,1,0:T(8,128)(2,1)S(1)}, u32[]{:S(2)}, u32[]{:S(2)}) %collective-permute-start.3) | collective-permute-done | bytes 98336 | tf_op jit(solution)/shard_map/kept_own_over_core/ppermute | solution.py:24
  13.5 2.5 %collective-permute-done.2.refs_4_ = bf16[4,96,128]{2,1,0:T(8,128)(2,1)S(1)} collective-permute-done((bf16[4,96,128]{2,1,0:T(8,128)(2,1)S(1)}, bf16[4,96,128]{2,1,0:T(8,128)(2,1)S(1)}, u32[]{:S(2)}, u32[]{:S(2)}) %collective-permute-start.2) | collective-permute-done | bytes 98336 | tf_op jit(solution)/shard_map/sent_by_three/ppermute | solution.py:24
  16.0 0.0 collective-permute-start.8
  16.0 3.9 %collective-permute-start.4 = (bf16[2,4,96,128]{3,2,1,0:T(8,128)(2,1)S(1)}, bf16[2,4,96,128]{3,2,1,0:T(8,128)(2,1)S(1)}, u32[]{:S(2)}, u32[]{:S(2)}) collective-permute-start(bf16[2,4,96,128]{3,2,1,0:T(8,128)(2,1)S(1)} %pad_maximum_fusion), channel_id=1, source_target_pairs={{0,8},{1,9},{2,10},{3,11},{4,20},{5,21},{6,22},{7,23},{8,0},{9,1},... | collective-permute-start | bytes 589832 | tf_op jit(solution)/shard_map/kept_by_core/ppermute | solution.py:24
  19.9 0.0 collective-permute-done.8.refs_5_
  19.9 0.0 collective-permute-done.7.refs_2_
  19.9 0.9 %collective-permute-start.9 = (bf16[2,4,96,128]{3,2,1,0:T(8,128)(2,1)S(1)}, bf16[2,4,96,128]{3,2,1,0:T(8,128)(2,1)S(1)}, u32[]{:S(2)}, u32[]{:S(2)}) collective-permute-start(bf16[2,4,96,128]{3,2,1,0:T(8,128)(2,1)S(1)} %collective-permute-done.7.refs_2_), channel_id=1, source_target_pairs={{0,4},{1,5},{2,6},{3,7},{4,0},{5,1},{6,2},{7,3},{8,12},{9,13},{10,... | collective-permute-start | bytes 589832 | tf_op jit(solution)/shard_map/sent_one_over_core/ppermute | solution.py:24
  20.9 0.0 collective-permute-done.10.refs_0_
  20.9 0.0 collective-permute-done.11.refs_1_
  20.9 1.1 %collective-permute-done.9.refs_3_ = bf16[2,4,96,128]{3,2,1,0:T(8,128)(2,1)S(1)} collective-permute-done((bf16[2,4,96,128]{3,2,1,0:T(8,128)(2,1)S(1)}, bf16[2,4,96,128]{3,2,1,0:T(8,128)(2,1)S(1)}, u32[]{:S(2)}, u32[]{:S(2)}) %collective-permute-start.9) | collective-permute-done | bytes 196640 | tf_op jit(solution)/shard_map/sent_one_over_core/ppermute | solution.py:24
  21.9 0.5 %shard_map.41 = f32[4,96,256]{2,1,0:T(8,128)S(1)} custom-call(bf16[4,96,128]{2,1,0:T(8,128)(2,1)S(1)} %get-tuple-element.30.refs_0_, bf16[4,96,128]{2,1,0:T(8,128)(2,1)S(1)} %collective-permute-done.6.refs_1_, bf16[2,4,96,128]{3,2,1,0:T(8,128)(2,1)S(1)} %collective-permute-done.7.refs_2_, bf16[2,4,96,128]{3,2,1,0:T(8,128)(2,1)S(1)} %collective-permute-done.9.refs_3_, ...), custom_call_target="tpu_custom_call" | custom-call | tf_op jit(solution)/shard_map/pallas_call | solution.py:202
  22.5 0.4 %collective-permute-start.14 = (f32[4,96,256]{2,1,0:T(8,128)S(1)}, f32[4,96,256]{2,1,0:T(8,128)S(1)}, u32[]{:S(2)}, u32[]{:S(2)}) collective-permute-start(f32[4,96,256]{2,1,0:T(8,128)S(1)} %shard_map.41), channel_id=1, source_target_pairs={{0,2},{1,3},{2,0},{3,1},{4,5},{5,4},{6,7},{7,6},{8,10},{9,11},{10,... | collective-permute-start | bytes 1179656 | tf_op jit(solution)/shard_map/sums_mine/ppermute | solution.py:24
  22.8 2.5 %collective-permute-start.5 = (bf16[4,96,128]{2,1,0:T(8,128)(2,1)S(1)}, bf16[4,96,128]{2,1,0:T(8,128)(2,1)S(1)}, u32[]{:S(2)}, u32[]{:S(2)}) collective-permute-start(bf16[4,96,128]{2,1,0:T(8,128)(2,1)S(1)} %get-tuple-element.38.refs_0_), channel_id=1, source_target_pairs={{0,24},{1,25},{2,26},{3,27},{4,28},{5,29},{6,30},{7,31},{8,16},{9,... | collective-permute-start | bytes 294920 | tf_op jit(solution)/shard_map/kept_by_three/ppermute | solution.py:24
  25.3 0.5 %shard_map.44 = f32[4,96,256]{2,1,0:T(8,128)S(1)} custom-call(bf16[4,96,128]{2,1,0:T(8,128)(2,1)S(1)} %get-tuple-element.30.refs_0_, bf16[4,96,128]{2,1,0:T(8,128)(2,1)S(1)} %collective-permute-done.6.refs_1_, bf16[2,4,96,128]{3,2,1,0:T(8,128)(2,1)S(1)} %collective-permute-done.7.refs_2_, bf16[2,4,96,128]{3,2,1,0:T(8,128)(2,1)S(1)} %collective-permute-done.9.refs_3_, ...), custom_call_target="tpu_custom_call" | custom-call | tf_op jit(solution)/shard_map/pallas_call | solution.py:202
  25.8 1.8 %collective-permute-start.15 = (f32[4,96,256]{2,1,0:T(8,128)S(1)}, f32[4,96,256]{2,1,0:T(8,128)S(1)}, u32[]{:S(2)}, u32[]{:S(2)}) collective-permute-start(f32[4,96,256]{2,1,0:T(8,128)S(1)} %shard_map.44), channel_id=1, source_target_pairs={{0,1},{1,0},{2,3},{3,2},{4,6},{5,7},{6,4},{7,5},{8,9},{9,8},{10,11... | collective-permute-start | bytes 1179656 | tf_op jit(solution)/shard_map/sums_other/ppermute | solution.py:24
  27.6 2.2 %collective-permute-done.5.refs_4_ = bf16[4,96,128]{2,1,0:T(8,128)(2,1)S(1)} collective-permute-done((bf16[4,96,128]{2,1,0:T(8,128)(2,1)S(1)}, bf16[4,96,128]{2,1,0:T(8,128)(2,1)S(1)}, u32[]{:S(2)}, u32[]{:S(2)}) %collective-permute-start.5) | collective-permute-done | bytes 98336 | tf_op jit(solution)/shard_map/kept_by_three/ppermute | solution.py:24
  29.8 0.0 collective-permute-done.4.refs_2_
  29.8 0.4 %collective-permute-start.12 = (bf16[2,4,96,128]{3,2,1,0:T(8,128)(2,1)S(1)}, bf16[2,4,96,128]{3,2,1,0:T(8,128)(2,1)S(1)}, u32[]{:S(2)}, u32[]{:S(2)}) collective-permute-start(bf16[2,4,96,128]{3,2,1,0:T(8,128)(2,1)S(1)} %collective-permute-done.4.refs_2_), channel_id=1, source_target_pairs={{0,4},{1,5},{2,6},{3,7},{4,0},{5,1},{6,2},{7,3},{8,12},{9,13},{10,... | collective-permute-start | bytes 589832 | tf_op jit(solution)/shard_map/kept_one_over_core/ppermute | solution.py:24
  30.2 0.1 collective-permute-start.13
  30.3 1.2 %collective-permute-done.13.refs_5_ = bf16[4,96,128]{2,1,0:T(8,128)(2,1)S(1)} collective-permute-done((bf16[4,96,128]{2,1,0:T(8,128)(2,1)S(1)}, bf16[4,96,128]{2,1,0:T(8,128)(2,1)S(1)}, u32[]{:S(2)}, u32[]{:S(2)}) %collective-permute-start.13) | collective-permute-done | bytes 98336 | tf_op jit(solution)/shard_map/kept_three_over_core/ppermute | solution.py:24
  31.5 0.0 collective-permute-done.12.refs_3_
  31.5 0.9 %shard_map.42 = (f32[4,96,256]{2,1,0:T(8,128)S(1)}, f32[4,96,256]{2,1,0:T(8,128)S(1)}) custom-call(bf16[4,96,128]{2,1,0:T(8,128)(2,1)S(1)} %get-tuple-element.38.refs_0_, bf16[4,96,128]{2,1,0:T(8,128)(2,1)S(1)} %collective-permute-done.3.refs_1_, bf16[2,4,96,128]{3,2,1,0:T(8,128)(2,1)S(1)} %collective-permute-done.4.refs_2_, ...), custom_call_target="tpu_custom_call" | custom-call | tf_op jit(solution)/shard_map/pallas_call | solution.py:202
  32.4 0.0 collective-permute-done.14.refs_0_
  32.4 1.6 %collective-permute-done.15.arrived_other_ref = f32[4,96,256]{2,1,0:T(8,128)S(1)} collective-permute-done((f32[4,96,256]{2,1,0:T(8,128)S(1)}, f32[4,96,256]{2,1,0:T(8,128)S(1)}, u32[]{:S(2)}, u32[]{:S(2)}) %collective-permute-start.15) | collective-permute-done | bytes 393248 | tf_op jit(solution)/shard_map/sums_other/ppermute | solution.py:24
  34.0 0.8 %shard_map.45 = bf16[8,96,256]{2,1,0:T(8,128)(2,1)} custom-call(f32[4,96,256]{2,1,0:T(8,128)S(1)} %get-tuple-element.43.kept_ref, f32[4,96,256]{2,1,0:T(8,128)S(1)} %get-tuple-element.44.kept_other_ref, f32[4,96,256]{2,1,0:T(8,128)S(1)} %shard_map.43.arrived_ref, f32[4,96,256]{2,1,0:T(8,128)S(1)} %collective-permute-done.15.arrived_other_ref), custom_call_target="tpu_custom_call" | custom-call | tf_op jit(solution)/shard_map/pallas_call | solution.py:238
  (5 shorter events, 0.1 us)
Async XLA Ops:
  0.0 0.9 %copy-start.2 = (bf16[8,384,32]{1,2,0:T(8,128)(2,1)S(1)}, bf16[8,384,32]{1,2,0:T(8,128)(2,1)}, u32[]{:S(2)}) copy-start(bf16[8,384,32]{1,2,0:T(8,128)(2,1)} %param.3) | copy-start | bytes 589828
  0.9 4.7 %copy-start = (bf16[8,256,256]{2,1,0:T(8,128)(2,1)S(1)}, bf16[8,256,256]{2,1,0:T(8,128)(2,1)}, u32[]{:S(2)}) copy-start(bf16[8,256,256]{2,1,0:T(8,128)(2,1)} %integrals_ref.1) | copy-start | bytes 3145732
  0.9 4.7 %copy-start.1 = (s32[8,8]{1,0:T(8,128)S(1)}, s32[8,8]{1,0:T(8,128)}, u32[]{:S(2)}) copy-start(s32[8,8]{1,0:T(8,128)} %mask_ref.1) | copy-start | bytes 772
  1.1 5.8 %collective-permute-start.1 = (bf16[2,96,128]{2,1,0:T(8,128)(2,1)S(1)}, bf16[2,96,128]{2,1,0:T(8,128)(2,1)S(1)}, u32[]{:S(2)}, u32[]{:S(2)}) collective-permute-start(bf16[2,96,128]{2,1,0:T(8,128)(2,1)S(1)} %get-tuple-element.28), channel_id=1, source_target_pairs={{0,2},{1,3},{2,0},{3,1},{4,5},{5,4},{6,7},{7,6},{8,10},{9,11},{10,... | collective-permute-start | bytes 147464 | tf_op jit(solution)/shard_map/lam_other/ppermute | solution.py:24
  4.1 4.3 %collective-permute-start = (bf16[2,96,128]{2,1,0:T(8,128)(2,1)S(1)}, bf16[2,96,128]{2,1,0:T(8,128)(2,1)S(1)}, u32[]{:S(2)}, u32[]{:S(2)}) collective-permute-start(bf16[2,96,128]{2,1,0:T(8,128)(2,1)S(1)} %get-tuple-element.27._), channel_id=1, source_target_pairs={{0,1},{1,0},{2,3},{3,2},{4,6},{5,7},{6,4},{7,5},{8,9},{9,8},{10,11... | collective-permute-start | bytes 147464 | tf_op jit(solution)/shard_map/lam_mine/ppermute | solution.py:24
  5.8 15.1 %collective-permute-start.10 = (bf16[4,256,256]{2,1,0:T(8,128)(2,1)S(1)}, bf16[4,256,256]{2,1,0:T(8,128)(2,1)S(1)}, u32[]{:S(2)}, u32[]{:S(2)}) collective-permute-start(bf16[4,256,256]{2,1,0:T(8,128)(2,1)S(1)} %get-tuple-element.35.refs_6_), channel_id=1, source_target_pairs={{0,1},{1,0},{2,3},{3,2},{4,6},{5,7},{6,4},{7,5},{8,9},{9,8},{10,11... | collective-permute-start | bytes 1572872 | tf_op jit(solution)/shard_map/integrals_mine/ppermute | solution.py:24
  6.4 14.5 %collective-permute-start.11 = (bf16[4,256,256]{2,1,0:T(8,128)(2,1)S(1)}, bf16[4,256,256]{2,1,0:T(8,128)(2,1)S(1)}, u32[]{:S(2)}, u32[]{:S(2)}) collective-permute-start(bf16[4,256,256]{2,1,0:T(8,128)(2,1)S(1)} %get-tuple-element.36.refs_8_.refs_6_), channel_id=1, source_target_pairs={{0,2},{1,3},{2,0},{3,1},{4,5},{5,4},{6,7},{7,6},{8,10},{9,11},{10,... | collective-permute-start | bytes 1572872 | tf_op jit(solution)/shard_map/integrals_other/ppermute | solution.py:24
  8.4 3.9 %collective-permute-start.6 = (bf16[4,96,128]{2,1,0:T(8,128)(2,1)S(1)}, bf16[4,96,128]{2,1,0:T(8,128)(2,1)S(1)}, u32[]{:S(2)}, u32[]{:S(2)}) collective-permute-start(bf16[4,96,128]{2,1,0:T(8,128)(2,1)S(1)} %get-tuple-element.30.refs_0_), channel_id=1, source_target_pairs={{0,4},{1,5},{2,6},{3,7},{4,0},{5,1},{6,2},{7,3},{8,12},{9,13},{10,... | collective-permute-start | bytes 294920 | tf_op jit(solution)/shard_map/sent_own_over_core/ppermute | solution.py:24
  8.5 7.5 %collective-permute-start.2 = (bf16[4,96,128]{2,1,0:T(8,128)(2,1)S(1)}, bf16[4,96,128]{2,1,0:T(8,128)(2,1)S(1)}, u32[]{:S(2)}, u32[]{:S(2)}) collective-permute-start(bf16[4,96,128]{2,1,0:T(8,128)(2,1)S(1)} %get-tuple-element.30.refs_0_), channel_id=1, source_target_pairs={{0,24},{1,25},{2,26},{3,27},{4,28},{5,29},{6,30},{7,31},{8,16},{9,... | collective-permute-start | bytes 294920 | tf_op jit(solution)/shard_map/sent_by_three/ppermute | solution.py:24
  12.2 1.3 %collective-permute-start.3 = (bf16[4,96,128]{2,1,0:T(8,128)(2,1)S(1)}, bf16[4,96,128]{2,1,0:T(8,128)(2,1)S(1)}, u32[]{:S(2)}, u32[]{:S(2)}) collective-permute-start(bf16[4,96,128]{2,1,0:T(8,128)(2,1)S(1)} %get-tuple-element.38.refs_0_), channel_id=1, source_target_pairs={{0,4},{1,5},{2,6},{3,7},{4,0},{5,1},{6,2},{7,3},{8,12},{9,13},{10,... | collective-permute-start | bytes 294920 | tf_op jit(solution)/shard_map/kept_own_over_core/ppermute | solution.py:24
  12.4 7.6 %collective-permute-start.7 = (bf16[2,4,96,128]{3,2,1,0:T(8,128)(2,1)S(1)}, bf16[2,4,96,128]{3,2,1,0:T(8,128)(2,1)S(1)}, u32[]{:S(2)}, u32[]{:S(2)}) collective-permute-start(bf16[2,4,96,128]{3,2,1,0:T(8,128)(2,1)S(1)} %pad_maximum_fusion.1), channel_id=1, source_target_pairs={{0,8},{1,9},{2,10},{3,11},{4,20},{5,21},{6,22},{7,23},{8,0},{9,1},... | collective-permute-start | bytes 589832 | tf_op jit(solution)/shard_map/sent_by_core/ppermute | solution.py:24
  16.0 4.0 %collective-permute-start.8 = (bf16[4,96,128]{2,1,0:T(8,128)(2,1)S(1)}, bf16[4,96,128]{2,1,0:T(8,128)(2,1)S(1)}, u32[]{:S(2)}, u32[]{:S(2)}) collective-permute-start(bf16[4,96,128]{2,1,0:T(8,128)(2,1)S(1)} %collective-permute-done.2.refs_4_), channel_id=1, source_target_pairs={{0,4},{1,5},{2,6},{3,7},{4,0},{5,1},{6,2},{7,3},{8,12},{9,13},{10,... | collective-permute-start | bytes 294920 | tf_op jit(solution)/shard_map/sent_three_over_core/ppermute | solution.py:24
  16.0 13.8 %collective-permute-start.4 = (bf16[2,4,96,128]{3,2,1,0:T(8,128)(2,1)S(1)}, bf16[2,4,96,128]{3,2,1,0:T(8,128)(2,1)S(1)}, u32[]{:S(2)}, u32[]{:S(2)}) collective-permute-start(bf16[2,4,96,128]{3,2,1,0:T(8,128)(2,1)S(1)} %pad_maximum_fusion), channel_id=1, source_target_pairs={{0,8},{1,9},{2,10},{3,11},{4,20},{5,21},{6,22},{7,23},{8,0},{9,1},... | collective-permute-start | bytes 589832 | tf_op jit(solution)/shard_map/kept_by_core/ppermute | solution.py:24
  19.9 2.0 %collective-permute-start.9 = (bf16[2,4,96,128]{3,2,1,0:T(8,128)(2,1)S(1)}, bf16[2,4,96,128]{3,2,1,0:T(8,128)(2,1)S(1)}, u32[]{:S(2)}, u32[]{:S(2)}) collective-permute-start(bf16[2,4,96,128]{3,2,1,0:T(8,128)(2,1)S(1)} %collective-permute-done.7.refs_2_), channel_id=1, source_target_pairs={{0,4},{1,5},{2,6},{3,7},{4,0},{5,1},{6,2},{7,3},{8,12},{9,13},{10,... | collective-permute-start | bytes 589832 | tf_op jit(solution)/shard_map/sent_one_over_core/ppermute | solution.py:24
  22.5 9.9 %collective-permute-start.14 = (f32[4,96,256]{2,1,0:T(8,128)S(1)}, f32[4,96,256]{2,1,0:T(8,128)S(1)}, u32[]{:S(2)}, u32[]{:S(2)}) collective-permute-start(f32[4,96,256]{2,1,0:T(8,128)S(1)} %shard_map.41), channel_id=1, source_target_pairs={{0,2},{1,3},{2,0},{3,1},{4,5},{5,4},{6,7},{7,6},{8,10},{9,11},{10,... | collective-permute-start | bytes 1179656 | tf_op jit(solution)/shard_map/sums_mine/ppermute | solution.py:24
  22.8 7.0 %collective-permute-start.5 = (bf16[4,96,128]{2,1,0:T(8,128)(2,1)S(1)}, bf16[4,96,128]{2,1,0:T(8,128)(2,1)S(1)}, u32[]{:S(2)}, u32[]{:S(2)}) collective-permute-start(bf16[4,96,128]{2,1,0:T(8,128)(2,1)S(1)} %get-tuple-element.38.refs_0_), channel_id=1, source_target_pairs={{0,24},{1,25},{2,26},{3,27},{4,28},{5,29},{6,30},{7,31},{8,16},{9,... | collective-permute-start | bytes 294920 | tf_op jit(solution)/shard_map/kept_by_three/ppermute | solution.py:24
  25.8 8.1 %collective-permute-start.15 = (f32[4,96,256]{2,1,0:T(8,128)S(1)}, f32[4,96,256]{2,1,0:T(8,128)S(1)}, u32[]{:S(2)}, u32[]{:S(2)}) collective-permute-start(f32[4,96,256]{2,1,0:T(8,128)S(1)} %shard_map.44), channel_id=1, source_target_pairs={{0,1},{1,0},{2,3},{3,2},{4,6},{5,7},{6,4},{7,5},{8,9},{9,8},{10,11... | collective-permute-start | bytes 1179656 | tf_op jit(solution)/shard_map/sums_other/ppermute | solution.py:24
  29.8 1.7 %collective-permute-start.12 = (bf16[2,4,96,128]{3,2,1,0:T(8,128)(2,1)S(1)}, bf16[2,4,96,128]{3,2,1,0:T(8,128)(2,1)S(1)}, u32[]{:S(2)}, u32[]{:S(2)}) collective-permute-start(bf16[2,4,96,128]{3,2,1,0:T(8,128)(2,1)S(1)} %collective-permute-done.4.refs_2_), channel_id=1, source_target_pairs={{0,4},{1,5},{2,6},{3,7},{4,0},{5,1},{6,2},{7,3},{8,12},{9,13},{10,... | collective-permute-start | bytes 589832 | tf_op jit(solution)/shard_map/kept_one_over_core/ppermute | solution.py:24
  30.2 1.3 %collective-permute-start.13 = (bf16[4,96,128]{2,1,0:T(8,128)(2,1)S(1)}, bf16[4,96,128]{2,1,0:T(8,128)(2,1)S(1)}, u32[]{:S(2)}, u32[]{:S(2)}) collective-permute-start(bf16[4,96,128]{2,1,0:T(8,128)(2,1)S(1)} %collective-permute-done.5.refs_4_), channel_id=1, source_target_pairs={{0,4},{1,5},{2,6},{3,7},{4,0},{5,1},{6,2},{7,3},{8,12},{9,13},{10,... | collective-permute-start | bytes 294920 | tf_op jit(solution)/shard_map/kept_three_over_core/ppermute | solution.py:24

commit v5 on v4

v5 whole, which is shorter than its diff:
```python
import functools

import jax
import jax.numpy as jnp
from jax import lax
from jax.experimental import pallas as pl
from jax.experimental.pallas import tpu as pltpu
from jax.sharding import PartitionSpec as P

VMEM = pltpu.VMEM
SENT, KEPT = (3, 1, 2), (1, 3, 2)
PARAMS = pltpu.CompilerParams(vmem_limit_bytes=16 << 20)
CHIPS = 4
COST_PACK, COST_JOIN, COST_FAR, COST_FAR_OTHER = 2 * 10**9, 4 * 10**9, 4 * 10**9, 2 * 10**9
COST_SENT, COST_OTHER, COST_KEPT, COST_SUM, TIE_NEAR = 0, 0, 0, 0, 1


def cost(flops):
    return pl.CostEstimate(flops=flops, bytes_accessed=0, transcendentals=0)


def swap(array, pairs, scope):
    with jax.named_scope(scope):
        return lax.ppermute(array, ("loop", "rep"), pairs)


def mark(flops, *arrays):
    return pl.pallas_call(
        lambda *refs: None,
        out_shape=[jax.ShapeDtypeStruct(array.shape, array.dtype) for array in arrays],
        in_specs=[pl.BlockSpec(memory_space=VMEM)] * len(arrays),
        out_specs=[pl.BlockSpec(memory_space=VMEM)] * len(arrays),
        input_output_aliases={i: i for i in range(len(arrays))},
        cost_estimate=cost(flops),
        compiler_params=PARAMS,
    )(*arrays)


def position():
    rep, spot = lax.axis_index("rep"), lax.axis_index("loop")
    return rep // 2, rep % 2, spot // 2, spot % 2


def pack_kernel(halves, lam_ref, sent_ref, kept_ref, to_mine_ref, to_other_ref, turned):
    y, x, _, core = position()
    rows = turned.shape[2]
    for kind in range(2):
        block = jnp.concatenate([lam_ref[kind * halves + h] for h in range(halves)], axis=0)
        flipped = block.T
        for quarter in range(4):
            turned[kind, quarter] = flipped[quarter * rows : (quarter + 1) * rows]
    kept, over_x, over_y, over_both = y * 2 + x, y * 2 + 1 - x, (1 - y) * 2 + x, (1 - y) * 2 + 1 - x
    for slot, (kind, to_ref) in enumerate(((core, to_mine_ref), (1 - core, to_other_ref))):
        summed, fetched = jnp.where(kind == 0, over_y, over_x), jnp.where(kind == 0, over_x, over_y)
        sent_ref[slot] = turned[kind, summed]
        kept_ref[slot] = turned[kind, kept]
        to_ref[0] = turned[kind, over_both]
        to_ref[1] = turned[kind, fetched]


def split_kernel(mask_ref, integrals_ref, _, mine_ref, other_ref):
    irreps, blocks = mask_ref.shape
    halves = irreps // 2
    _, depth, columns = integrals_ref.shape
    core = position()[3]
    for kind, out_ref in ((core, mine_ref), (1 - core, other_ref)):
        live = mask_ref[pl.ds(kind * halves, halves)].astype(jnp.float32)
        for h in range(halves):
            for b in range(blocks):
                rows = slice(b * depth // blocks, (b + 1) * depth // blocks)
                factor = jnp.broadcast_to(live[h : h + 1, b : b + 1], (depth // blocks, columns)).astype(jnp.bfloat16)
                out_ref[h, rows] = integrals_ref[kind * halves + h, rows] * factor


def join_kernel(sent_own_ref, kept_own_ref, far_mine_ref, far_other_ref, sent_ref, sent_far_ref, kept_ref):
    for which, (own_ref, out_ref) in enumerate(((sent_own_ref, sent_ref), (kept_own_ref, kept_ref))):
        for slot, ref in enumerate((far_mine_ref, far_other_ref)):
            out_ref[slot] = own_ref[slot]
            out_ref[2 + slot] = ref[which]
    sent_far_ref[0] = far_mine_ref[0]
    sent_far_ref[1] = far_other_ref[0]


def product_kernel(kinds, hops, held, names, *refs):
    count = len(names)
    messages, integrals_refs, rest = dict(zip(names, refs)), refs[count : count + 2 * len(kinds)], refs[count + 2 * len(kinds) :]
    before, out_refs = (rest[: len(kinds)], rest[len(kinds) :]) if held else (None, rest)
    _, _, z, core = position()
    by_core = jnp.where(core == 0, hops[1], hops[2])
    passed = jnp.where(core == 0, hops[2], hops[1])
    parts = []
    for name, ref in messages.items():
        layers = (0,) if "near" in name else (1,) if "far" in name else (0, 1)
        if "one" in name.split("_"):
            parts += [(ref.at[0], by_core, False, layers), (ref.at[1], by_core, True, layers)]
        elif "two" in name:
            parts += [(ref.at[0], passed, True, layers), (ref.at[1], passed, False, layers)]
        else:
            parts.append((ref, hops[0] if "alone" in name else 0, "sibling" in name, layers))
    for slot, kind in enumerate(kinds):
        integrals = integrals_refs[2 * slot : 2 * slot + 2]
        halves = integrals[0].shape[0]
        depth = messages[names[0]].shape[-1] // halves
        for h in range(halves):
            lam, kept = [], []
            for layer in range(2):
                for ref, hop, from_sibling, layers in parts:
                    if layer in layers:
                        block = (z ^ hop) * 2 + (1 - core if from_sibling else core)
                        unit = 2 * layers.index(layer) + (1 - kind if from_sibling else kind)
                        lam.append(ref[unit][:, h * depth : (h + 1) * depth])
                        kept.append(integrals[layer][h, pl.ds(pl.multiple_of(block * depth, depth), depth)])
            value = jnp.dot(
                jnp.concatenate(lam, axis=1), jnp.concatenate(kept, axis=0), preferred_element_type=jnp.float32
            )
            out_refs[slot][h] = before[slot][h] + value if held else value


def total_kernel(kept_ref, kept_other_ref, arrived_ref, arrived_other_ref, out_ref, rounded, done):
    core = position()[3]
    halves = kept_ref.shape[0]
    copies = []
    for kind, kept, arrived in ((0, kept_ref, arrived_ref), (1, kept_other_ref, arrived_other_ref)):
        at = (1 - core if kind else core) * halves
        for h in range(halves):
            step = kind * halves + h
            rounded[step] = (kept[h] + arrived[h]).astype(rounded.dtype)
            copies.append(pltpu.make_async_copy(rounded.at[step], out_ref.at[at + h], done.at[step]))
            copies[-1].start()
    for copy in copies:
        copy.wait()


def square(lam, integrals, block_mask):
    irreps, occ, depth = lam.shape
    halves = irreps // 2
    rows = occ // 4
    columns = integrals.shape[2]
    loops = 2 * CHIPS
    bf16, f32 = jnp.bfloat16, jnp.float32
    lanes = halves * depth
    in_vmem = pl.BlockSpec(memory_space=VMEM)
    quarters = jax.ShapeDtypeStruct((2, rows, lanes), bf16)
    half = jax.ShapeDtypeStruct((halves,) + integrals.shape[1:], bf16)
    sums = jax.ShapeDtypeStruct((halves, rows, columns), f32)

    def pairs(aim):
        places = [(s, r) for s in range(loops) for r in range(4)]
        return [(at, places.index(aim(s, r, s % 2))) for at, (s, r) in enumerate(places)]

    over_core = pairs(lambda s, r, core: (s ^ 1, r))
    fetch = pairs(lambda s, r, core: (s, r ^ (1 + core)))
    reduce = pairs(lambda s, r, core: (s, r ^ (2 - core)))
    alone = lambda hops: pairs(lambda s, r, core: (s ^ (2 * hops[0]), r))
    by_core = lambda hops: pairs(lambda s, r, core: (s ^ (2 * hops[1 + core]), r))

    sent_own, kept_own, to_mine, to_other = pl.pallas_call(
        functools.partial(pack_kernel, halves),
        out_shape=[quarters] * 4,
        in_specs=[in_vmem],
        out_specs=[in_vmem] * 4,
        scratch_shapes=[VMEM((2, 4, rows, lanes), bf16)],
        cost_estimate=cost(COST_PACK),
        compiler_params=PARAMS,
    )(lam.transpose(0, 2, 1))
    far_mine = swap(to_mine, fetch, "lam_mine")
    far_other = swap(to_other, reduce, "lam_other")

    near_sibling = swap(sent_own, over_core, "sent_near_over_core")
    one_near = swap(jnp.stack([sent_own, near_sibling]), by_core(SENT), "sent_near_by_core")

    near, near_other = pl.pallas_call(
        split_kernel,
        out_shape=[half] * 2,
        in_specs=[in_vmem, in_vmem, pl.BlockSpec(memory_space=pl.ANY)],
        out_specs=[in_vmem] * 2,
        compiler_params=PARAMS,
    )(block_mask, integrals, to_mine)
    far = swap(near, fetch, "integrals_mine")
    if TIE_NEAR == 1:
        near_other, one_near = lax.optimization_barrier((near_other, one_near))
    far_other_integrals = swap(near_other, reduce, "integrals_other")

    message = jax.ShapeDtypeStruct((4, rows, lanes), bf16)
    sent, sent_far, kept = pl.pallas_call(
        join_kernel,
        out_shape=[message, quarters, message],
        in_specs=[in_vmem] * 4,
        out_specs=[in_vmem] * 3,
        cost_estimate=cost(COST_JOIN),
        compiler_params=PARAMS,
    )(sent_own, kept_own, far_mine, far_other)

    def over_cores(array, scope):
        return swap(array, over_core, scope + "_over_core")

    def for_chip(own, sibling, hops, scope):
        return swap(jnp.stack([own, sibling]), by_core(hops), scope + "_by_core")

    def product(parts, kinds, hops, flops, before=()):
        given = [(near, far), (near_other, far_other_integrals)]
        return pl.pallas_call(
            functools.partial(product_kernel, kinds, hops, bool(before), tuple(parts)),
            out_shape=[sums] * len(kinds),
            in_specs=[in_vmem] * (len(parts) + 2 * len(kinds) + len(before)),
            out_specs=[in_vmem] * len(kinds),
            cost_estimate=cost(flops),
            compiler_params=PARAMS,
        )(*parts.values(), *(array for kind in kinds for array in given[kind]), *before)

    parts = dict(own=sent, sibling_near=near_sibling)
    parts["sibling_far"] = over_cores(sent_far, "sent_far")
    parts["alone"] = swap(sent, alone(SENT), "sent_alone")
    parts["one_far"] = for_chip(sent_far, parts["sibling_far"], SENT, "sent_far")
    kept_sibling = over_cores(kept, "kept")
    parts["alone"], kept_sibling = lax.optimization_barrier((parts["alone"], kept_sibling))
    kept_parts = dict(own=kept, sibling=kept_sibling)
    kept_parts["one"] = for_chip(kept, kept_sibling, KEPT, "kept")
    if COST_FAR:
        (far,) = mark(COST_FAR, far)
    if COST_FAR_OTHER:
        (far_other_integrals,) = mark(COST_FAR_OTHER, far_other_integrals)
    parts["alone_sibling"] = over_cores(parts["alone"], "sent_alone")
    parts["one_far"], parts["alone_sibling"] = lax.optimization_barrier((parts["one_far"], parts["alone_sibling"]))
    parts["one_near"], parts["two_near"] = one_near, over_cores(one_near, "sent_near_one")
    last = dict(two_far=over_cores(parts["one_far"], "sent_far_one"))
    sent_parts = parts
    (sent,) = product(last, (0,), SENT, COST_SENT, product(sent_parts, (0,), SENT, COST_SENT))
    (first_other,) = product(sent_parts, (1,), SENT, COST_OTHER)
    kept, first_other = lax.optimization_barrier((kept, first_other))
    kept_parts["alone"] = swap(kept, alone(KEPT), "kept_alone")
    (sent_other,) = product(last, (1,), SENT, COST_OTHER, (first_other,))
    sum_mine = swap(sent, reduce, "sums_mine")
    sum_other = swap(sent_other, fetch, "sums_other")
    if COST_SUM:
        (sum_mine,) = mark(COST_SUM, sum_mine)
    kept_parts, sent = lax.optimization_barrier((kept_parts, sent))
    kept_parts["two"] = over_cores(kept_parts["one"], "kept_one")
    kept_parts["alone_sibling"] = over_cores(kept_parts["alone"], "kept_alone")
    last = {name: kept_parts.pop(name) for name in ("alone", "alone_sibling")}
    kept, kept_other = product(last, (0, 1), KEPT, COST_KEPT, product(kept_parts, (0, 1), KEPT, COST_KEPT))
    return pl.pallas_call(
        total_kernel,
        out_shape=jax.ShapeDtypeStruct((irreps, rows, columns), bf16),
        in_specs=[in_vmem] * 4,
        out_specs=pl.BlockSpec(memory_space=pl.ANY),
        scratch_shapes=[VMEM((irreps, rows, columns), bf16), pltpu.SemaphoreType.DMA((irreps,))],
        compiler_params=PARAMS,
    )(kept, kept_other, sum_mine, sum_other)


def general(lam, integrals, block_mask):
    live = jnp.repeat(block_mask, lam.shape[2], axis=1) == 1
    kept = jnp.where(live[:, :, None], integrals, jnp.zeros_like(integrals))
    layer_lam = lax.all_gather(lam, "loop", axis=2, tiled=True)
    partial_sum = jnp.einsum("hpk,hka->hpa", layer_lam, kept, preferred_element_type=jnp.float32)
    return lax.psum_scatter(partial_sum, "rep", scatter_dimension=1, tiled=True).astype(jnp.bfloat16)


def solution(mesh):
    return jax.shard_map(
        square if (mesh.shape["rep"], mesh.shape["loop"]) == (4, 2 * CHIPS) else general,
        mesh=mesh,
        in_specs=(P(None, None, ("rep", "loop")), P(None, "rep", "loop"), P(None, "rep")),
        out_specs=P(None, "rep", "loop"),
        check_vma=False,
    )
```

time: 34.9 us -> 34.2 us (0.980)
  waiting for transfers between devices: 11.1 us -> 9.63 us
  Pallas kernels: 3.07 us -> 3.56 us
    ppermute x16 -> x19, waiting for transfers between devices: 11.1 us -> 9.63 us  [swap(): return lax.ppermute(array, ('loop', 'rep'), pairs)]
    pallas_call x4 -> x7, Pallas kernels: 1.95 us -> 2.44 us  [the longest x6 2.41 us: product(): pl.pallas_call(functools.partial(product_kernel, kinds, hops, bool(before...]
    ppermute x16 -> x19, starting transfers between devices: 19.6 us -> 19.8 us  [swap(): return lax.ppermute(array, ('loop', 'rep'), pairs)]
  transfers between devices with their start and end apart: 16 -> 19, of which waited for: 7 -> 7; matrix products, arithmetic and copies ran while one was open for 0% -> 0% of each run, Pallas kernels for 6% -> 8%
where the time goes in v5:
time: 34.2 us; the launch traced here: 34.1 us
  starting transfers between devices  19.8 us (58%)
  waiting for transfers between devices  9.63 us (28%)
  Pallas kernels  3.56 us (10%)
  local copies, waits for them, and re-layouts  0.94 us (3%)
    ppermute x19, starting transfers between devices, swap(): return lax.ppermute(array, ('loop', 'rep'), pairs)  19.8 us
    ppermute x19, waiting for transfers between devices, swap(): return lax.ppermute(array, ('loop', 'rep'), pairs)  9.63 us
    pallas_call x6, Pallas kernels, product(): pl.pallas_call(functools.partial(product_kernel, kinds, hops, bool(before...  2.41 us
    unnamed x6, local copies, waits for them, and re-layouts  0.94 us
    pallas_call x1, Pallas kernels, square(): pl.pallas_call(total_kernel, out_shape=jax.ShapeDtypeStruct((irreps, rows...  0.82 us
  transfers between devices with their start and end apart: 19, of which 7 were waited for; matrix products, arithmetic and copies ran while one was open for 0% of the time, Pallas kernels for 8%

profile of v5, /device:TPU:0, one launch (start us, length us, event | category | flops | bytes accessed | tf_op | source)
XLA Modules:
  0.0 34.1 jit_solution(6044916804468158704)
XLA Ops:
  0.0 0.9 %copy-done.2 = bf16[8,384,32]{1,2,0:T(8,128)(2,1)S(1)} copy-done((bf16[8,384,32]{1,2,0:T(8,128)(2,1)S(1)}, bf16[8,384,32]{1,2,0:T(8,128)(2,1)}, u32[]{:S(2)}) %copy-start.2) | copy-done | bytes 196632
  0.9 0.1 shard_map.37
  1.1 0.0 copy-start.1
  1.1 0.5 %collective-permute-start.2 = (bf16[2,96,128]{2,1,0:T(8,128)(2,1)S(1)}, bf16[2,96,128]{2,1,0:T(8,128)(2,1)S(1)}, u32[]{:S(2)}, u32[]{:S(2)}) collective-permute-start(bf16[2,96,128]{2,1,0:T(8,128)(2,1)S(1)} %get-tuple-element.30.sent_own_ref), channel_id=1, source_target_pairs={{0,4},{1,5},{2,6},{3,7},{4,0},{5,1},{6,2},{7,3},{8,12},{9,13},{10,... | collective-permute-start | bytes 147464 | tf_op jit(solution)/shard_map/sent_near_over_core/ppermute | solution.py:24
  1.6 2.6 %collective-permute-start.1 = (bf16[2,96,128]{2,1,0:T(8,128)(2,1)S(1)}, bf16[2,96,128]{2,1,0:T(8,128)(2,1)S(1)}, u32[]{:S(2)}, u32[]{:S(2)}) collective-permute-start(bf16[2,96,128]{2,1,0:T(8,128)(2,1)S(1)} %get-tuple-element.33), channel_id=1, source_target_pairs={{0,2},{1,3},{2,0},{3,1},{4,5},{5,4},{6,7},{7,6},{8,10},{9,11},{10,... | collective-permute-start | bytes 147464 | tf_op jit(solution)/shard_map/lam_other/ppermute | solution.py:24
  4.2 1.5 %collective-permute-start = (bf16[2,96,128]{2,1,0:T(8,128)(2,1)S(1)}, bf16[2,96,128]{2,1,0:T(8,128)(2,1)S(1)}, u32[]{:S(2)}, u32[]{:S(2)}) collective-permute-start(bf16[2,96,128]{2,1,0:T(8,128)(2,1)S(1)} %get-tuple-element.32._), channel_id=1, source_target_pairs={{0,1},{1,0},{2,3},{3,2},{4,6},{5,7},{6,4},{7,5},{8,9},{9,8},{10,11... | collective-permute-start | bytes 147464 | tf_op jit(solution)/shard_map/lam_mine/ppermute | solution.py:24
  5.7 0.2 shard_map.39
  5.9 0.6 %collective-permute-start.14 = (bf16[4,256,256]{2,1,0:T(8,128)(2,1)S(1)}, bf16[4,256,256]{2,1,0:T(8,128)(2,1)S(1)}, u32[]{:S(2)}, u32[]{:S(2)}) collective-permute-start(bf16[4,256,256]{2,1,0:T(8,128)(2,1)S(1)} %get-tuple-element.45.refs_8_.refs_1_.refs_4_.refs_2_), channel_id=1, source_target_pairs={{0,1},{1,0},{2,3},{3,2},{4,6},{5,7},{6,4},{7,5},{8,9},{9,8},{10,11... | collective-permute-start | bytes 1572872 | tf_op jit(solution)/shard_map/integrals_mine/ppermute | solution.py:24
  6.5 0.0 collective-permute-done.2.refs_1_
  6.5 1.6 %collective-permute-start.8 = (bf16[2,2,96,128]{3,2,1,0:T(8,128)(2,1)S(1)}, bf16[2,2,96,128]{3,2,1,0:T(8,128)(2,1)S(1)}, u32[]{:S(2)}, u32[]{:S(2)}) collective-permute-start(bf16[2,2,96,128]{3,2,1,0:T(8,128)(2,1)S(1)} %pad_maximum_fusion.2), channel_id=1, source_target_pairs={{0,8},{1,9},{2,10},{3,11},{4,20},{5,21},{6,22},{7,23},{8,0},{9,1},... | collective-permute-start | bytes 294920 | tf_op jit(solution)/shard_map/sent_near_by_core/ppermute | solution.py:24
  8.1 0.0 collective-permute-done.1.far_other_ref
  8.1 0.1 collective-permute-done.far_mine_ref
  8.3 0.2 collective-permute-start.3
  8.5 3.5 %collective-permute-start.4 = (bf16[4,96,128]{2,1,0:T(8,128)(2,1)S(1)}, bf16[4,96,128]{2,1,0:T(8,128)(2,1)S(1)}, u32[]{:S(2)}, u32[]{:S(2)}) collective-permute-start(bf16[4,96,128]{2,1,0:T(8,128)(2,1)S(1)} %get-tuple-element.35.refs_0_), channel_id=1, source_target_pairs={{0,24},{1,25},{2,26},{3,27},{4,28},{5,29},{6,30},{7,31},{8,16},{9,... | collective-permute-start | bytes 294920 | tf_op jit(solution)/shard_map/sent_alone/ppermute | solution.py:24
  12.0 0.2 collective-permute-start.5
  12.2 0.0 collective-permute-done.8.refs_6_
  12.2 0.5 %collective-permute-start.10 = (bf16[4,256,256]{2,1,0:T(8,128)(2,1)S(1)}, bf16[4,256,256]{2,1,0:T(8,128)(2,1)S(1)}, u32[]{:S(2)}, u32[]{:S(2)}) collective-permute-start(bf16[4,256,256]{2,1,0:T(8,128)(2,1)S(1)} %get-tuple-element.42.refs_8_.refs_6_.refs_4_.refs_1_), channel_id=1, source_target_pairs={{0,2},{1,3},{2,0},{3,1},{4,5},{5,4},{6,7},{7,6},{8,10},{9,11},{10,... | collective-permute-start | bytes 1572872 | tf_op jit(solution)/shard_map/integrals_other/ppermute | solution.py:24
  12.7 0.0 collective-permute-done.3.refs_2_
  12.8 1.1 %collective-permute-start.6 = (bf16[2,2,96,128]{3,2,1,0:T(8,128)(2,1)S(1)}, bf16[2,2,96,128]{3,2,1,0:T(8,128)(2,1)S(1)}, u32[]{:S(2)}, u32[]{:S(2)}) collective-permute-start(bf16[2,2,96,128]{3,2,1,0:T(8,128)(2,1)S(1)} %pad_maximum_fusion.1), channel_id=1, source_target_pairs={{0,8},{1,9},{2,10},{3,11},{4,20},{5,21},{6,22},{7,23},{8,0},{9,1},... | collective-permute-start | bytes 294920 | tf_op jit(solution)/shard_map/sent_far_by_core/ppermute | solution.py:24
  13.8 1.7 %collective-permute-done.4.refs_3_ = bf16[4,96,128]{2,1,0:T(8,128)(2,1)S(1)} collective-permute-done((bf16[4,96,128]{2,1,0:T(8,128)(2,1)S(1)}, bf16[4,96,128]{2,1,0:T(8,128)(2,1)S(1)}, u32[]{:S(2)}, u32[]{:S(2)}) %collective-permute-start.4) | collective-permute-done | bytes 98336 | tf_op jit(solution)/shard_map/sent_alone/ppermute | solution.py:24
  15.5 0.0 collective-permute-done.5.refs_2_
  15.5 0.0 collective-permute-start.7
  15.6 4.1 %collective-permute-start.12 = (bf16[2,4,96,128]{3,2,1,0:T(8,128)(2,1)S(1)}, bf16[2,4,96,128]{3,2,1,0:T(8,128)(2,1)S(1)}, u32[]{:S(2)}, u32[]{:S(2)}) collective-permute-start(bf16[2,4,96,128]{3,2,1,0:T(8,128)(2,1)S(1)} %pad_maximum_fusion), channel_id=1, source_target_pairs={{0,24},{1,25},{2,26},{3,27},{4,20},{5,21},{6,22},{7,23},{8,16},{9,... | collective-permute-start | bytes 589832 | tf_op jit(solution)/shard_map/kept_by_core/ppermute | solution.py:24
  19.6 0.0 collective-permute-done.6.refs_4_
  19.6 0.5 %collective-permute-start.9 = (bf16[2,2,96,128]{3,2,1,0:T(8,128)(2,1)S(1)}, bf16[2,2,96,128]{3,2,1,0:T(8,128)(2,1)S(1)}, u32[]{:S(2)}, u32[]{:S(2)}) collective-permute-start(bf16[2,2,96,128]{3,2,1,0:T(8,128)(2,1)S(1)} %collective-permute-done.8.refs_6_), channel_id=1, source_target_pairs={{0,4},{1,5},{2,6},{3,7},{4,0},{5,1},{6,2},{7,3},{8,12},{9,13},{10,... | collective-permute-start | bytes 294920 | tf_op jit(solution)/shard_map/sent_near_one_over_core/ppermute | solution.py:24
  20.2 0.0 collective-permute-done.7.refs_5_
  20.2 0.1 collective-permute-start.13
  20.3 0.9 %collective-permute-done.9.refs_7_ = bf16[2,2,96,128]{3,2,1,0:T(8,128)(2,1)S(1)} collective-permute-done((bf16[2,2,96,128]{3,2,1,0:T(8,128)(2,1)S(1)}, bf16[2,2,96,128]{3,2,1,0:T(8,128)(2,1)S(1)}, u32[]{:S(2)}, u32[]{:S(2)}) %collective-permute-start.9) | collective-permute-done | bytes 98336 | tf_op jit(solution)/shard_map/sent_near_one_over_core/ppermute | solution.py:24
  21.1 0.4 %shard_map.43.refs_3_ = f32[4,96,256]{2,1,0:T(8,128)S(1)} custom-call(bf16[4,96,128]{2,1,0:T(8,128)(2,1)S(1)} %get-tuple-element.35.refs_0_, bf16[2,96,128]{2,1,0:T(8,128)(2,1)S(1)} %collective-permute-done.2.refs_1_, bf16[2,96,128]{2,1,0:T(8,128)(2,1)S(1)} %collective-permute-done.3.refs_2_, bf16[4,96,128]{2,1,0:T(8,128)(2,1)S(1)} %collective-permute-done.4.refs_3_, ...), custom_call_target="tpu_custom_call" | custom-call | tf_op jit(solution)/shard_map/pallas_call | solution.py:202
  21.6 0.0 collective-permute-done.13.refs_0_
  21.6 0.3 shard_map.44
  21.8 0.9 %collective-permute-start.17 = (f32[4,96,256]{2,1,0:T(8,128)S(1)}, f32[4,96,256]{2,1,0:T(8,128)S(1)}, u32[]{:S(2)}, u32[]{:S(2)}) collective-permute-start(f32[4,96,256]{2,1,0:T(8,128)S(1)} %shard_map.44), channel_id=1, source_target_pairs={{0,2},{1,3},{2,0},{3,1},{4,5},{5,4},{6,7},{7,6},{8,10},{9,11},{10,... | collective-permute-start | bytes 1179656 | tf_op jit(solution)/shard_map/sums_mine/ppermute | solution.py:24
  22.8 0.0 collective-permute-done.10.refs_0_
  22.8 0.5 %shard_map.41.refs_3_ = f32[4,96,256]{2,1,0:T(8,128)S(1)} custom-call(bf16[4,96,128]{2,1,0:T(8,128)(2,1)S(1)} %get-tuple-element.35.refs_0_, bf16[2,96,128]{2,1,0:T(8,128)(2,1)S(1)} %collective-permute-done.2.refs_1_, bf16[2,96,128]{2,1,0:T(8,128)(2,1)S(1)} %collective-permute-done.3.refs_2_, bf16[4,96,128]{2,1,0:T(8,128)(2,1)S(1)} %collective-permute-done.4.refs_3_, ...), custom_call_target="tpu_custom_call" | custom-call | tf_op jit(solution)/shard_map/pallas_call | solution.py:202
  23.2 0.3 shard_map.47
  23.5 0.6 %collective-permute-start.18 = (f32[4,96,256]{2,1,0:T(8,128)S(1)}, f32[4,96,256]{2,1,0:T(8,128)S(1)}, u32[]{:S(2)}, u32[]{:S(2)}) collective-permute-start(f32[4,96,256]{2,1,0:T(8,128)S(1)} %shard_map.47), channel_id=1, source_target_pairs={{0,1},{1,0},{2,3},{3,2},{4,6},{5,7},{6,4},{7,5},{8,9},{9,8},{10,11... | collective-permute-start | bytes 1179656 | tf_op jit(solution)/shard_map/sums_other/ppermute | solution.py:24
  24.1 0.8 %collective-permute-start.11 = (bf16[4,96,128]{2,1,0:T(8,128)(2,1)S(1)}, bf16[4,96,128]{2,1,0:T(8,128)(2,1)S(1)}, u32[]{:S(2)}, u32[]{:S(2)}) collective-permute-start(bf16[4,96,128]{2,1,0:T(8,128)(2,1)S(1)} %get-tuple-element.48.refs_1_), channel_id=1, source_target_pairs={{0,8},{1,9},{2,10},{3,11},{4,12},{5,13},{6,14},{7,15},{8,0},{9,1},... | collective-permute-start | bytes 294920 | tf_op jit(solution)/shard_map/kept_alone/ppermute | solution.py:24
  24.9 0.0 collective-permute-done.12.refs_0_
  24.9 5.3 %collective-permute-done.11.refs_0_ = bf16[4,96,128]{2,1,0:T(8,128)(2,1)S(1)} collective-permute-done((bf16[4,96,128]{2,1,0:T(8,128)(2,1)S(1)}, bf16[4,96,128]{2,1,0:T(8,128)(2,1)S(1)}, u32[]{:S(2)}, u32[]{:S(2)}) %collective-permute-start.11) | collective-permute-done | bytes 98336 | tf_op jit(solution)/shard_map/kept_alone/ppermute | solution.py:24
  30.2 0.0 collective-permute-start.16
  30.2 0.5 %collective-permute-start.15 = (bf16[4,96,128]{2,1,0:T(8,128)(2,1)S(1)}, bf16[4,96,128]{2,1,0:T(8,128)(2,1)S(1)}, u32[]{:S(2)}, u32[]{:S(2)}) collective-permute-start(bf16[4,96,128]{2,1,0:T(8,128)(2,1)S(1)} %collective-permute-done.11.refs_0_), channel_id=1, source_target_pairs={{0,4},{1,5},{2,6},{3,7},{4,0},{5,1},{6,2},{7,3},{8,12},{9,13},{10,... | collective-permute-start | bytes 294920 | tf_op jit(solution)/shard_map/kept_alone_over_core/ppermute | solution.py:24
  30.7 0.9 %collective-permute-done.16.refs_3_ = bf16[2,4,96,128]{3,2,1,0:T(8,128)(2,1)S(1)} collective-permute-done((bf16[2,4,96,128]{3,2,1,0:T(8,128)(2,1)S(1)}, bf16[2,4,96,128]{3,2,1,0:T(8,128)(2,1)S(1)}, u32[]{:S(2)}, u32[]{:S(2)}) %collective-permute-start.16) | collective-permute-done | bytes 196640 | tf_op jit(solution)/shard_map/kept_one_over_core/ppermute | solution.py:24
  31.6 0.6 %shard_map.45 = (f32[4,96,256]{2,1,0:T(8,128)S(1)}, f32[4,96,256]{2,1,0:T(8,128)S(1)}) custom-call(bf16[2,4,96,128]{3,2,1,0:T(8,128)(2,1)S(1)} %collective-permute-done.12.refs_0_, bf16[4,96,128]{2,1,0:T(8,128)(2,1)S(1)} %get-tuple-element.48.refs_1_, bf16[4,96,128]{2,1,0:T(8,128)(2,1)S(1)} %collective-permute-done.5.refs_2_, ...), custom_call_target="tpu_custom_call" | custom-call | tf_op jit(solution)/shard_map/pallas_call | solution.py:202
  32.3 0.0 collective-permute-done.15.refs_1_
  32.3 0.4 %shard_map.46 = (f32[4,96,256]{2,1,0:T(8,128)S(1)}, f32[4,96,256]{2,1,0:T(8,128)S(1)}) custom-call(bf16[4,96,128]{2,1,0:T(8,128)(2,1)S(1)} %collective-permute-done.11.refs_0_, bf16[4,96,128]{2,1,0:T(8,128)(2,1)S(1)} %collective-permute-done.15.refs_1_, bf16[4,256,256]{2,1,0:T(8,128)(2,1)S(1)} %get-tuple-element.45.refs_8_.refs_1_.refs_4_.refs_2_, ...), custom_call_target="tpu_custom_call" | custom-call | tf_op jit(solution)/shard_map/pallas_call | solution.py:202
  32.6 0.3 collective-permute-done.17.arrived_ref
  32.9 0.4 %collective-permute-done.18.arrived_other_ref = f32[4,96,256]{2,1,0:T(8,128)S(1)} collective-permute-done((f32[4,96,256]{2,1,0:T(8,128)S(1)}, f32[4,96,256]{2,1,0:T(8,128)S(1)}, u32[]{:S(2)}, u32[]{:S(2)}) %collective-permute-start.18) | collective-permute-done | bytes 393248 | tf_op jit(solution)/shard_map/sums_other/ppermute | solution.py:24
  33.3 0.8 %shard_map.48 = bf16[8,96,256]{2,1,0:T(8,128)(2,1)} custom-call(f32[4,96,256]{2,1,0:T(8,128)S(1)} %get-tuple-element.52.kept_ref, f32[4,96,256]{2,1,0:T(8,128)S(1)} %get-tuple-element.53.kept_other_ref, f32[4,96,256]{2,1,0:T(8,128)S(1)} %collective-permute-done.17.arrived_ref, f32[4,96,256]{2,1,0:T(8,128)S(1)} %collective-permute-done.18.arrived_other_ref), custom_call_target="tpu_custom_call" | custom-call | tf_op jit(solution)/shard_map/pallas_call | solution.py:242
  (11 shorter events, 0.1 us)
Async XLA Ops:
  0.0 0.9 %copy-start.2 = (bf16[8,384,32]{1,2,0:T(8,128)(2,1)S(1)}, bf16[8,384,32]{1,2,0:T(8,128)(2,1)}, u32[]{:S(2)}) copy-start(bf16[8,384,32]{1,2,0:T(8,128)(2,1)} %param.3) | copy-start | bytes 589828
  0.9 4.7 %copy-start = (bf16[8,256,256]{2,1,0:T(8,128)(2,1)S(1)}, bf16[8,256,256]{2,1,0:T(8,128)(2,1)}, u32[]{:S(2)}) copy-start(bf16[8,256,256]{2,1,0:T(8,128)(2,1)} %integrals_ref.1) | copy-start | bytes 3145732
  1.1 4.6 %copy-start.1 = (s32[8,8]{1,0:T(8,128)S(1)}, s32[8,8]{1,0:T(8,128)}, u32[]{:S(2)}) copy-start(s32[8,8]{1,0:T(8,128)} %mask_ref.1) | copy-start | bytes 772
  1.1 5.4 %collective-permute-start.2 = (bf16[2,96,128]{2,1,0:T(8,128)(2,1)S(1)}, bf16[2,96,128]{2,1,0:T(8,128)(2,1)S(1)}, u32[]{:S(2)}, u32[]{:S(2)}) collective-permute-start(bf16[2,96,128]{2,1,0:T(8,128)(2,1)S(1)} %get-tuple-element.30.sent_own_ref), channel_id=1, source_target_pairs={{0,4},{1,5},{2,6},{3,7},{4,0},{5,1},{6,2},{7,3},{8,12},{9,13},{10,... | collective-permute-start | bytes 147464 | tf_op jit(solution)/shard_map/sent_near_over_core/ppermute | solution.py:24
  1.6 6.6 %collective-permute-start.1 = (bf16[2,96,128]{2,1,0:T(8,128)(2,1)S(1)}, bf16[2,96,128]{2,1,0:T(8,128)(2,1)S(1)}, u32[]{:S(2)}, u32[]{:S(2)}) collective-permute-start(bf16[2,96,128]{2,1,0:T(8,128)(2,1)S(1)} %get-tuple-element.33), channel_id=1, source_target_pairs={{0,2},{1,3},{2,0},{3,1},{4,5},{5,4},{6,7},{7,6},{8,10},{9,11},{10,... | collective-permute-start | bytes 147464 | tf_op jit(solution)/shard_map/lam_other/ppermute | solution.py:24
  4.2 4.1 %collective-permute-start = (bf16[2,96,128]{2,1,0:T(8,128)(2,1)S(1)}, bf16[2,96,128]{2,1,0:T(8,128)(2,1)S(1)}, u32[]{:S(2)}, u32[]{:S(2)}) collective-permute-start(bf16[2,96,128]{2,1,0:T(8,128)(2,1)S(1)} %get-tuple-element.32._), channel_id=1, source_target_pairs={{0,1},{1,0},{2,3},{3,2},{4,6},{5,7},{6,4},{7,5},{8,9},{9,8},{10,11... | collective-permute-start | bytes 147464 | tf_op jit(solution)/shard_map/lam_mine/ppermute | solution.py:24
  5.9 14.4 %collective-permute-start.14 = (bf16[4,256,256]{2,1,0:T(8,128)(2,1)S(1)}, bf16[4,256,256]{2,1,0:T(8,128)(2,1)S(1)}, u32[]{:S(2)}, u32[]{:S(2)}) collective-permute-start(bf16[4,256,256]{2,1,0:T(8,128)(2,1)S(1)} %get-tuple-element.45.refs_8_.refs_1_.refs_4_.refs_2_), channel_id=1, source_target_pairs={{0,1},{1,0},{2,3},{3,2},{4,6},{5,7},{6,4},{7,5},{8,9},{9,8},{10,11... | collective-permute-start | bytes 1572872 | tf_op jit(solution)/shard_map/integrals_mine/ppermute | solution.py:24
  6.5 5.7 %collective-permute-start.8 = (bf16[2,2,96,128]{3,2,1,0:T(8,128)(2,1)S(1)}, bf16[2,2,96,128]{3,2,1,0:T(8,128)(2,1)S(1)}, u32[]{:S(2)}, u32[]{:S(2)}) collective-permute-start(bf16[2,2,96,128]{3,2,1,0:T(8,128)(2,1)S(1)} %pad_maximum_fusion.2), channel_id=1, source_target_pairs={{0,8},{1,9},{2,10},{3,11},{4,20},{5,21},{6,22},{7,23},{8,0},{9,1},... | collective-permute-start | bytes 294920 | tf_op jit(solution)/shard_map/sent_near_by_core/ppermute | solution.py:24
  8.3 4.4 %collective-permute-start.3 = (bf16[2,96,128]{2,1,0:T(8,128)(2,1)S(1)}, bf16[2,96,128]{2,1,0:T(8,128)(2,1)S(1)}, u32[]{:S(2)}, u32[]{:S(2)}) collective-permute-start(bf16[2,96,128]{2,1,0:T(8,128)(2,1)S(1)} %get-tuple-element.36), channel_id=1, source_target_pairs={{0,4},{1,5},{2,6},{3,7},{4,0},{5,1},{6,2},{7,3},{8,12},{9,13},{10,... | collective-permute-start | bytes 147464 | tf_op jit(solution)/shard_map/sent_far_over_core/ppermute | solution.py:24
  8.5 7.0 %collective-permute-start.4 = (bf16[4,96,128]{2,1,0:T(8,128)(2,1)S(1)}, bf16[4,96,128]{2,1,0:T(8,128)(2,1)S(1)}, u32[]{:S(2)}, u32[]{:S(2)}) collective-permute-start(bf16[4,96,128]{2,1,0:T(8,128)(2,1)S(1)} %get-tuple-element.35.refs_0_), channel_id=1, source_target_pairs={{0,24},{1,25},{2,26},{3,27},{4,28},{5,29},{6,30},{7,31},{8,16},{9,... | collective-permute-start | bytes 294920 | tf_op jit(solution)/shard_map/sent_alone/ppermute | solution.py:24
  12.0 3.5 %collective-permute-start.5 = (bf16[4,96,128]{2,1,0:T(8,128)(2,1)S(1)}, bf16[4,96,128]{2,1,0:T(8,128)(2,1)S(1)}, u32[]{:S(2)}, u32[]{:S(2)}) collective-permute-start(bf16[4,96,128]{2,1,0:T(8,128)(2,1)S(1)} %get-tuple-element.48.refs_1_), channel_id=1, source_target_pairs={{0,4},{1,5},{2,6},{3,7},{4,0},{5,1},{6,2},{7,3},{8,12},{9,13},{10,... | collective-permute-start | bytes 294920 | tf_op jit(solution)/shard_map/kept_over_core/ppermute | solution.py:24
  12.2 10.6 %collective-permute-start.10 = (bf16[4,256,256]{2,1,0:T(8,128)(2,1)S(1)}, bf16[4,256,256]{2,1,0:T(8,128)(2,1)S(1)}, u32[]{:S(2)}, u32[]{:S(2)}) collective-permute-start(bf16[4,256,256]{2,1,0:T(8,128)(2,1)S(1)} %get-tuple-element.42.refs_8_.refs_6_.refs_4_.refs_1_), channel_id=1, source_target_pairs={{0,2},{1,3},{2,0},{3,1},{4,5},{5,4},{6,7},{7,6},{8,10},{9,11},{10,... | collective-permute-start | bytes 1572872 | tf_op jit(solution)/shard_map/integrals_other/ppermute | solution.py:24
  12.8 6.9 %collective-permute-start.6 = (bf16[2,2,96,128]{3,2,1,0:T(8,128)(2,1)S(1)}, bf16[2,2,96,128]{3,2,1,0:T(8,128)(2,1)S(1)}, u32[]{:S(2)}, u32[]{:S(2)}) collective-permute-start(bf16[2,2,96,128]{3,2,1,0:T(8,128)(2,1)S(1)} %pad_maximum_fusion.1), channel_id=1, source_target_pairs={{0,8},{1,9},{2,10},{3,11},{4,20},{5,21},{6,22},{7,23},{8,0},{9,1},... | collective-permute-start | bytes 294920 | tf_op jit(solution)/shard_map/sent_far_by_core/ppermute | solution.py:24
  15.5 4.6 %collective-permute-start.7 = (bf16[4,96,128]{2,1,0:T(8,128)(2,1)S(1)}, bf16[4,96,128]{2,1,0:T(8,128)(2,1)S(1)}, u32[]{:S(2)}, u32[]{:S(2)}) collective-permute-start(bf16[4,96,128]{2,1,0:T(8,128)(2,1)S(1)} %collective-permute-done.4.refs_3_), channel_id=1, source_target_pairs={{0,4},{1,5},{2,6},{3,7},{4,0},{5,1},{6,2},{7,3},{8,12},{9,13},{10,... | collective-permute-start | bytes 294920 | tf_op jit(solution)/shard_map/sent_alone_over_core/ppermute | solution.py:24
  15.6 9.3 %collective-permute-start.12 = (bf16[2,4,96,128]{3,2,1,0:T(8,128)(2,1)S(1)}, bf16[2,4,96,128]{3,2,1,0:T(8,128)(2,1)S(1)}, u32[]{:S(2)}, u32[]{:S(2)}) collective-permute-start(bf16[2,4,96,128]{3,2,1,0:T(8,128)(2,1)S(1)} %pad_maximum_fusion), channel_id=1, source_target_pairs={{0,24},{1,25},{2,26},{3,27},{4,20},{5,21},{6,22},{7,23},{8,16},{9,... | collective-permute-start | bytes 589832 | tf_op jit(solution)/shard_map/kept_by_core/ppermute | solution.py:24
  19.6 1.5 %collective-permute-start.9 = (bf16[2,2,96,128]{3,2,1,0:T(8,128)(2,1)S(1)}, bf16[2,2,96,128]{3,2,1,0:T(8,128)(2,1)S(1)}, u32[]{:S(2)}, u32[]{:S(2)}) collective-permute-start(bf16[2,2,96,128]{3,2,1,0:T(8,128)(2,1)S(1)} %collective-permute-done.8.refs_6_), channel_id=1, source_target_pairs={{0,4},{1,5},{2,6},{3,7},{4,0},{5,1},{6,2},{7,3},{8,12},{9,13},{10,... | collective-permute-start | bytes 294920 | tf_op jit(solution)/shard_map/sent_near_one_over_core/ppermute | solution.py:24
  20.2 1.4 %collective-permute-start.13 = (bf16[2,2,96,128]{3,2,1,0:T(8,128)(2,1)S(1)}, bf16[2,2,96,128]{3,2,1,0:T(8,128)(2,1)S(1)}, u32[]{:S(2)}, u32[]{:S(2)}) collective-permute-start(bf16[2,2,96,128]{3,2,1,0:T(8,128)(2,1)S(1)} %collective-permute-done.6.refs_4_), channel_id=1, source_target_pairs={{0,4},{1,5},{2,6},{3,7},{4,0},{5,1},{6,2},{7,3},{8,12},{9,13},{10,... | collective-permute-start | bytes 294920 | tf_op jit(solution)/shard_map/sent_far_one_over_core/ppermute | solution.py:24
  21.8 11.1 %collective-permute-start.17 = (f32[4,96,256]{2,1,0:T(8,128)S(1)}, f32[4,96,256]{2,1,0:T(8,128)S(1)}, u32[]{:S(2)}, u32[]{:S(2)}) collective-permute-start(f32[4,96,256]{2,1,0:T(8,128)S(1)} %shard_map.44), channel_id=1, source_target_pairs={{0,2},{1,3},{2,0},{3,1},{4,5},{5,4},{6,7},{7,6},{8,10},{9,11},{10,... | collective-permute-start | bytes 1179656 | tf_op jit(solution)/shard_map/sums_mine/ppermute | solution.py:24
  23.5 9.8 %collective-permute-start.18 = (f32[4,96,256]{2,1,0:T(8,128)S(1)}, f32[4,96,256]{2,1,0:T(8,128)S(1)}, u32[]{:S(2)}, u32[]{:S(2)}) collective-permute-start(f32[4,96,256]{2,1,0:T(8,128)S(1)} %shard_map.47), channel_id=1, source_target_pairs={{0,1},{1,0},{2,3},{3,2},{4,6},{5,7},{6,4},{7,5},{8,9},{9,8},{10,11... | collective-permute-start | bytes 1179656 | tf_op jit(solution)/shard_map/sums_other/ppermute | solution.py:24
  24.1 6.1 %collective-permute-start.11 = (bf16[4,96,128]{2,1,0:T(8,128)(2,1)S(1)}, bf16[4,96,128]{2,1,0:T(8,128)(2,1)S(1)}, u32[]{:S(2)}, u32[]{:S(2)}) collective-permute-start(bf16[4,96,128]{2,1,0:T(8,128)(2,1)S(1)} %get-tuple-element.48.refs_1_), channel_id=1, source_target_pairs={{0,8},{1,9},{2,10},{3,11},{4,12},{5,13},{6,14},{7,15},{8,0},{9,1},... | collective-permute-start | bytes 294920 | tf_op jit(solution)/shard_map/kept_alone/ppermute | solution.py:24
  30.2 1.4 %collective-permute-start.16 = (bf16[2,4,96,128]{3,2,1,0:T(8,128)(2,1)S(1)}, bf16[2,4,96,128]{3,2,1,0:T(8,128)(2,1)S(1)}, u32[]{:S(2)}, u32[]{:S(2)}) collective-permute-start(bf16[2,4,96,128]{3,2,1,0:T(8,128)(2,1)S(1)} %collective-permute-done.12.refs_0_), channel_id=1, source_target_pairs={{0,4},{1,5},{2,6},{3,7},{4,0},{5,1},{6,2},{7,3},{8,12},{9,13},{10,... | collective-permute-start | bytes 589832 | tf_op jit(solution)/shard_map/kept_one_over_core/ppermute | solution.py:24
  30.2 2.1 %collective-permute-start.15 = (bf16[4,96,128]{2,1,0:T(8,128)(2,1)S(1)}, bf16[4,96,128]{2,1,0:T(8,128)(2,1)S(1)}, u32[]{:S(2)}, u32[]{:S(2)}) collective-permute-start(bf16[4,96,128]{2,1,0:T(8,128)(2,1)S(1)} %collective-permute-done.11.refs_0_), channel_id=1, source_target_pairs={{0,4},{1,5},{2,6},{3,7},{4,0},{5,1},{6,2},{7,3},{8,12},{9,13},{10,... | collective-permute-start | bytes 294920 | tf_op jit(solution)/shard_map/kept_alone_over_core/ppermute | solution.py:24

commit v6 on v5

--- a/solution.py
+++ b/solution.py
@@ -12,7 +12,6 @@
 PARAMS = pltpu.CompilerParams(vmem_limit_bytes=16 << 20)
 CHIPS = 4
 COST_PACK, COST_JOIN, COST_FAR, COST_FAR_OTHER = 2 * 10**9, 4 * 10**9, 4 * 10**9, 2 * 10**9
-COST_SENT, COST_OTHER, COST_KEPT, COST_SUM, TIE_NEAR = 0, 0, 0, 0, 1
 
 
 def cost(flops):
@@ -24,16 +23,16 @@
         return lax.ppermute(array, ("loop", "rep"), pairs)
 
 
-def mark(flops, *arrays):
+def mark(flops, array):
     return pl.pallas_call(
         lambda *refs: None,
-        out_shape=[jax.ShapeDtypeStruct(array.shape, array.dtype) for array in arrays],
-        in_specs=[pl.BlockSpec(memory_space=VMEM)] * len(arrays),
-        out_specs=[pl.BlockSpec(memory_space=VMEM)] * len(arrays),
-        input_output_aliases={i: i for i in range(len(arrays))},
+        out_shape=jax.ShapeDtypeStruct(array.shape, array.dtype),
+        in_specs=[pl.BlockSpec(memory_space=VMEM)],
+        out_specs=pl.BlockSpec(memory_space=VMEM),
+        input_output_aliases={0: 0},
         cost_estimate=cost(flops),
         compiler_params=PARAMS,
-    )(*arrays)
+    )(array)
 
 
 def position():
@@ -177,8 +176,7 @@
         compiler_params=PARAMS,
     )(block_mask, integrals, to_mine)
     far = swap(near, fetch, "integrals_mine")
-    if TIE_NEAR == 1:
-        near_other, one_near = lax.optimization_barrier((near_other, one_near))
+    near_other, one_near = lax.optimization_barrier((near_other, one_near))
     far_other_integrals = swap(near_other, reduce, "integrals_other")
 
     message = jax.ShapeDtypeStruct((4, rows, lanes), bf16)
@@ -197,14 +195,14 @@
     def for_chip(own, sibling, hops, scope):
         return swap(jnp.stack([own, sibling]), by_core(hops), scope + "_by_core")
 
-    def product(parts, kinds, hops, flops, before=()):
+    def product(parts, kinds, hops, before=()):
         given = [(near, far), (near_other, far_other_integrals)]
         return pl.pallas_call(
             functools.partial(product_kernel, kinds, hops, bool(before), tuple(parts)),
             out_shape=[sums] * len(kinds),
             in_specs=[in_vmem] * (len(parts) + 2 * len(kinds) + len(before)),
             out_specs=[in_vmem] * len(kinds),
-            cost_estimate=cost(flops),
+            cost_estimate=cost(0),
             compiler_params=PARAMS,
         )(*parts.values(), *(array for kind in kinds for array in given[kind]), *before)
 
@@ -216,29 +214,24 @@
     parts["alone"], kept_sibling = lax.optimization_barrier((parts["alone"], kept_sibling))
     kept_parts = dict(own=kept, sibling=kept_sibling)
     kept_parts["one"] = for_chip(kept, kept_sibling, KEPT, "kept")
-    if COST_FAR:
-        (far,) = mark(COST_FAR, far)
-    if COST_FAR_OTHER:
-        (far_other_integrals,) = mark(COST_FAR_OTHER, far_other_integrals)
+    far = mark(COST_FAR, far)
+    far_other_integrals = mark(COST_FAR_OTHER, far_other_integrals)
     parts["alone_sibling"] = over_cores(parts["alone"], "sent_alone")
     parts["one_far"], parts["alone_sibling"] = lax.optimization_barrier((parts["one_far"], parts["alone_sibling"]))
     parts["one_near"], parts["two_near"] = one_near, over_cores(one_near, "sent_near_one")
     last = dict(two_far=over_cores(parts["one_far"], "sent_far_one"))
-    sent_parts = parts
-    (sent,) = product(last, (0,), SENT, COST_SENT, product(sent_parts, (0,), SENT, COST_SENT))
-    (first_other,) = product(sent_parts, (1,), SENT, COST_OTHER)
+    (sent,) = product(last, (0,), SENT, product(parts, (0,), SENT))
+    (first_other,) = product(parts, (1,), SENT)
     kept, first_other = lax.optimization_barrier((kept, first_other))
     kept_parts["alone"] = swap(kept, alone(KEPT), "kept_alone")
-    (sent_other,) = product(last, (1,), SENT, COST_OTHER, (first_other,))
+    (sent_other,) = product(last, (1,), SENT, (first_other,))
     sum_mine = swap(sent, reduce, "sums_mine")
     sum_other = swap(sent_other, fetch, "sums_other")
-    if COST_SUM:
-        (sum_mine,) = mark(COST_SUM, sum_mine)
     kept_parts, sent = lax.optimization_barrier((kept_parts, sent))
     kept_parts["two"] = over_cores(kept_parts["one"], "kept_one")
     kept_parts["alone_sibling"] = over_cores(kept_parts["alone"], "kept_alone")
     last = {name: kept_parts.pop(name) for name in ("alone", "alone_sibling")}
-    kept, kept_other = product(last, (0, 1), KEPT, COST_KEPT, product(kept_parts, (0, 1), KEPT, COST_KEPT))
+    kept, kept_other = product(last, (0, 1), KEPT, product(kept_parts, (0, 1), KEPT))
     return pl.pallas_call(
         total_kernel,
         out_shape=jax.ShapeDtypeStruct((irreps, rows, columns), bf16),

time: 34.2 us -> 34.2 us (level)
  no operation moved by 1% of the time
where the time goes in v6:
time: 34.2 us; the launch traced here: 34.1 us
  starting transfers between devices  19.8 us (58%)
  waiting for transfers between devices  9.63 us (28%)
  Pallas kernels  3.56 us (10%)
  local copies, waits for them, and re-layouts  0.94 us (3%)
    ppermute x19, starting transfers between devices, swap(): return lax.ppermute(array, ('loop', 'rep'), pairs)  19.8 us
    ppermute x19, waiting for transfers between devices, swap(): return lax.ppermute(array, ('loop', 'rep'), pairs)  9.63 us
    pallas_call x6, Pallas kernels, product(): pl.pallas_call(functools.partial(product_kernel, kinds, hops, bool(before...  2.41 us
    unnamed x6, local copies, waits for them, and re-layouts  0.94 us
    pallas_call x1, Pallas kernels, square(): pl.pallas_call(total_kernel, out_shape=jax.ShapeDtypeStruct((irreps, rows...  0.82 us
  transfers between devices with their start and end apart: 19, of which 7 were waited for; matrix products, arithmetic and copies ran while one was open for 0% of the time, Pallas kernels for 8%

profile of v6, /device:TPU:0, one launch (start us, length us, event | category | flops | bytes accessed | tf_op | source)
XLA Modules:
  0.0 34.1 jit_solution(6044916804468158704)
XLA Ops:
  0.0 0.9 %copy-done.2 = bf16[8,384,32]{1,2,0:T(8,128)(2,1)S(1)} copy-done((bf16[8,384,32]{1,2,0:T(8,128)(2,1)S(1)}, bf16[8,384,32]{1,2,0:T(8,128)(2,1)}, u32[]{:S(2)}) %copy-start.2) | copy-done | bytes 196632
  0.9 0.1 shard_map.37
  1.1 0.0 copy-start.1
  1.1 0.5 %collective-permute-start.2 = (bf16[2,96,128]{2,1,0:T(8,128)(2,1)S(1)}, bf16[2,96,128]{2,1,0:T(8,128)(2,1)S(1)}, u32[]{:S(2)}, u32[]{:S(2)}) collective-permute-start(bf16[2,96,128]{2,1,0:T(8,128)(2,1)S(1)} %get-tuple-element.30.sent_own_ref), channel_id=1, source_target_pairs={{0,4},{1,5},{2,6},{3,7},{4,0},{5,1},{6,2},{7,3},{8,12},{9,13},{10,... | collective-permute-start | bytes 147464 | tf_op jit(solution)/shard_map/sent_near_over_core/ppermute | solution.py:23
  1.6 2.6 %collective-permute-start.1 = (bf16[2,96,128]{2,1,0:T(8,128)(2,1)S(1)}, bf16[2,96,128]{2,1,0:T(8,128)(2,1)S(1)}, u32[]{:S(2)}, u32[]{:S(2)}) collective-permute-start(bf16[2,96,128]{2,1,0:T(8,128)(2,1)S(1)} %get-tuple-element.33), channel_id=1, source_target_pairs={{0,2},{1,3},{2,0},{3,1},{4,5},{5,4},{6,7},{7,6},{8,10},{9,11},{10,... | collective-permute-start | bytes 147464 | tf_op jit(solution)/shard_map/lam_other/ppermute | solution.py:23
  4.2 1.5 %collective-permute-start = (bf16[2,96,128]{2,1,0:T(8,128)(2,1)S(1)}, bf16[2,96,128]{2,1,0:T(8,128)(2,1)S(1)}, u32[]{:S(2)}, u32[]{:S(2)}) collective-permute-start(bf16[2,96,128]{2,1,0:T(8,128)(2,1)S(1)} %get-tuple-element.32._), channel_id=1, source_target_pairs={{0,1},{1,0},{2,3},{3,2},{4,6},{5,7},{6,4},{7,5},{8,9},{9,8},{10,11... | collective-permute-start | bytes 147464 | tf_op jit(solution)/shard_map/lam_mine/ppermute | solution.py:23
  5.7 0.2 shard_map.39
  5.9 0.6 %collective-permute-start.14 = (bf16[4,256,256]{2,1,0:T(8,128)(2,1)S(1)}, bf16[4,256,256]{2,1,0:T(8,128)(2,1)S(1)}, u32[]{:S(2)}, u32[]{:S(2)}) collective-permute-start(bf16[4,256,256]{2,1,0:T(8,128)(2,1)S(1)} %get-tuple-element.45.refs_8_.refs_1_.refs_4_.refs_2_), channel_id=1, source_target_pairs={{0,1},{1,0},{2,3},{3,2},{4,6},{5,7},{6,4},{7,5},{8,9},{9,8},{10,11... | collective-permute-start | bytes 1572872 | tf_op jit(solution)/shard_map/integrals_mine/ppermute | solution.py:23
  6.5 0.0 collective-permute-done.2.refs_1_
  6.5 1.6 %collective-permute-start.8 = (bf16[2,2,96,128]{3,2,1,0:T(8,128)(2,1)S(1)}, bf16[2,2,96,128]{3,2,1,0:T(8,128)(2,1)S(1)}, u32[]{:S(2)}, u32[]{:S(2)}) collective-permute-start(bf16[2,2,96,128]{3,2,1,0:T(8,128)(2,1)S(1)} %pad_maximum_fusion.2), channel_id=1, source_target_pairs={{0,8},{1,9},{2,10},{3,11},{4,20},{5,21},{6,22},{7,23},{8,0},{9,1},... | collective-permute-start | bytes 294920 | tf_op jit(solution)/shard_map/sent_near_by_core/ppermute | solution.py:23
  8.1 0.0 collective-permute-done.1.far_other_ref
  8.1 0.1 collective-permute-done.far_mine_ref
  8.3 0.2 collective-permute-start.3
  8.5 3.5 %collective-permute-start.4 = (bf16[4,96,128]{2,1,0:T(8,128)(2,1)S(1)}, bf16[4,96,128]{2,1,0:T(8,128)(2,1)S(1)}, u32[]{:S(2)}, u32[]{:S(2)}) collective-permute-start(bf16[4,96,128]{2,1,0:T(8,128)(2,1)S(1)} %get-tuple-element.35.refs_0_), channel_id=1, source_target_pairs={{0,24},{1,25},{2,26},{3,27},{4,28},{5,29},{6,30},{7,31},{8,16},{9,... | collective-permute-start | bytes 294920 | tf_op jit(solution)/shard_map/sent_alone/ppermute | solution.py:23
  12.0 0.2 collective-permute-start.5
  12.2 0.0 collective-permute-done.8.refs_6_
  12.2 0.5 %collective-permute-start.10 = (bf16[4,256,256]{2,1,0:T(8,128)(2,1)S(1)}, bf16[4,256,256]{2,1,0:T(8,128)(2,1)S(1)}, u32[]{:S(2)}, u32[]{:S(2)}) collective-permute-start(bf16[4,256,256]{2,1,0:T(8,128)(2,1)S(1)} %get-tuple-element.42.refs_8_.refs_6_.refs_4_.refs_1_), channel_id=1, source_target_pairs={{0,2},{1,3},{2,0},{3,1},{4,5},{5,4},{6,7},{7,6},{8,10},{9,11},{10,... | collective-permute-start | bytes 1572872 | tf_op jit(solution)/shard_map/integrals_other/ppermute | solution.py:23
  12.7 0.0 collective-permute-done.3.refs_2_
  12.8 1.1 %collective-permute-start.6 = (bf16[2,2,96,128]{3,2,1,0:T(8,128)(2,1)S(1)}, bf16[2,2,96,128]{3,2,1,0:T(8,128)(2,1)S(1)}, u32[]{:S(2)}, u32[]{:S(2)}) collective-permute-start(bf16[2,2,96,128]{3,2,1,0:T(8,128)(2,1)S(1)} %pad_maximum_fusion.1), channel_id=1, source_target_pairs={{0,8},{1,9},{2,10},{3,11},{4,20},{5,21},{6,22},{7,23},{8,0},{9,1},... | collective-permute-start | bytes 294920 | tf_op jit(solution)/shard_map/sent_far_by_core/ppermute | solution.py:23
  13.8 1.7 %collective-permute-done.4.refs_3_ = bf16[4,96,128]{2,1,0:T(8,128)(2,1)S(1)} collective-permute-done((bf16[4,96,128]{2,1,0:T(8,128)(2,1)S(1)}, bf16[4,96,128]{2,1,0:T(8,128)(2,1)S(1)}, u32[]{:S(2)}, u32[]{:S(2)}) %collective-permute-start.4) | collective-permute-done | bytes 98336 | tf_op jit(solution)/shard_map/sent_alone/ppermute | solution.py:23
  15.5 0.0 collective-permute-done.5.refs_2_
  15.5 0.0 collective-permute-start.7
  15.6 4.1 %collective-permute-start.12 = (bf16[2,4,96,128]{3,2,1,0:T(8,128)(2,1)S(1)}, bf16[2,4,96,128]{3,2,1,0:T(8,128)(2,1)S(1)}, u32[]{:S(2)}, u32[]{:S(2)}) collective-permute-start(bf16[2,4,96,128]{3,2,1,0:T(8,128)(2,1)S(1)} %pad_maximum_fusion), channel_id=1, source_target_pairs={{0,24},{1,25},{2,26},{3,27},{4,20},{5,21},{6,22},{7,23},{8,16},{9,... | collective-permute-start | bytes 589832 | tf_op jit(solution)/shard_map/kept_by_core/ppermute | solution.py:23
  19.6 0.0 collective-permute-done.6.refs_4_
  19.6 0.5 %collective-permute-start.9 = (bf16[2,2,96,128]{3,2,1,0:T(8,128)(2,1)S(1)}, bf16[2,2,96,128]{3,2,1,0:T(8,128)(2,1)S(1)}, u32[]{:S(2)}, u32[]{:S(2)}) collective-permute-start(bf16[2,2,96,128]{3,2,1,0:T(8,128)(2,1)S(1)} %collective-permute-done.8.refs_6_), channel_id=1, source_target_pairs={{0,4},{1,5},{2,6},{3,7},{4,0},{5,1},{6,2},{7,3},{8,12},{9,13},{10,... | collective-permute-start | bytes 294920 | tf_op jit(solution)/shard_map/sent_near_one_over_core/ppermute | solution.py:23
  20.2 0.0 collective-permute-done.7.refs_5_
  20.2 0.1 collective-permute-start.13
  20.3 0.9 %collective-permute-done.9.refs_7_ = bf16[2,2,96,128]{3,2,1,0:T(8,128)(2,1)S(1)} collective-permute-done((bf16[2,2,96,128]{3,2,1,0:T(8,128)(2,1)S(1)}, bf16[2,2,96,128]{3,2,1,0:T(8,128)(2,1)S(1)}, u32[]{:S(2)}, u32[]{:S(2)}) %collective-permute-start.9) | collective-permute-done | bytes 98336 | tf_op jit(solution)/shard_map/sent_near_one_over_core/ppermute | solution.py:23
  21.1 0.4 %shard_map.43.refs_3_ = f32[4,96,256]{2,1,0:T(8,128)S(1)} custom-call(bf16[4,96,128]{2,1,0:T(8,128)(2,1)S(1)} %get-tuple-element.35.refs_0_, bf16[2,96,128]{2,1,0:T(8,128)(2,1)S(1)} %collective-permute-done.2.refs_1_, bf16[2,96,128]{2,1,0:T(8,128)(2,1)S(1)} %collective-permute-done.3.refs_2_, bf16[4,96,128]{2,1,0:T(8,128)(2,1)S(1)} %collective-permute-done.4.refs_3_, ...), custom_call_target="tpu_custom_call" | custom-call | tf_op jit(solution)/shard_map/pallas_call | solution.py:200
  21.6 0.0 collective-permute-done.13.refs_0_
  21.6 0.3 shard_map.44
  21.8 0.9 %collective-permute-start.17 = (f32[4,96,256]{2,1,0:T(8,128)S(1)}, f32[4,96,256]{2,1,0:T(8,128)S(1)}, u32[]{:S(2)}, u32[]{:S(2)}) collective-permute-start(f32[4,96,256]{2,1,0:T(8,128)S(1)} %shard_map.44), channel_id=1, source_target_pairs={{0,2},{1,3},{2,0},{3,1},{4,5},{5,4},{6,7},{7,6},{8,10},{9,11},{10,... | collective-permute-start | bytes 1179656 | tf_op jit(solution)/shard_map/sums_mine/ppermute | solution.py:23
  22.8 0.0 collective-permute-done.10.refs_0_
  22.8 0.5 %shard_map.41.refs_3_ = f32[4,96,256]{2,1,0:T(8,128)S(1)} custom-call(bf16[4,96,128]{2,1,0:T(8,128)(2,1)S(1)} %get-tuple-element.35.refs_0_, bf16[2,96,128]{2,1,0:T(8,128)(2,1)S(1)} %collective-permute-done.2.refs_1_, bf16[2,96,128]{2,1,0:T(8,128)(2,1)S(1)} %collective-permute-done.3.refs_2_, bf16[4,96,128]{2,1,0:T(8,128)(2,1)S(1)} %collective-permute-done.4.refs_3_, ...), custom_call_target="tpu_custom_call" | custom-call | tf_op jit(solution)/shard_map/pallas_call | solution.py:200
  23.2 0.3 shard_map.47
  23.5 0.6 %collective-permute-start.18 = (f32[4,96,256]{2,1,0:T(8,128)S(1)}, f32[4,96,256]{2,1,0:T(8,128)S(1)}, u32[]{:S(2)}, u32[]{:S(2)}) collective-permute-start(f32[4,96,256]{2,1,0:T(8,128)S(1)} %shard_map.47), channel_id=1, source_target_pairs={{0,1},{1,0},{2,3},{3,2},{4,6},{5,7},{6,4},{7,5},{8,9},{9,8},{10,11... | collective-permute-start | bytes 1179656 | tf_op jit(solution)/shard_map/sums_other/ppermute | solution.py:23
  24.1 0.8 %collective-permute-start.11 = (bf16[4,96,128]{2,1,0:T(8,128)(2,1)S(1)}, bf16[4,96,128]{2,1,0:T(8,128)(2,1)S(1)}, u32[]{:S(2)}, u32[]{:S(2)}) collective-permute-start(bf16[4,96,128]{2,1,0:T(8,128)(2,1)S(1)} %get-tuple-element.48.refs_1_), channel_id=1, source_target_pairs={{0,8},{1,9},{2,10},{3,11},{4,12},{5,13},{6,14},{7,15},{8,0},{9,1},... | collective-permute-start | bytes 294920 | tf_op jit(solution)/shard_map/kept_alone/ppermute | solution.py:23
  24.9 0.0 collective-permute-done.12.refs_0_
  24.9 5.3 %collective-permute-done.11.refs_0_ = bf16[4,96,128]{2,1,0:T(8,128)(2,1)S(1)} collective-permute-done((bf16[4,96,128]{2,1,0:T(8,128)(2,1)S(1)}, bf16[4,96,128]{2,1,0:T(8,128)(2,1)S(1)}, u32[]{:S(2)}, u32[]{:S(2)}) %collective-permute-start.11) | collective-permute-done | bytes 98336 | tf_op jit(solution)/shard_map/kept_alone/ppermute | solution.py:23
  30.2 0.0 collective-permute-start.16
  30.2 0.5 %collective-permute-start.15 = (bf16[4,96,128]{2,1,0:T(8,128)(2,1)S(1)}, bf16[4,96,128]{2,1,0:T(8,128)(2,1)S(1)}, u32[]{:S(2)}, u32[]{:S(2)}) collective-permute-start(bf16[4,96,128]{2,1,0:T(8,128)(2,1)S(1)} %collective-permute-done.11.refs_0_), channel_id=1, source_target_pairs={{0,4},{1,5},{2,6},{3,7},{4,0},{5,1},{6,2},{7,3},{8,12},{9,13},{10,... | collective-permute-start | bytes 294920 | tf_op jit(solution)/shard_map/kept_alone_over_core/ppermute | solution.py:23
  30.7 0.9 %collective-permute-done.16.refs_3_ = bf16[2,4,96,128]{3,2,1,0:T(8,128)(2,1)S(1)} collective-permute-done((bf16[2,4,96,128]{3,2,1,0:T(8,128)(2,1)S(1)}, bf16[2,4,96,128]{3,2,1,0:T(8,128)(2,1)S(1)}, u32[]{:S(2)}, u32[]{:S(2)}) %collective-permute-start.16) | collective-permute-done | bytes 196640 | tf_op jit(solution)/shard_map/kept_one_over_core/ppermute | solution.py:23
  31.6 0.6 %shard_map.45 = (f32[4,96,256]{2,1,0:T(8,128)S(1)}, f32[4,96,256]{2,1,0:T(8,128)S(1)}) custom-call(bf16[2,4,96,128]{3,2,1,0:T(8,128)(2,1)S(1)} %collective-permute-done.12.refs_0_, bf16[4,96,128]{2,1,0:T(8,128)(2,1)S(1)} %get-tuple-element.48.refs_1_, bf16[4,96,128]{2,1,0:T(8,128)(2,1)S(1)} %collective-permute-done.5.refs_2_, ...), custom_call_target="tpu_custom_call" | custom-call | tf_op jit(solution)/shard_map/pallas_call | solution.py:200
  32.3 0.0 collective-permute-done.15.refs_1_
  32.3 0.4 %shard_map.46 = (f32[4,96,256]{2,1,0:T(8,128)S(1)}, f32[4,96,256]{2,1,0:T(8,128)S(1)}) custom-call(bf16[4,96,128]{2,1,0:T(8,128)(2,1)S(1)} %collective-permute-done.11.refs_0_, bf16[4,96,128]{2,1,0:T(8,128)(2,1)S(1)} %collective-permute-done.15.refs_1_, bf16[4,256,256]{2,1,0:T(8,128)(2,1)S(1)} %get-tuple-element.45.refs_8_.refs_1_.refs_4_.refs_2_, ...), custom_call_target="tpu_custom_call" | custom-call | tf_op jit(solution)/shard_map/pallas_call | solution.py:200
  32.6 0.3 collective-permute-done.17.arrived_ref
  32.9 0.4 %collective-permute-done.18.arrived_other_ref = f32[4,96,256]{2,1,0:T(8,128)S(1)} collective-permute-done((f32[4,96,256]{2,1,0:T(8,128)S(1)}, f32[4,96,256]{2,1,0:T(8,128)S(1)}, u32[]{:S(2)}, u32[]{:S(2)}) %collective-permute-start.18) | collective-permute-done | bytes 393248 | tf_op jit(solution)/shard_map/sums_other/ppermute | solution.py:23
  33.3 0.8 %shard_map.48 = bf16[8,96,256]{2,1,0:T(8,128)(2,1)} custom-call(f32[4,96,256]{2,1,0:T(8,128)S(1)} %get-tuple-element.52.kept_ref, f32[4,96,256]{2,1,0:T(8,128)S(1)} %get-tuple-element.53.kept_other_ref, f32[4,96,256]{2,1,0:T(8,128)S(1)} %collective-permute-done.17.arrived_ref, f32[4,96,256]{2,1,0:T(8,128)S(1)} %collective-permute-done.18.arrived_other_ref), custom_call_target="tpu_custom_call" | custom-call | tf_op jit(solution)/shard_map/pallas_call | solution.py:235
  (11 shorter events, 0.1 us)
Async XLA Ops:
  0.0 0.9 %copy-start.2 = (bf16[8,384,32]{1,2,0:T(8,128)(2,1)S(1)}, bf16[8,384,32]{1,2,0:T(8,128)(2,1)}, u32[]{:S(2)}) copy-start(bf16[8,384,32]{1,2,0:T(8,128)(2,1)} %param.3) | copy-start | bytes 589828
  0.9 4.7 %copy-start = (bf16[8,256,256]{2,1,0:T(8,128)(2,1)S(1)}, bf16[8,256,256]{2,1,0:T(8,128)(2,1)}, u32[]{:S(2)}) copy-start(bf16[8,256,256]{2,1,0:T(8,128)(2,1)} %integrals_ref.1) | copy-start | bytes 3145732
  1.1 4.6 %copy-start.1 = (s32[8,8]{1,0:T(8,128)S(1)}, s32[8,8]{1,0:T(8,128)}, u32[]{:S(2)}) copy-start(s32[8,8]{1,0:T(8,128)} %mask_ref.1) | copy-start | bytes 772
  1.1 5.4 %collective-permute-start.2 = (bf16[2,96,128]{2,1,0:T(8,128)(2,1)S(1)}, bf16[2,96,128]{2,1,0:T(8,128)(2,1)S(1)}, u32[]{:S(2)}, u32[]{:S(2)}) collective-permute-start(bf16[2,96,128]{2,1,0:T(8,128)(2,1)S(1)} %get-tuple-element.30.sent_own_ref), channel_id=1, source_target_pairs={{0,4},{1,5},{2,6},{3,7},{4,0},{5,1},{6,2},{7,3},{8,12},{9,13},{10,... | collective-permute-start | bytes 147464 | tf_op jit(solution)/shard_map/sent_near_over_core/ppermute | solution.py:23
  1.6 6.6 %collective-permute-start.1 = (bf16[2,96,128]{2,1,0:T(8,128)(2,1)S(1)}, bf16[2,96,128]{2,1,0:T(8,128)(2,1)S(1)}, u32[]{:S(2)}, u32[]{:S(2)}) collective-permute-start(bf16[2,96,128]{2,1,0:T(8,128)(2,1)S(1)} %get-tuple-element.33), channel_id=1, source_target_pairs={{0,2},{1,3},{2,0},{3,1},{4,5},{5,4},{6,7},{7,6},{8,10},{9,11},{10,... | collective-permute-start | bytes 147464 | tf_op jit(solution)/shard_map/lam_other/ppermute | solution.py:23
  4.2 4.1 %collective-permute-start = (bf16[2,96,128]{2,1,0:T(8,128)(2,1)S(1)}, bf16[2,96,128]{2,1,0:T(8,128)(2,1)S(1)}, u32[]{:S(2)}, u32[]{:S(2)}) collective-permute-start(bf16[2,96,128]{2,1,0:T(8,128)(2,1)S(1)} %get-tuple-element.32._), channel_id=1, source_target_pairs={{0,1},{1,0},{2,3},{3,2},{4,6},{5,7},{6,4},{7,5},{8,9},{9,8},{10,11... | collective-permute-start | bytes 147464 | tf_op jit(solution)/shard_map/lam_mine/ppermute | solution.py:23
  5.9 14.4 %collective-permute-start.14 = (bf16[4,256,256]{2,1,0:T(8,128)(2,1)S(1)}, bf16[4,256,256]{2,1,0:T(8,128)(2,1)S(1)}, u32[]{:S(2)}, u32[]{:S(2)}) collective-permute-start(bf16[4,256,256]{2,1,0:T(8,128)(2,1)S(1)} %get-tuple-element.45.refs_8_.refs_1_.refs_4_.refs_2_), channel_id=1, source_target_pairs={{0,1},{1,0},{2,3},{3,2},{4,6},{5,7},{6,4},{7,5},{8,9},{9,8},{10,11... | collective-permute-start | bytes 1572872 | tf_op jit(solution)/shard_map/integrals_mine/ppermute | solution.py:23
  6.5 5.7 %collective-permute-start.8 = (bf16[2,2,96,128]{3,2,1,0:T(8,128)(2,1)S(1)}, bf16[2,2,96,128]{3,2,1,0:T(8,128)(2,1)S(1)}, u32[]{:S(2)}, u32[]{:S(2)}) collective-permute-start(bf16[2,2,96,128]{3,2,1,0:T(8,128)(2,1)S(1)} %pad_maximum_fusion.2), channel_id=1, source_target_pairs={{0,8},{1,9},{2,10},{3,11},{4,20},{5,21},{6,22},{7,23},{8,0},{9,1},... | collective-permute-start | bytes 294920 | tf_op jit(solution)/shard_map/sent_near_by_core/ppermute | solution.py:23
  8.3 4.4 %collective-permute-start.3 = (bf16[2,96,128]{2,1,0:T(8,128)(2,1)S(1)}, bf16[2,96,128]{2,1,0:T(8,128)(2,1)S(1)}, u32[]{:S(2)}, u32[]{:S(2)}) collective-permute-start(bf16[2,96,128]{2,1,0:T(8,128)(2,1)S(1)} %get-tuple-element.36), channel_id=1, source_target_pairs={{0,4},{1,5},{2,6},{3,7},{4,0},{5,1},{6,2},{7,3},{8,12},{9,13},{10,... | collective-permute-start | bytes 147464 | tf_op jit(solution)/shard_map/sent_far_over_core/ppermute | solution.py:23
  8.5 7.0 %collective-permute-start.4 = (bf16[4,96,128]{2,1,0:T(8,128)(2,1)S(1)}, bf16[4,96,128]{2,1,0:T(8,128)(2,1)S(1)}, u32[]{:S(2)}, u32[]{:S(2)}) collective-permute-start(bf16[4,96,128]{2,1,0:T(8,128)(2,1)S(1)} %get-tuple-element.35.refs_0_), channel_id=1, source_target_pairs={{0,24},{1,25},{2,26},{3,27},{4,28},{5,29},{6,30},{7,31},{8,16},{9,... | collective-permute-start | bytes 294920 | tf_op jit(solution)/shard_map/sent_alone/ppermute | solution.py:23
  12.0 3.5 %collective-permute-start.5 = (bf16[4,96,128]{2,1,0:T(8,128)(2,1)S(1)}, bf16[4,96,128]{2,1,0:T(8,128)(2,1)S(1)}, u32[]{:S(2)}, u32[]{:S(2)}) collective-permute-start(bf16[4,96,128]{2,1,0:T(8,128)(2,1)S(1)} %get-tuple-element.48.refs_1_), channel_id=1, source_target_pairs={{0,4},{1,5},{2,6},{3,7},{4,0},{5,1},{6,2},{7,3},{8,12},{9,13},{10,... | collective-permute-start | bytes 294920 | tf_op jit(solution)/shard_map/kept_over_core/ppermute | solution.py:23
  12.2 10.6 %collective-permute-start.10 = (bf16[4,256,256]{2,1,0:T(8,128)(2,1)S(1)}, bf16[4,256,256]{2,1,0:T(8,128)(2,1)S(1)}, u32[]{:S(2)}, u32[]{:S(2)}) collective-permute-start(bf16[4,256,256]{2,1,0:T(8,128)(2,1)S(1)} %get-tuple-element.42.refs_8_.refs_6_.refs_4_.refs_1_), channel_id=1, source_target_pairs={{0,2},{1,3},{2,0},{3,1},{4,5},{5,4},{6,7},{7,6},{8,10},{9,11},{10,... | collective-permute-start | bytes 1572872 | tf_op jit(solution)/shard_map/integrals_other/ppermute | solution.py:23
  12.8 6.9 %collective-permute-start.6 = (bf16[2,2,96,128]{3,2,1,0:T(8,128)(2,1)S(1)}, bf16[2,2,96,128]{3,2,1,0:T(8,128)(2,1)S(1)}, u32[]{:S(2)}, u32[]{:S(2)}) collective-permute-start(bf16[2,2,96,128]{3,2,1,0:T(8,128)(2,1)S(1)} %pad_maximum_fusion.1), channel_id=1, source_target_pairs={{0,8},{1,9},{2,10},{3,11},{4,20},{5,21},{6,22},{7,23},{8,0},{9,1},... | collective-permute-start | bytes 294920 | tf_op jit(solution)/shard_map/sent_far_by_core/ppermute | solution.py:23
  15.5 4.6 %collective-permute-start.7 = (bf16[4,96,128]{2,1,0:T(8,128)(2,1)S(1)}, bf16[4,96,128]{2,1,0:T(8,128)(2,1)S(1)}, u32[]{:S(2)}, u32[]{:S(2)}) collective-permute-start(bf16[4,96,128]{2,1,0:T(8,128)(2,1)S(1)} %collective-permute-done.4.refs_3_), channel_id=1, source_target_pairs={{0,4},{1,5},{2,6},{3,7},{4,0},{5,1},{6,2},{7,3},{8,12},{9,13},{10,... | collective-permute-start | bytes 294920 | tf_op jit(solution)/shard_map/sent_alone_over_core/ppermute | solution.py:23
  15.6 9.3 %collective-permute-start.12 = (bf16[2,4,96,128]{3,2,1,0:T(8,128)(2,1)S(1)}, bf16[2,4,96,128]{3,2,1,0:T(8,128)(2,1)S(1)}, u32[]{:S(2)}, u32[]{:S(2)}) collective-permute-start(bf16[2,4,96,128]{3,2,1,0:T(8,128)(2,1)S(1)} %pad_maximum_fusion), channel_id=1, source_target_pairs={{0,24},{1,25},{2,26},{3,27},{4,20},{5,21},{6,22},{7,23},{8,16},{9,... | collective-permute-start | bytes 589832 | tf_op jit(solution)/shard_map/kept_by_core/ppermute | solution.py:23
  19.6 1.5 %collective-permute-start.9 = (bf16[2,2,96,128]{3,2,1,0:T(8,128)(2,1)S(1)}, bf16[2,2,96,128]{3,2,1,0:T(8,128)(2,1)S(1)}, u32[]{:S(2)}, u32[]{:S(2)}) collective-permute-start(bf16[2,2,96,128]{3,2,1,0:T(8,128)(2,1)S(1)} %collective-permute-done.8.refs_6_), channel_id=1, source_target_pairs={{0,4},{1,5},{2,6},{3,7},{4,0},{5,1},{6,2},{7,3},{8,12},{9,13},{10,... | collective-permute-start | bytes 294920 | tf_op jit(solution)/shard_map/sent_near_one_over_core/ppermute | solution.py:23
  20.2 1.4 %collective-permute-start.13 = (bf16[2,2,96,128]{3,2,1,0:T(8,128)(2,1)S(1)}, bf16[2,2,96,128]{3,2,1,0:T(8,128)(2,1)S(1)}, u32[]{:S(2)}, u32[]{:S(2)}) collective-permute-start(bf16[2,2,96,128]{3,2,1,0:T(8,128)(2,1)S(1)} %collective-permute-done.6.refs_4_), channel_id=1, source_target_pairs={{0,4},{1,5},{2,6},{3,7},{4,0},{5,1},{6,2},{7,3},{8,12},{9,13},{10,... | collective-permute-start | bytes 294920 | tf_op jit(solution)/shard_map/sent_far_one_over_core/ppermute | solution.py:23
  21.8 11.1 %collective-permute-start.17 = (f32[4,96,256]{2,1,0:T(8,128)S(1)}, f32[4,96,256]{2,1,0:T(8,128)S(1)}, u32[]{:S(2)}, u32[]{:S(2)}) collective-permute-start(f32[4,96,256]{2,1,0:T(8,128)S(1)} %shard_map.44), channel_id=1, source_target_pairs={{0,2},{1,3},{2,0},{3,1},{4,5},{5,4},{6,7},{7,6},{8,10},{9,11},{10,... | collective-permute-start | bytes 1179656 | tf_op jit(solution)/shard_map/sums_mine/ppermute | solution.py:23
  23.5 9.8 %collective-permute-start.18 = (f32[4,96,256]{2,1,0:T(8,128)S(1)}, f32[4,96,256]{2,1,0:T(8,128)S(1)}, u32[]{:S(2)}, u32[]{:S(2)}) collective-permute-start(f32[4,96,256]{2,1,0:T(8,128)S(1)} %shard_map.47), channel_id=1, source_target_pairs={{0,1},{1,0},{2,3},{3,2},{4,6},{5,7},{6,4},{7,5},{8,9},{9,8},{10,11... | collective-permute-start | bytes 1179656 | tf_op jit(solution)/shard_map/sums_other/ppermute | solution.py:23
  24.1 6.1 %collective-permute-start.11 = (bf16[4,96,128]{2,1,0:T(8,128)(2,1)S(1)}, bf16[4,96,128]{2,1,0:T(8,128)(2,1)S(1)}, u32[]{:S(2)}, u32[]{:S(2)}) collective-permute-start(bf16[4,96,128]{2,1,0:T(8,128)(2,1)S(1)} %get-tuple-element.48.refs_1_), channel_id=1, source_target_pairs={{0,8},{1,9},{2,10},{3,11},{4,12},{5,13},{6,14},{7,15},{8,0},{9,1},... | collective-permute-start | bytes 294920 | tf_op jit(solution)/shard_map/kept_alone/ppermute | solution.py:23
  30.2 1.4 %collective-permute-start.16 = (bf16[2,4,96,128]{3,2,1,0:T(8,128)(2,1)S(1)}, bf16[2,4,96,128]{3,2,1,0:T(8,128)(2,1)S(1)}, u32[]{:S(2)}, u32[]{:S(2)}) collective-permute-start(bf16[2,4,96,128]{3,2,1,0:T(8,128)(2,1)S(1)} %collective-permute-done.12.refs_0_), channel_id=1, source_target_pairs={{0,4},{1,5},{2,6},{3,7},{4,0},{5,1},{6,2},{7,3},{8,12},{9,13},{10,... | collective-permute-start | bytes 589832 | tf_op jit(solution)/shard_map/kept_one_over_core/ppermute | solution.py:23
  30.2 2.1 %collective-permute-start.15 = (bf16[4,96,128]{2,1,0:T(8,128)(2,1)S(1)}, bf16[4,96,128]{2,1,0:T(8,128)(2,1)S(1)}, u32[]{:S(2)}, u32[]{:S(2)}) collective-permute-start(bf16[4,96,128]{2,1,0:T(8,128)(2,1)S(1)} %collective-permute-done.11.refs_0_), channel_id=1, source_target_pairs={{0,4},{1,5},{2,6},{3,7},{4,0},{5,1},{6,2},{7,3},{8,12},{9,13},{10,... | collective-permute-start | bytes 294920 | tf_op jit(solution)/shard_map/kept_alone_over_core/ppermute | solution.py:23

commit v7 on v6

--- a/solution.py
+++ b/solution.py
@@ -230,7 +230,7 @@
     kept_parts, sent = lax.optimization_barrier((kept_parts, sent))
     kept_parts["two"] = over_cores(kept_parts["one"], "kept_one")
     kept_parts["alone_sibling"] = over_cores(kept_parts["alone"], "kept_alone")
-    last = {name: kept_parts.pop(name) for name in ("alone", "alone_sibling")}
+    last = {name: kept_parts.pop(name) for name in ("two", "alone_sibling")}
     kept, kept_other = product(last, (0, 1), KEPT, product(kept_parts, (0, 1), KEPT))
     return pl.pallas_call(
         total_kernel,

time: 34.2 us -> 34.2 us (level)
  no operation moved by 1% of the time
where the time goes in v7:
time: 34.2 us; the launch traced here: 34.1 us
  starting transfers between devices  19.8 us (58%)
  waiting for transfers between devices  9.62 us (28%)
  Pallas kernels  3.57 us (10%)
  local copies, waits for them, and re-layouts  0.94 us (3%)
    ppermute x19, starting transfers between devices, swap(): return lax.ppermute(array, ('loop', 'rep'), pairs)  19.8 us
    ppermute x19, waiting for transfers between devices, swap(): return lax.ppermute(array, ('loop', 'rep'), pairs)  9.62 us
    pallas_call x6, Pallas kernels, product(): pl.pallas_call(functools.partial(product_kernel, kinds, hops, bool(before...  2.42 us
    unnamed x6, local copies, waits for them, and re-layouts  0.94 us
    pallas_call x1, Pallas kernels, square(): pl.pallas_call(total_kernel, out_shape=jax.ShapeDtypeStruct((irreps, rows...  0.82 us
  transfers between devices with their start and end apart: 19, of which 7 were waited for; matrix products, arithmetic and copies ran while one was open for 0% of the time, Pallas kernels for 8%

profile of v7, /device:TPU:0, one launch (start us, length us, event | category | flops | bytes accessed | tf_op | source)
XLA Modules:
  0.0 34.1 jit_solution(1690179763448108380)
XLA Ops:
  0.0 0.9 %copy-done.2 = bf16[8,384,32]{1,2,0:T(8,128)(2,1)S(1)} copy-done((bf16[8,384,32]{1,2,0:T(8,128)(2,1)S(1)}, bf16[8,384,32]{1,2,0:T(8,128)(2,1)}, u32[]{:S(2)}) %copy-start.2) | copy-done | bytes 196632
  0.9 0.1 shard_map.37
  1.1 0.0 copy-start.1
  1.1 0.5 %collective-permute-start.2 = (bf16[2,96,128]{2,1,0:T(8,128)(2,1)S(1)}, bf16[2,96,128]{2,1,0:T(8,128)(2,1)S(1)}, u32[]{:S(2)}, u32[]{:S(2)}) collective-permute-start(bf16[2,96,128]{2,1,0:T(8,128)(2,1)S(1)} %get-tuple-element.30.sent_own_ref), channel_id=1, source_target_pairs={{0,4},{1,5},{2,6},{3,7},{4,0},{5,1},{6,2},{7,3},{8,12},{9,13},{10,... | collective-permute-start | bytes 147464 | tf_op jit(solution)/shard_map/sent_near_over_core/ppermute | solution.py:23
  1.6 2.6 %collective-permute-start.1 = (bf16[2,96,128]{2,1,0:T(8,128)(2,1)S(1)}, bf16[2,96,128]{2,1,0:T(8,128)(2,1)S(1)}, u32[]{:S(2)}, u32[]{:S(2)}) collective-permute-start(bf16[2,96,128]{2,1,0:T(8,128)(2,1)S(1)} %get-tuple-element.33), channel_id=1, source_target_pairs={{0,2},{1,3},{2,0},{3,1},{4,5},{5,4},{6,7},{7,6},{8,10},{9,11},{10,... | collective-permute-start | bytes 147464 | tf_op jit(solution)/shard_map/lam_other/ppermute | solution.py:23
  4.2 1.5 %collective-permute-start = (bf16[2,96,128]{2,1,0:T(8,128)(2,1)S(1)}, bf16[2,96,128]{2,1,0:T(8,128)(2,1)S(1)}, u32[]{:S(2)}, u32[]{:S(2)}) collective-permute-start(bf16[2,96,128]{2,1,0:T(8,128)(2,1)S(1)} %get-tuple-element.32._), channel_id=1, source_target_pairs={{0,1},{1,0},{2,3},{3,2},{4,6},{5,7},{6,4},{7,5},{8,9},{9,8},{10,11... | collective-permute-start | bytes 147464 | tf_op jit(solution)/shard_map/lam_mine/ppermute | solution.py:23
  5.7 0.2 shard_map.39
  5.9 0.6 %collective-permute-start.14 = (bf16[4,256,256]{2,1,0:T(8,128)(2,1)S(1)}, bf16[4,256,256]{2,1,0:T(8,128)(2,1)S(1)}, u32[]{:S(2)}, u32[]{:S(2)}) collective-permute-start(bf16[4,256,256]{2,1,0:T(8,128)(2,1)S(1)} %get-tuple-element.45.refs_8_.refs_1_.refs_4_.refs_2_), channel_id=1, source_target_pairs={{0,1},{1,0},{2,3},{3,2},{4,6},{5,7},{6,4},{7,5},{8,9},{9,8},{10,11... | collective-permute-start | bytes 1572872 | tf_op jit(solution)/shard_map/integrals_mine/ppermute | solution.py:23
  6.5 0.0 collective-permute-done.2.refs_1_
  6.5 1.6 %collective-permute-start.8 = (bf16[2,2,96,128]{3,2,1,0:T(8,128)(2,1)S(1)}, bf16[2,2,96,128]{3,2,1,0:T(8,128)(2,1)S(1)}, u32[]{:S(2)}, u32[]{:S(2)}) collective-permute-start(bf16[2,2,96,128]{3,2,1,0:T(8,128)(2,1)S(1)} %pad_maximum_fusion.2), channel_id=1, source_target_pairs={{0,8},{1,9},{2,10},{3,11},{4,20},{5,21},{6,22},{7,23},{8,0},{9,1},... | collective-permute-start | bytes 294920 | tf_op jit(solution)/shard_map/sent_near_by_core/ppermute | solution.py:23
  8.1 0.0 collective-permute-done.1.far_other_ref
  8.1 0.1 collective-permute-done.far_mine_ref
  8.3 0.2 collective-permute-start.3
  8.5 3.5 %collective-permute-start.4 = (bf16[4,96,128]{2,1,0:T(8,128)(2,1)S(1)}, bf16[4,96,128]{2,1,0:T(8,128)(2,1)S(1)}, u32[]{:S(2)}, u32[]{:S(2)}) collective-permute-start(bf16[4,96,128]{2,1,0:T(8,128)(2,1)S(1)} %get-tuple-element.35.refs_0_), channel_id=1, source_target_pairs={{0,24},{1,25},{2,26},{3,27},{4,28},{5,29},{6,30},{7,31},{8,16},{9,... | collective-permute-start | bytes 294920 | tf_op jit(solution)/shard_map/sent_alone/ppermute | solution.py:23
  12.0 0.2 collective-permute-start.5
  12.2 0.0 collective-permute-done.8.refs_6_
  12.2 0.5 %collective-permute-start.10 = (bf16[4,256,256]{2,1,0:T(8,128)(2,1)S(1)}, bf16[4,256,256]{2,1,0:T(8,128)(2,1)S(1)}, u32[]{:S(2)}, u32[]{:S(2)}) collective-permute-start(bf16[4,256,256]{2,1,0:T(8,128)(2,1)S(1)} %get-tuple-element.42.refs_8_.refs_6_.refs_4_.refs_1_), channel_id=1, source_target_pairs={{0,2},{1,3},{2,0},{3,1},{4,5},{5,4},{6,7},{7,6},{8,10},{9,11},{10,... | collective-permute-start | bytes 1572872 | tf_op jit(solution)/shard_map/integrals_other/ppermute | solution.py:23
  12.7 0.0 collective-permute-done.3.refs_2_
  12.8 1.1 %collective-permute-start.6 = (bf16[2,2,96,128]{3,2,1,0:T(8,128)(2,1)S(1)}, bf16[2,2,96,128]{3,2,1,0:T(8,128)(2,1)S(1)}, u32[]{:S(2)}, u32[]{:S(2)}) collective-permute-start(bf16[2,2,96,128]{3,2,1,0:T(8,128)(2,1)S(1)} %pad_maximum_fusion.1), channel_id=1, source_target_pairs={{0,8},{1,9},{2,10},{3,11},{4,20},{5,21},{6,22},{7,23},{8,0},{9,1},... | collective-permute-start | bytes 294920 | tf_op jit(solution)/shard_map/sent_far_by_core/ppermute | solution.py:23
  13.8 1.7 %collective-permute-done.4.refs_3_ = bf16[4,96,128]{2,1,0:T(8,128)(2,1)S(1)} collective-permute-done((bf16[4,96,128]{2,1,0:T(8,128)(2,1)S(1)}, bf16[4,96,128]{2,1,0:T(8,128)(2,1)S(1)}, u32[]{:S(2)}, u32[]{:S(2)}) %collective-permute-start.4) | collective-permute-done | bytes 98336 | tf_op jit(solution)/shard_map/sent_alone/ppermute | solution.py:23
  15.5 0.0 collective-permute-done.5.refs_3_
  15.5 0.0 collective-permute-start.7
  15.6 4.1 %collective-permute-start.12 = (bf16[2,4,96,128]{3,2,1,0:T(8,128)(2,1)S(1)}, bf16[2,4,96,128]{3,2,1,0:T(8,128)(2,1)S(1)}, u32[]{:S(2)}, u32[]{:S(2)}) collective-permute-start(bf16[2,4,96,128]{3,2,1,0:T(8,128)(2,1)S(1)} %pad_maximum_fusion), channel_id=1, source_target_pairs={{0,24},{1,25},{2,26},{3,27},{4,20},{5,21},{6,22},{7,23},{8,16},{9,... | collective-permute-start | bytes 589832 | tf_op jit(solution)/shard_map/kept_by_core/ppermute | solution.py:23
  19.6 0.0 collective-permute-done.6.refs_4_
  19.6 0.5 %collective-permute-start.9 = (bf16[2,2,96,128]{3,2,1,0:T(8,128)(2,1)S(1)}, bf16[2,2,96,128]{3,2,1,0:T(8,128)(2,1)S(1)}, u32[]{:S(2)}, u32[]{:S(2)}) collective-permute-start(bf16[2,2,96,128]{3,2,1,0:T(8,128)(2,1)S(1)} %collective-permute-done.8.refs_6_), channel_id=1, source_target_pairs={{0,4},{1,5},{2,6},{3,7},{4,0},{5,1},{6,2},{7,3},{8,12},{9,13},{10,... | collective-permute-start | bytes 294920 | tf_op jit(solution)/shard_map/sent_near_one_over_core/ppermute | solution.py:23
  20.2 0.0 collective-permute-done.7.refs_5_
  20.2 0.1 collective-permute-start.13
  20.3 0.0 collective-permute-done.14.refs_0_
  20.3 0.9 %collective-permute-done.9.refs_7_ = bf16[2,2,96,128]{3,2,1,0:T(8,128)(2,1)S(1)} collective-permute-done((bf16[2,2,96,128]{3,2,1,0:T(8,128)(2,1)S(1)}, bf16[2,2,96,128]{3,2,1,0:T(8,128)(2,1)S(1)}, u32[]{:S(2)}, u32[]{:S(2)}) %collective-permute-start.9) | collective-permute-done | bytes 98336 | tf_op jit(solution)/shard_map/sent_near_one_over_core/ppermute | solution.py:23
  21.1 0.4 %shard_map.43.refs_3_ = f32[4,96,256]{2,1,0:T(8,128)S(1)} custom-call(bf16[4,96,128]{2,1,0:T(8,128)(2,1)S(1)} %get-tuple-element.35.refs_0_, bf16[2,96,128]{2,1,0:T(8,128)(2,1)S(1)} %collective-permute-done.2.refs_1_, bf16[2,96,128]{2,1,0:T(8,128)(2,1)S(1)} %collective-permute-done.3.refs_2_, bf16[4,96,128]{2,1,0:T(8,128)(2,1)S(1)} %collective-permute-done.4.refs_3_, ...), custom_call_target="tpu_custom_call" | custom-call | tf_op jit(solution)/shard_map/pallas_call | solution.py:200
  21.6 0.0 collective-permute-done.13.refs_0_
  21.6 0.3 shard_map.44
  21.8 0.9 %collective-permute-start.17 = (f32[4,96,256]{2,1,0:T(8,128)S(1)}, f32[4,96,256]{2,1,0:T(8,128)S(1)}, u32[]{:S(2)}, u32[]{:S(2)}) collective-permute-start(f32[4,96,256]{2,1,0:T(8,128)S(1)} %shard_map.44), channel_id=1, source_target_pairs={{0,2},{1,3},{2,0},{3,1},{4,5},{5,4},{6,7},{7,6},{8,10},{9,11},{10,... | collective-permute-start | bytes 1179656 | tf_op jit(solution)/shard_map/sums_mine/ppermute | solution.py:23
  22.8 0.0 collective-permute-done.10.refs_0_
  22.8 0.5 %shard_map.41.refs_3_ = f32[4,96,256]{2,1,0:T(8,128)S(1)} custom-call(bf16[4,96,128]{2,1,0:T(8,128)(2,1)S(1)} %get-tuple-element.35.refs_0_, bf16[2,96,128]{2,1,0:T(8,128)(2,1)S(1)} %collective-permute-done.2.refs_1_, bf16[2,96,128]{2,1,0:T(8,128)(2,1)S(1)} %collective-permute-done.3.refs_2_, bf16[4,96,128]{2,1,0:T(8,128)(2,1)S(1)} %collective-permute-done.4.refs_3_, ...), custom_call_target="tpu_custom_call" | custom-call | tf_op jit(solution)/shard_map/pallas_call | solution.py:200
  23.2 0.3 shard_map.47
  23.5 0.6 %collective-permute-start.18 = (f32[4,96,256]{2,1,0:T(8,128)S(1)}, f32[4,96,256]{2,1,0:T(8,128)S(1)}, u32[]{:S(2)}, u32[]{:S(2)}) collective-permute-start(f32[4,96,256]{2,1,0:T(8,128)S(1)} %shard_map.47), channel_id=1, source_target_pairs={{0,1},{1,0},{2,3},{3,2},{4,6},{5,7},{6,4},{7,5},{8,9},{9,8},{10,11... | collective-permute-start | bytes 1179656 | tf_op jit(solution)/shard_map/sums_other/ppermute | solution.py:23
  24.1 0.8 %collective-permute-start.11 = (bf16[4,96,128]{2,1,0:T(8,128)(2,1)S(1)}, bf16[4,96,128]{2,1,0:T(8,128)(2,1)S(1)}, u32[]{:S(2)}, u32[]{:S(2)}) collective-permute-start(bf16[4,96,128]{2,1,0:T(8,128)(2,1)S(1)} %get-tuple-element.48.refs_2_), channel_id=1, source_target_pairs={{0,8},{1,9},{2,10},{3,11},{4,12},{5,13},{6,14},{7,15},{8,0},{9,1},... | collective-permute-start | bytes 294920 | tf_op jit(solution)/shard_map/kept_alone/ppermute | solution.py:23
  24.9 0.0 collective-permute-done.12.refs_1_
  24.9 5.3 %collective-permute-done.11.refs_0_ = bf16[4,96,128]{2,1,0:T(8,128)(2,1)S(1)} collective-permute-done((bf16[4,96,128]{2,1,0:T(8,128)(2,1)S(1)}, bf16[4,96,128]{2,1,0:T(8,128)(2,1)S(1)}, u32[]{:S(2)}, u32[]{:S(2)}) %collective-permute-start.11) | collective-permute-done | bytes 98336 | tf_op jit(solution)/shard_map/kept_alone/ppermute | solution.py:23
  30.2 0.0 collective-permute-start.15
  30.2 0.5 %collective-permute-start.16 = (bf16[4,96,128]{2,1,0:T(8,128)(2,1)S(1)}, bf16[4,96,128]{2,1,0:T(8,128)(2,1)S(1)}, u32[]{:S(2)}, u32[]{:S(2)}) collective-permute-start(bf16[4,96,128]{2,1,0:T(8,128)(2,1)S(1)} %collective-permute-done.11.refs_0_), channel_id=1, source_target_pairs={{0,4},{1,5},{2,6},{3,7},{4,0},{5,1},{6,2},{7,3},{8,12},{9,13},{10,... | collective-permute-start | bytes 294920 | tf_op jit(solution)/shard_map/kept_alone_over_core/ppermute | solution.py:23
  30.7 0.6 %shard_map.45 = (f32[4,96,256]{2,1,0:T(8,128)S(1)}, f32[4,96,256]{2,1,0:T(8,128)S(1)}) custom-call(bf16[4,96,128]{2,1,0:T(8,128)(2,1)S(1)} %collective-permute-done.11.refs_0_, bf16[2,4,96,128]{3,2,1,0:T(8,128)(2,1)S(1)} %collective-permute-done.12.refs_1_, bf16[4,96,128]{2,1,0:T(8,128)(2,1)S(1)} %get-tuple-element.48.refs_2_, ...), custom_call_target="tpu_custom_call" | custom-call | tf_op jit(solution)/shard_map/pallas_call | solution.py:200
  31.3 0.5 %collective-permute-done.16.refs_1_ = bf16[4,96,128]{2,1,0:T(8,128)(2,1)S(1)} collective-permute-done((bf16[4,96,128]{2,1,0:T(8,128)(2,1)S(1)}, bf16[4,96,128]{2,1,0:T(8,128)(2,1)S(1)}, u32[]{:S(2)}, u32[]{:S(2)}) %collective-permute-start.16) | collective-permute-done | bytes 98336 | tf_op jit(solution)/shard_map/kept_alone_over_core/ppermute | solution.py:23
  31.8 0.4 %shard_map.46 = (f32[4,96,256]{2,1,0:T(8,128)S(1)}, f32[4,96,256]{2,1,0:T(8,128)S(1)}) custom-call(bf16[2,4,96,128]{3,2,1,0:T(8,128)(2,1)S(1)} %collective-permute-done.15.refs_0_, bf16[4,96,128]{2,1,0:T(8,128)(2,1)S(1)} %collective-permute-done.16.refs_1_, bf16[4,256,256]{2,1,0:T(8,128)(2,1)S(1)} %get-tuple-element.45.refs_8_.refs_1_.refs_4_.refs_2_, ...), custom_call_target="tpu_custom_call" | custom-call | tf_op jit(solution)/shard_map/pallas_call | solution.py:200
  32.2 0.7 %collective-permute-done.17.arrived_ref = f32[4,96,256]{2,1,0:T(8,128)S(1)} collective-permute-done((f32[4,96,256]{2,1,0:T(8,128)S(1)}, f32[4,96,256]{2,1,0:T(8,128)S(1)}, u32[]{:S(2)}, u32[]{:S(2)}) %collective-permute-start.17) | collective-permute-done | bytes 393248 | tf_op jit(solution)/shard_map/sums_mine/ppermute | solution.py:23
  32.9 0.4 %collective-permute-done.18.arrived_other_ref = f32[4,96,256]{2,1,0:T(8,128)S(1)} collective-permute-done((f32[4,96,256]{2,1,0:T(8,128)S(1)}, f32[4,96,256]{2,1,0:T(8,128)S(1)}, u32[]{:S(2)}, u32[]{:S(2)}) %collective-permute-start.18) | collective-permute-done | bytes 393248 | tf_op jit(solution)/shard_map/sums_other/ppermute | solution.py:23
  33.3 0.8 %shard_map.48 = bf16[8,96,256]{2,1,0:T(8,128)(2,1)} custom-call(f32[4,96,256]{2,1,0:T(8,128)S(1)} %get-tuple-element.52.kept_ref, f32[4,96,256]{2,1,0:T(8,128)S(1)} %get-tuple-element.53.kept_other_ref, f32[4,96,256]{2,1,0:T(8,128)S(1)} %collective-permute-done.17.arrived_ref, f32[4,96,256]{2,1,0:T(8,128)S(1)} %collective-permute-done.18.arrived_other_ref), custom_call_target="tpu_custom_call" | custom-call | tf_op jit(solution)/shard_map/pallas_call | solution.py:235
  (11 shorter events, 0.1 us)
Async XLA Ops:
  0.0 0.9 %copy-start.2 = (bf16[8,384,32]{1,2,0:T(8,128)(2,1)S(1)}, bf16[8,384,32]{1,2,0:T(8,128)(2,1)}, u32[]{:S(2)}) copy-start(bf16[8,384,32]{1,2,0:T(8,128)(2,1)} %param.3) | copy-start | bytes 589828
  0.9 4.7 %copy-start = (bf16[8,256,256]{2,1,0:T(8,128)(2,1)S(1)}, bf16[8,256,256]{2,1,0:T(8,128)(2,1)}, u32[]{:S(2)}) copy-start(bf16[8,256,256]{2,1,0:T(8,128)(2,1)} %integrals_ref.1) | copy-start | bytes 3145732
  1.1 4.6 %copy-start.1 = (s32[8,8]{1,0:T(8,128)S(1)}, s32[8,8]{1,0:T(8,128)}, u32[]{:S(2)}) copy-start(s32[8,8]{1,0:T(8,128)} %mask_ref.1) | copy-start | bytes 772
  1.1 5.4 %collective-permute-start.2 = (bf16[2,96,128]{2,1,0:T(8,128)(2,1)S(1)}, bf16[2,96,128]{2,1,0:T(8,128)(2,1)S(1)}, u32[]{:S(2)}, u32[]{:S(2)}) collective-permute-start(bf16[2,96,128]{2,1,0:T(8,128)(2,1)S(1)} %get-tuple-element.30.sent_own_ref), channel_id=1, source_target_pairs={{0,4},{1,5},{2,6},{3,7},{4,0},{5,1},{6,2},{7,3},{8,12},{9,13},{10,... | collective-permute-start | bytes 147464 | tf_op jit(solution)/shard_map/sent_near_over_core/ppermute | solution.py:23
  1.6 6.6 %collective-permute-start.1 = (bf16[2,96,128]{2,1,0:T(8,128)(2,1)S(1)}, bf16[2,96,128]{2,1,0:T(8,128)(2,1)S(1)}, u32[]{:S(2)}, u32[]{:S(2)}) collective-permute-start(bf16[2,96,128]{2,1,0:T(8,128)(2,1)S(1)} %get-tuple-element.33), channel_id=1, source_target_pairs={{0,2},{1,3},{2,0},{3,1},{4,5},{5,4},{6,7},{7,6},{8,10},{9,11},{10,... | collective-permute-start | bytes 147464 | tf_op jit(solution)/shard_map/lam_other/ppermute | solution.py:23
  4.2 4.1 %collective-permute-start = (bf16[2,96,128]{2,1,0:T(8,128)(2,1)S(1)}, bf16[2,96,128]{2,1,0:T(8,128)(2,1)S(1)}, u32[]{:S(2)}, u32[]{:S(2)}) collective-permute-start(bf16[2,96,128]{2,1,0:T(8,128)(2,1)S(1)} %get-tuple-element.32._), channel_id=1, source_target_pairs={{0,1},{1,0},{2,3},{3,2},{4,6},{5,7},{6,4},{7,5},{8,9},{9,8},{10,11... | collective-permute-start | bytes 147464 | tf_op jit(solution)/shard_map/lam_mine/ppermute | solution.py:23
  5.9 14.4 %collective-permute-start.14 = (bf16[4,256,256]{2,1,0:T(8,128)(2,1)S(1)}, bf16[4,256,256]{2,1,0:T(8,128)(2,1)S(1)}, u32[]{:S(2)}, u32[]{:S(2)}) collective-permute-start(bf16[4,256,256]{2,1,0:T(8,128)(2,1)S(1)} %get-tuple-element.45.refs_8_.refs_1_.refs_4_.refs_2_), channel_id=1, source_target_pairs={{0,1},{1,0},{2,3},{3,2},{4,6},{5,7},{6,4},{7,5},{8,9},{9,8},{10,11... | collective-permute-start | bytes 1572872 | tf_op jit(solution)/shard_map/integrals_mine/ppermute | solution.py:23
  6.5 5.7 %collective-permute-start.8 = (bf16[2,2,96,128]{3,2,1,0:T(8,128)(2,1)S(1)}, bf16[2,2,96,128]{3,2,1,0:T(8,128)(2,1)S(1)}, u32[]{:S(2)}, u32[]{:S(2)}) collective-permute-start(bf16[2,2,96,128]{3,2,1,0:T(8,128)(2,1)S(1)} %pad_maximum_fusion.2), channel_id=1, source_target_pairs={{0,8},{1,9},{2,10},{3,11},{4,20},{5,21},{6,22},{7,23},{8,0},{9,1},... | collective-permute-start | bytes 294920 | tf_op jit(solution)/shard_map/sent_near_by_core/ppermute | solution.py:23
  8.3 4.4 %collective-permute-start.3 = (bf16[2,96,128]{2,1,0:T(8,128)(2,1)S(1)}, bf16[2,96,128]{2,1,0:T(8,128)(2,1)S(1)}, u32[]{:S(2)}, u32[]{:S(2)}) collective-permute-start(bf16[2,96,128]{2,1,0:T(8,128)(2,1)S(1)} %get-tuple-element.36), channel_id=1, source_target_pairs={{0,4},{1,5},{2,6},{3,7},{4,0},{5,1},{6,2},{7,3},{8,12},{9,13},{10,... | collective-permute-start | bytes 147464 | tf_op jit(solution)/shard_map/sent_far_over_core/ppermute | solution.py:23
  8.5 7.0 %collective-permute-start.4 = (bf16[4,96,128]{2,1,0:T(8,128)(2,1)S(1)}, bf16[4,96,128]{2,1,0:T(8,128)(2,1)S(1)}, u32[]{:S(2)}, u32[]{:S(2)}) collective-permute-start(bf16[4,96,128]{2,1,0:T(8,128)(2,1)S(1)} %get-tuple-element.35.refs_0_), channel_id=1, source_target_pairs={{0,24},{1,25},{2,26},{3,27},{4,28},{5,29},{6,30},{7,31},{8,16},{9,... | collective-permute-start | bytes 294920 | tf_op jit(solution)/shard_map/sent_alone/ppermute | solution.py:23
  12.0 3.5 %collective-permute-start.5 = (bf16[4,96,128]{2,1,0:T(8,128)(2,1)S(1)}, bf16[4,96,128]{2,1,0:T(8,128)(2,1)S(1)}, u32[]{:S(2)}, u32[]{:S(2)}) collective-permute-start(bf16[4,96,128]{2,1,0:T(8,128)(2,1)S(1)} %get-tuple-element.48.refs_2_), channel_id=1, source_target_pairs={{0,4},{1,5},{2,6},{3,7},{4,0},{5,1},{6,2},{7,3},{8,12},{9,13},{10,... | collective-permute-start | bytes 294920 | tf_op jit(solution)/shard_map/kept_over_core/ppermute | solution.py:23
  12.2 10.6 %collective-permute-start.10 = (bf16[4,256,256]{2,1,0:T(8,128)(2,1)S(1)}, bf16[4,256,256]{2,1,0:T(8,128)(2,1)S(1)}, u32[]{:S(2)}, u32[]{:S(2)}) collective-permute-start(bf16[4,256,256]{2,1,0:T(8,128)(2,1)S(1)} %get-tuple-element.42.refs_8_.refs_6_.refs_4_.refs_1_), channel_id=1, source_target_pairs={{0,2},{1,3},{2,0},{3,1},{4,5},{5,4},{6,7},{7,6},{8,10},{9,11},{10,... | collective-permute-start | bytes 1572872 | tf_op jit(solution)/shard_map/integrals_other/ppermute | solution.py:23
  12.8 6.9 %collective-permute-start.6 = (bf16[2,2,96,128]{3,2,1,0:T(8,128)(2,1)S(1)}, bf16[2,2,96,128]{3,2,1,0:T(8,128)(2,1)S(1)}, u32[]{:S(2)}, u32[]{:S(2)}) collective-permute-start(bf16[2,2,96,128]{3,2,1,0:T(8,128)(2,1)S(1)} %pad_maximum_fusion.1), channel_id=1, source_target_pairs={{0,8},{1,9},{2,10},{3,11},{4,20},{5,21},{6,22},{7,23},{8,0},{9,1},... | collective-permute-start | bytes 294920 | tf_op jit(solution)/shard_map/sent_far_by_core/ppermute | solution.py:23
  15.5 4.6 %collective-permute-start.7 = (bf16[4,96,128]{2,1,0:T(8,128)(2,1)S(1)}, bf16[4,96,128]{2,1,0:T(8,128)(2,1)S(1)}, u32[]{:S(2)}, u32[]{:S(2)}) collective-permute-start(bf16[4,96,128]{2,1,0:T(8,128)(2,1)S(1)} %collective-permute-done.4.refs_3_), channel_id=1, source_target_pairs={{0,4},{1,5},{2,6},{3,7},{4,0},{5,1},{6,2},{7,3},{8,12},{9,13},{10,... | collective-permute-start | bytes 294920 | tf_op jit(solution)/shard_map/sent_alone_over_core/ppermute | solution.py:23
  15.6 9.3 %collective-permute-start.12 = (bf16[2,4,96,128]{3,2,1,0:T(8,128)(2,1)S(1)}, bf16[2,4,96,128]{3,2,1,0:T(8,128)(2,1)S(1)}, u32[]{:S(2)}, u32[]{:S(2)}) collective-permute-start(bf16[2,4,96,128]{3,2,1,0:T(8,128)(2,1)S(1)} %pad_maximum_fusion), channel_id=1, source_target_pairs={{0,24},{1,25},{2,26},{3,27},{4,20},{5,21},{6,22},{7,23},{8,16},{9,... | collective-permute-start | bytes 589832 | tf_op jit(solution)/shard_map/kept_by_core/ppermute | solution.py:23
  19.6 1.5 %collective-permute-start.9 = (bf16[2,2,96,128]{3,2,1,0:T(8,128)(2,1)S(1)}, bf16[2,2,96,128]{3,2,1,0:T(8,128)(2,1)S(1)}, u32[]{:S(2)}, u32[]{:S(2)}) collective-permute-start(bf16[2,2,96,128]{3,2,1,0:T(8,128)(2,1)S(1)} %collective-permute-done.8.refs_6_), channel_id=1, source_target_pairs={{0,4},{1,5},{2,6},{3,7},{4,0},{5,1},{6,2},{7,3},{8,12},{9,13},{10,... | collective-permute-start | bytes 294920 | tf_op jit(solution)/shard_map/sent_near_one_over_core/ppermute | solution.py:23
  20.2 1.4 %collective-permute-start.13 = (bf16[2,2,96,128]{3,2,1,0:T(8,128)(2,1)S(1)}, bf16[2,2,96,128]{3,2,1,0:T(8,128)(2,1)S(1)}, u32[]{:S(2)}, u32[]{:S(2)}) collective-permute-start(bf16[2,2,96,128]{3,2,1,0:T(8,128)(2,1)S(1)} %collective-permute-done.6.refs_4_), channel_id=1, source_target_pairs={{0,4},{1,5},{2,6},{3,7},{4,0},{5,1},{6,2},{7,3},{8,12},{9,13},{10,... | collective-permute-start | bytes 294920 | tf_op jit(solution)/shard_map/sent_far_one_over_core/ppermute | solution.py:23
  21.8 11.1 %collective-permute-start.17 = (f32[4,96,256]{2,1,0:T(8,128)S(1)}, f32[4,96,256]{2,1,0:T(8,128)S(1)}, u32[]{:S(2)}, u32[]{:S(2)}) collective-permute-start(f32[4,96,256]{2,1,0:T(8,128)S(1)} %shard_map.44), channel_id=1, source_target_pairs={{0,2},{1,3},{2,0},{3,1},{4,5},{5,4},{6,7},{7,6},{8,10},{9,11},{10,... | collective-permute-start | bytes 1179656 | tf_op jit(solution)/shard_map/sums_mine/ppermute | solution.py:23
  23.5 9.8 %collective-permute-start.18 = (f32[4,96,256]{2,1,0:T(8,128)S(1)}, f32[4,96,256]{2,1,0:T(8,128)S(1)}, u32[]{:S(2)}, u32[]{:S(2)}) collective-permute-start(f32[4,96,256]{2,1,0:T(8,128)S(1)} %shard_map.47), channel_id=1, source_target_pairs={{0,1},{1,0},{2,3},{3,2},{4,6},{5,7},{6,4},{7,5},{8,9},{9,8},{10,11... | collective-permute-start | bytes 1179656 | tf_op jit(solution)/shard_map/sums_other/ppermute | solution.py:23
  24.1 6.1 %collective-permute-start.11 = (bf16[4,96,128]{2,1,0:T(8,128)(2,1)S(1)}, bf16[4,96,128]{2,1,0:T(8,128)(2,1)S(1)}, u32[]{:S(2)}, u32[]{:S(2)}) collective-permute-start(bf16[4,96,128]{2,1,0:T(8,128)(2,1)S(1)} %get-tuple-element.48.refs_2_), channel_id=1, source_target_pairs={{0,8},{1,9},{2,10},{3,11},{4,12},{5,13},{6,14},{7,15},{8,0},{9,1},... | collective-permute-start | bytes 294920 | tf_op jit(solution)/shard_map/kept_alone/ppermute | solution.py:23
  30.2 1.6 %collective-permute-start.15 = (bf16[2,4,96,128]{3,2,1,0:T(8,128)(2,1)S(1)}, bf16[2,4,96,128]{3,2,1,0:T(8,128)(2,1)S(1)}, u32[]{:S(2)}, u32[]{:S(2)}) collective-permute-start(bf16[2,4,96,128]{3,2,1,0:T(8,128)(2,1)S(1)} %collective-permute-done.12.refs_1_), channel_id=1, source_target_pairs={{0,4},{1,5},{2,6},{3,7},{4,0},{5,1},{6,2},{7,3},{8,12},{9,13},{10,... | collective-permute-start | bytes 589832 | tf_op jit(solution)/shard_map/kept_one_over_core/ppermute | solution.py:23
  30.2 1.6 %collective-permute-start.16 = (bf16[4,96,128]{2,1,0:T(8,128)(2,1)S(1)}, bf16[4,96,128]{2,1,0:T(8,128)(2,1)S(1)}, u32[]{:S(2)}, u32[]{:S(2)}) collective-permute-start(bf16[4,96,128]{2,1,0:T(8,128)(2,1)S(1)} %collective-permute-done.11.refs_0_), channel_id=1, source_target_pairs={{0,4},{1,5},{2,6},{3,7},{4,0},{5,1},{6,2},{7,3},{8,12},{9,13},{10,... | collective-permute-start | bytes 294920 | tf_op jit(solution)/shard_map/kept_alone_over_core/ppermute | solution.py:23

commit v8 on v7

--- a/solution.py
+++ b/solution.py
@@ -121,11 +121,9 @@
     copies = []
     for kind, kept, arrived in ((0, kept_ref, arrived_ref), (1, kept_other_ref, arrived_other_ref)):
         at = (1 - core if kind else core) * halves
-        for h in range(halves):
-            step = kind * halves + h
-            rounded[step] = (kept[h] + arrived[h]).astype(rounded.dtype)
-            copies.append(pltpu.make_async_copy(rounded.at[step], out_ref.at[at + h], done.at[step]))
-            copies[-1].start()
+        rounded[kind] = (kept[...] + arrived[...]).astype(rounded.dtype)
+        copies.append(pltpu.make_async_copy(rounded.at[kind], out_ref.at[pl.ds(at, halves)], done.at[kind]))
+        copies[-1].start()
     for copy in copies:
         copy.wait()
 
@@ -237,7 +235,7 @@
         out_shape=jax.ShapeDtypeStruct((irreps, rows, columns), bf16),
         in_specs=[in_vmem] * 4,
         out_specs=pl.BlockSpec(memory_space=pl.ANY),
-        scratch_shapes=[VMEM((irreps, rows, columns), bf16), pltpu.SemaphoreType.DMA((irreps,))],
+        scratch_shapes=[VMEM((2,) + sums.shape, bf16), pltpu.SemaphoreType.DMA((2,))],
         compiler_params=PARAMS,
     )(kept, kept_other, sum_mine, sum_other)
 

time: 34.2 us -> 34.2 us (level)
  no operation moved by 1% of the time
where the time goes in v8:
time: 34.2 us; the launch traced here: 34.1 us
  starting transfers between devices  19.8 us (58%)
  waiting for transfers between devices  9.62 us (28%)
  Pallas kernels  3.55 us (10%)
  local copies, waits for them, and re-layouts  0.94 us (3%)
    ppermute x19, starting transfers between devices, swap(): return lax.ppermute(array, ('loop', 'rep'), pairs)  19.8 us
    ppermute x19, waiting for transfers between devices, swap(): return lax.ppermute(array, ('loop', 'rep'), pairs)  9.62 us
    pallas_call x6, Pallas kernels, product(): pl.pallas_call(functools.partial(product_kernel, kinds, hops, bool(before...  2.42 us
    unnamed x6, local copies, waits for them, and re-layouts  0.94 us
    pallas_call x1, Pallas kernels, square(): pl.pallas_call(total_kernel, out_shape=jax.ShapeDtypeStruct((irreps, rows...  0.79 us
  transfers between devices with their start and end apart: 19, of which 7 were waited for; matrix products, arithmetic and copies ran while one was open for 0% of the time, Pallas kernels for 8%

profile of v8, /device:TPU:0, one launch (start us, length us, event | category | flops | bytes accessed | tf_op | source)
XLA Modules:
  0.0 34.1 jit_solution(4259699051815416573)
XLA Ops:
  0.0 0.9 %copy-done.2 = bf16[8,384,32]{1,2,0:T(8,128)(2,1)S(1)} copy-done((bf16[8,384,32]{1,2,0:T(8,128)(2,1)S(1)}, bf16[8,384,32]{1,2,0:T(8,128)(2,1)}, u32[]{:S(2)}) %copy-start.2) | copy-done | bytes 196632
  0.9 0.1 shard_map.37
  1.1 0.0 copy-start.1
  1.1 0.5 %collective-permute-start.2 = (bf16[2,96,128]{2,1,0:T(8,128)(2,1)S(1)}, bf16[2,96,128]{2,1,0:T(8,128)(2,1)S(1)}, u32[]{:S(2)}, u32[]{:S(2)}) collective-permute-start(bf16[2,96,128]{2,1,0:T(8,128)(2,1)S(1)} %get-tuple-element.30.sent_own_ref), channel_id=1, source_target_pairs={{0,4},{1,5},{2,6},{3,7},{4,0},{5,1},{6,2},{7,3},{8,12},{9,13},{10,... | collective-permute-start | bytes 147464 | tf_op jit(solution)/shard_map/sent_near_over_core/ppermute | solution.py:23
  1.6 2.6 %collective-permute-start.1 = (bf16[2,96,128]{2,1,0:T(8,128)(2,1)S(1)}, bf16[2,96,128]{2,1,0:T(8,128)(2,1)S(1)}, u32[]{:S(2)}, u32[]{:S(2)}) collective-permute-start(bf16[2,96,128]{2,1,0:T(8,128)(2,1)S(1)} %get-tuple-element.33), channel_id=1, source_target_pairs={{0,2},{1,3},{2,0},{3,1},{4,5},{5,4},{6,7},{7,6},{8,10},{9,11},{10,... | collective-permute-start | bytes 147464 | tf_op jit(solution)/shard_map/lam_other/ppermute | solution.py:23
  4.2 1.5 %collective-permute-start = (bf16[2,96,128]{2,1,0:T(8,128)(2,1)S(1)}, bf16[2,96,128]{2,1,0:T(8,128)(2,1)S(1)}, u32[]{:S(2)}, u32[]{:S(2)}) collective-permute-start(bf16[2,96,128]{2,1,0:T(8,128)(2,1)S(1)} %get-tuple-element.32._), channel_id=1, source_target_pairs={{0,1},{1,0},{2,3},{3,2},{4,6},{5,7},{6,4},{7,5},{8,9},{9,8},{10,11... | collective-permute-start | bytes 147464 | tf_op jit(solution)/shard_map/lam_mine/ppermute | solution.py:23
  5.7 0.2 shard_map.39
  5.9 0.6 %collective-permute-start.14 = (bf16[4,256,256]{2,1,0:T(8,128)(2,1)S(1)}, bf16[4,256,256]{2,1,0:T(8,128)(2,1)S(1)}, u32[]{:S(2)}, u32[]{:S(2)}) collective-permute-start(bf16[4,256,256]{2,1,0:T(8,128)(2,1)S(1)} %get-tuple-element.45.refs_8_.refs_1_.refs_4_.refs_2_), channel_id=1, source_target_pairs={{0,1},{1,0},{2,3},{3,2},{4,6},{5,7},{6,4},{7,5},{8,9},{9,8},{10,11... | collective-permute-start | bytes 1572872 | tf_op jit(solution)/shard_map/integrals_mine/ppermute | solution.py:23
  6.5 0.0 collective-permute-done.2.refs_1_
  6.5 1.6 %collective-permute-start.8 = (bf16[2,2,96,128]{3,2,1,0:T(8,128)(2,1)S(1)}, bf16[2,2,96,128]{3,2,1,0:T(8,128)(2,1)S(1)}, u32[]{:S(2)}, u32[]{:S(2)}) collective-permute-start(bf16[2,2,96,128]{3,2,1,0:T(8,128)(2,1)S(1)} %pad_maximum_fusion.2), channel_id=1, source_target_pairs={{0,8},{1,9},{2,10},{3,11},{4,20},{5,21},{6,22},{7,23},{8,0},{9,1},... | collective-permute-start | bytes 294920 | tf_op jit(solution)/shard_map/sent_near_by_core/ppermute | solution.py:23
  8.1 0.0 collective-permute-done.1.far_other_ref
  8.1 0.1 collective-permute-done.far_mine_ref
  8.3 0.2 collective-permute-start.3
  8.5 3.5 %collective-permute-start.4 = (bf16[4,96,128]{2,1,0:T(8,128)(2,1)S(1)}, bf16[4,96,128]{2,1,0:T(8,128)(2,1)S(1)}, u32[]{:S(2)}, u32[]{:S(2)}) collective-permute-start(bf16[4,96,128]{2,1,0:T(8,128)(2,1)S(1)} %get-tuple-element.35.refs_0_), channel_id=1, source_target_pairs={{0,24},{1,25},{2,26},{3,27},{4,28},{5,29},{6,30},{7,31},{8,16},{9,... | collective-permute-start | bytes 294920 | tf_op jit(solution)/shard_map/sent_alone/ppermute | solution.py:23
  12.0 0.2 collective-permute-start.5
  12.2 0.0 collective-permute-done.8.refs_6_
  12.2 0.5 %collective-permute-start.10 = (bf16[4,256,256]{2,1,0:T(8,128)(2,1)S(1)}, bf16[4,256,256]{2,1,0:T(8,128)(2,1)S(1)}, u32[]{:S(2)}, u32[]{:S(2)}) collective-permute-start(bf16[4,256,256]{2,1,0:T(8,128)(2,1)S(1)} %get-tuple-element.42.refs_8_.refs_6_.refs_4_.refs_1_), channel_id=1, source_target_pairs={{0,2},{1,3},{2,0},{3,1},{4,5},{5,4},{6,7},{7,6},{8,10},{9,11},{10,... | collective-permute-start | bytes 1572872 | tf_op jit(solution)/shard_map/integrals_other/ppermute | solution.py:23
  12.7 0.0 collective-permute-done.3.refs_2_
  12.8 1.1 %collective-permute-start.6 = (bf16[2,2,96,128]{3,2,1,0:T(8,128)(2,1)S(1)}, bf16[2,2,96,128]{3,2,1,0:T(8,128)(2,1)S(1)}, u32[]{:S(2)}, u32[]{:S(2)}) collective-permute-start(bf16[2,2,96,128]{3,2,1,0:T(8,128)(2,1)S(1)} %pad_maximum_fusion.1), channel_id=1, source_target_pairs={{0,8},{1,9},{2,10},{3,11},{4,20},{5,21},{6,22},{7,23},{8,0},{9,1},... | collective-permute-start | bytes 294920 | tf_op jit(solution)/shard_map/sent_far_by_core/ppermute | solution.py:23
  13.8 1.7 %collective-permute-done.4.refs_3_ = bf16[4,96,128]{2,1,0:T(8,128)(2,1)S(1)} collective-permute-done((bf16[4,96,128]{2,1,0:T(8,128)(2,1)S(1)}, bf16[4,96,128]{2,1,0:T(8,128)(2,1)S(1)}, u32[]{:S(2)}, u32[]{:S(2)}) %collective-permute-start.4) | collective-permute-done | bytes 98336 | tf_op jit(solution)/shard_map/sent_alone/ppermute | solution.py:23
  15.5 0.0 collective-permute-done.5.refs_3_
  15.5 0.0 collective-permute-start.7
  15.6 4.1 %collective-permute-start.12 = (bf16[2,4,96,128]{3,2,1,0:T(8,128)(2,1)S(1)}, bf16[2,4,96,128]{3,2,1,0:T(8,128)(2,1)S(1)}, u32[]{:S(2)}, u32[]{:S(2)}) collective-permute-start(bf16[2,4,96,128]{3,2,1,0:T(8,128)(2,1)S(1)} %pad_maximum_fusion), channel_id=1, source_target_pairs={{0,24},{1,25},{2,26},{3,27},{4,20},{5,21},{6,22},{7,23},{8,16},{9,... | collective-permute-start | bytes 589832 | tf_op jit(solution)/shard_map/kept_by_core/ppermute | solution.py:23
  19.6 0.0 collective-permute-done.6.refs_4_
  19.6 0.5 %collective-permute-start.9 = (bf16[2,2,96,128]{3,2,1,0:T(8,128)(2,1)S(1)}, bf16[2,2,96,128]{3,2,1,0:T(8,128)(2,1)S(1)}, u32[]{:S(2)}, u32[]{:S(2)}) collective-permute-start(bf16[2,2,96,128]{3,2,1,0:T(8,128)(2,1)S(1)} %collective-permute-done.8.refs_6_), channel_id=1, source_target_pairs={{0,4},{1,5},{2,6},{3,7},{4,0},{5,1},{6,2},{7,3},{8,12},{9,13},{10,... | collective-permute-start | bytes 294920 | tf_op jit(solution)/shard_map/sent_near_one_over_core/ppermute | solution.py:23
  20.2 0.0 collective-permute-done.7.refs_5_
  20.2 0.1 collective-permute-start.13
  20.3 0.0 collective-permute-done.14.refs_0_
  20.3 0.9 %collective-permute-done.9.refs_7_ = bf16[2,2,96,128]{3,2,1,0:T(8,128)(2,1)S(1)} collective-permute-done((bf16[2,2,96,128]{3,2,1,0:T(8,128)(2,1)S(1)}, bf16[2,2,96,128]{3,2,1,0:T(8,128)(2,1)S(1)}, u32[]{:S(2)}, u32[]{:S(2)}) %collective-permute-start.9) | collective-permute-done | bytes 98336 | tf_op jit(solution)/shard_map/sent_near_one_over_core/ppermute | solution.py:23
  21.1 0.4 %shard_map.43.refs_3_ = f32[4,96,256]{2,1,0:T(8,128)S(1)} custom-call(bf16[4,96,128]{2,1,0:T(8,128)(2,1)S(1)} %get-tuple-element.35.refs_0_, bf16[2,96,128]{2,1,0:T(8,128)(2,1)S(1)} %collective-permute-done.2.refs_1_, bf16[2,96,128]{2,1,0:T(8,128)(2,1)S(1)} %collective-permute-done.3.refs_2_, bf16[4,96,128]{2,1,0:T(8,128)(2,1)S(1)} %collective-permute-done.4.refs_3_, ...), custom_call_target="tpu_custom_call" | custom-call | tf_op jit(solution)/shard_map/pallas_call | solution.py:198
  21.6 0.0 collective-permute-done.13.refs_0_
  21.6 0.3 shard_map.44
  21.8 0.9 %collective-permute-start.17 = (f32[4,96,256]{2,1,0:T(8,128)S(1)}, f32[4,96,256]{2,1,0:T(8,128)S(1)}, u32[]{:S(2)}, u32[]{:S(2)}) collective-permute-start(f32[4,96,256]{2,1,0:T(8,128)S(1)} %shard_map.44), channel_id=1, source_target_pairs={{0,2},{1,3},{2,0},{3,1},{4,5},{5,4},{6,7},{7,6},{8,10},{9,11},{10,... | collective-permute-start | bytes 1179656 | tf_op jit(solution)/shard_map/sums_mine/ppermute | solution.py:23
  22.8 0.0 collective-permute-done.10.refs_0_
  22.8 0.5 %shard_map.41.refs_3_ = f32[4,96,256]{2,1,0:T(8,128)S(1)} custom-call(bf16[4,96,128]{2,1,0:T(8,128)(2,1)S(1)} %get-tuple-element.35.refs_0_, bf16[2,96,128]{2,1,0:T(8,128)(2,1)S(1)} %collective-permute-done.2.refs_1_, bf16[2,96,128]{2,1,0:T(8,128)(2,1)S(1)} %collective-permute-done.3.refs_2_, bf16[4,96,128]{2,1,0:T(8,128)(2,1)S(1)} %collective-permute-done.4.refs_3_, ...), custom_call_target="tpu_custom_call" | custom-call | tf_op jit(solution)/shard_map/pallas_call | solution.py:198
  23.2 0.3 shard_map.47
  23.5 0.6 %collective-permute-start.18 = (f32[4,96,256]{2,1,0:T(8,128)S(1)}, f32[4,96,256]{2,1,0:T(8,128)S(1)}, u32[]{:S(2)}, u32[]{:S(2)}) collective-permute-start(f32[4,96,256]{2,1,0:T(8,128)S(1)} %shard_map.47), channel_id=1, source_target_pairs={{0,1},{1,0},{2,3},{3,2},{4,6},{5,7},{6,4},{7,5},{8,9},{9,8},{10,11... | collective-permute-start | bytes 1179656 | tf_op jit(solution)/shard_map/sums_other/ppermute | solution.py:23
  24.1 0.8 %collective-permute-start.11 = (bf16[4,96,128]{2,1,0:T(8,128)(2,1)S(1)}, bf16[4,96,128]{2,1,0:T(8,128)(2,1)S(1)}, u32[]{:S(2)}, u32[]{:S(2)}) collective-permute-start(bf16[4,96,128]{2,1,0:T(8,128)(2,1)S(1)} %get-tuple-element.48.refs_2_), channel_id=1, source_target_pairs={{0,8},{1,9},{2,10},{3,11},{4,12},{5,13},{6,14},{7,15},{8,0},{9,1},... | collective-permute-start | bytes 294920 | tf_op jit(solution)/shard_map/kept_alone/ppermute | solution.py:23
  24.9 0.0 collective-permute-done.12.refs_1_
  24.9 5.3 %collective-permute-done.11.refs_0_ = bf16[4,96,128]{2,1,0:T(8,128)(2,1)S(1)} collective-permute-done((bf16[4,96,128]{2,1,0:T(8,128)(2,1)S(1)}, bf16[4,96,128]{2,1,0:T(8,128)(2,1)S(1)}, u32[]{:S(2)}, u32[]{:S(2)}) %collective-permute-start.11) | collective-permute-done | bytes 98336 | tf_op jit(solution)/shard_map/kept_alone/ppermute | solution.py:23
  30.2 0.0 collective-permute-start.15
  30.2 0.5 %collective-permute-start.16 = (bf16[4,96,128]{2,1,0:T(8,128)(2,1)S(1)}, bf16[4,96,128]{2,1,0:T(8,128)(2,1)S(1)}, u32[]{:S(2)}, u32[]{:S(2)}) collective-permute-start(bf16[4,96,128]{2,1,0:T(8,128)(2,1)S(1)} %collective-permute-done.11.refs_0_), channel_id=1, source_target_pairs={{0,4},{1,5},{2,6},{3,7},{4,0},{5,1},{6,2},{7,3},{8,12},{9,13},{10,... | collective-permute-start | bytes 294920 | tf_op jit(solution)/shard_map/kept_alone_over_core/ppermute | solution.py:23
  30.7 0.6 %shard_map.45 = (f32[4,96,256]{2,1,0:T(8,128)S(1)}, f32[4,96,256]{2,1,0:T(8,128)S(1)}) custom-call(bf16[4,96,128]{2,1,0:T(8,128)(2,1)S(1)} %collective-permute-done.11.refs_0_, bf16[2,4,96,128]{3,2,1,0:T(8,128)(2,1)S(1)} %collective-permute-done.12.refs_1_, bf16[4,96,128]{2,1,0:T(8,128)(2,1)S(1)} %get-tuple-element.48.refs_2_, ...), custom_call_target="tpu_custom_call" | custom-call | tf_op jit(solution)/shard_map/pallas_call | solution.py:198
  31.3 0.5 %collective-permute-done.16.refs_1_ = bf16[4,96,128]{2,1,0:T(8,128)(2,1)S(1)} collective-permute-done((bf16[4,96,128]{2,1,0:T(8,128)(2,1)S(1)}, bf16[4,96,128]{2,1,0:T(8,128)(2,1)S(1)}, u32[]{:S(2)}, u32[]{:S(2)}) %collective-permute-start.16) | collective-permute-done | bytes 98336 | tf_op jit(solution)/shard_map/kept_alone_over_core/ppermute | solution.py:23
  31.8 0.4 %shard_map.46 = (f32[4,96,256]{2,1,0:T(8,128)S(1)}, f32[4,96,256]{2,1,0:T(8,128)S(1)}) custom-call(bf16[2,4,96,128]{3,2,1,0:T(8,128)(2,1)S(1)} %collective-permute-done.15.refs_0_, bf16[4,96,128]{2,1,0:T(8,128)(2,1)S(1)} %collective-permute-done.16.refs_1_, bf16[4,256,256]{2,1,0:T(8,128)(2,1)S(1)} %get-tuple-element.45.refs_8_.refs_1_.refs_4_.refs_2_, ...), custom_call_target="tpu_custom_call" | custom-call | tf_op jit(solution)/shard_map/pallas_call | solution.py:198
  32.2 0.7 %collective-permute-done.17.arrived_ref = f32[4,96,256]{2,1,0:T(8,128)S(1)} collective-permute-done((f32[4,96,256]{2,1,0:T(8,128)S(1)}, f32[4,96,256]{2,1,0:T(8,128)S(1)}, u32[]{:S(2)}, u32[]{:S(2)}) %collective-permute-start.17) | collective-permute-done | bytes 393248 | tf_op jit(solution)/shard_map/sums_mine/ppermute | solution.py:23
  32.9 0.4 %collective-permute-done.18.arrived_other_ref = f32[4,96,256]{2,1,0:T(8,128)S(1)} collective-permute-done((f32[4,96,256]{2,1,0:T(8,128)S(1)}, f32[4,96,256]{2,1,0:T(8,128)S(1)}, u32[]{:S(2)}, u32[]{:S(2)}) %collective-permute-start.18) | collective-permute-done | bytes 393248 | tf_op jit(solution)/shard_map/sums_other/ppermute | solution.py:23
  33.3 0.8 %shard_map.48 = bf16[8,96,256]{2,1,0:T(8,128)(2,1)} custom-call(f32[4,96,256]{2,1,0:T(8,128)S(1)} %get-tuple-element.52.kept_ref, f32[4,96,256]{2,1,0:T(8,128)S(1)} %get-tuple-element.53.kept_other_ref, f32[4,96,256]{2,1,0:T(8,128)S(1)} %collective-permute-done.17.arrived_ref, f32[4,96,256]{2,1,0:T(8,128)S(1)} %collective-permute-done.18.arrived_other_ref), custom_call_target="tpu_custom_call" | custom-call | tf_op jit(solution)/shard_map/pallas_call | solution.py:233
  (11 shorter events, 0.1 us)
Async XLA Ops:
  0.0 0.9 %copy-start.2 = (bf16[8,384,32]{1,2,0:T(8,128)(2,1)S(1)}, bf16[8,384,32]{1,2,0:T(8,128)(2,1)}, u32[]{:S(2)}) copy-start(bf16[8,384,32]{1,2,0:T(8,128)(2,1)} %param.3) | copy-start | bytes 589828
  0.9 4.7 %copy-start = (bf16[8,256,256]{2,1,0:T(8,128)(2,1)S(1)}, bf16[8,256,256]{2,1,0:T(8,128)(2,1)}, u32[]{:S(2)}) copy-start(bf16[8,256,256]{2,1,0:T(8,128)(2,1)} %integrals_ref.1) | copy-start | bytes 3145732
  1.1 4.6 %copy-start.1 = (s32[8,8]{1,0:T(8,128)S(1)}, s32[8,8]{1,0:T(8,128)}, u32[]{:S(2)}) copy-start(s32[8,8]{1,0:T(8,128)} %mask_ref.1) | copy-start | bytes 772
  1.1 5.4 %collective-permute-start.2 = (bf16[2,96,128]{2,1,0:T(8,128)(2,1)S(1)}, bf16[2,96,128]{2,1,0:T(8,128)(2,1)S(1)}, u32[]{:S(2)}, u32[]{:S(2)}) collective-permute-start(bf16[2,96,128]{2,1,0:T(8,128)(2,1)S(1)} %get-tuple-element.30.sent_own_ref), channel_id=1, source_target_pairs={{0,4},{1,5},{2,6},{3,7},{4,0},{5,1},{6,2},{7,3},{8,12},{9,13},{10,... | collective-permute-start | bytes 147464 | tf_op jit(solution)/shard_map/sent_near_over_core/ppermute | solution.py:23
  1.6 6.6 %collective-permute-start.1 = (bf16[2,96,128]{2,1,0:T(8,128)(2,1)S(1)}, bf16[2,96,128]{2,1,0:T(8,128)(2,1)S(1)}, u32[]{:S(2)}, u32[]{:S(2)}) collective-permute-start(bf16[2,96,128]{2,1,0:T(8,128)(2,1)S(1)} %get-tuple-element.33), channel_id=1, source_target_pairs={{0,2},{1,3},{2,0},{3,1},{4,5},{5,4},{6,7},{7,6},{8,10},{9,11},{10,... | collective-permute-start | bytes 147464 | tf_op jit(solution)/shard_map/lam_other/ppermute | solution.py:23
  4.2 4.1 %collective-permute-start = (bf16[2,96,128]{2,1,0:T(8,128)(2,1)S(1)}, bf16[2,96,128]{2,1,0:T(8,128)(2,1)S(1)}, u32[]{:S(2)}, u32[]{:S(2)}) collective-permute-start(bf16[2,96,128]{2,1,0:T(8,128)(2,1)S(1)} %get-tuple-element.32._), channel_id=1, source_target_pairs={{0,1},{1,0},{2,3},{3,2},{4,6},{5,7},{6,4},{7,5},{8,9},{9,8},{10,11... | collective-permute-start | bytes 147464 | tf_op jit(solution)/shard_map/lam_mine/ppermute | solution.py:23
  5.9 14.4 %collective-permute-start.14 = (bf16[4,256,256]{2,1,0:T(8,128)(2,1)S(1)}, bf16[4,256,256]{2,1,0:T(8,128)(2,1)S(1)}, u32[]{:S(2)}, u32[]{:S(2)}) collective-permute-start(bf16[4,256,256]{2,1,0:T(8,128)(2,1)S(1)} %get-tuple-element.45.refs_8_.refs_1_.refs_4_.refs_2_), channel_id=1, source_target_pairs={{0,1},{1,0},{2,3},{3,2},{4,6},{5,7},{6,4},{7,5},{8,9},{9,8},{10,11... | collective-permute-start | bytes 1572872 | tf_op jit(solution)/shard_map/integrals_mine/ppermute | solution.py:23
  6.5 5.7 %collective-permute-start.8 = (bf16[2,2,96,128]{3,2,1,0:T(8,128)(2,1)S(1)}, bf16[2,2,96,128]{3,2,1,0:T(8,128)(2,1)S(1)}, u32[]{:S(2)}, u32[]{:S(2)}) collective-permute-start(bf16[2,2,96,128]{3,2,1,0:T(8,128)(2,1)S(1)} %pad_maximum_fusion.2), channel_id=1, source_target_pairs={{0,8},{1,9},{2,10},{3,11},{4,20},{5,21},{6,22},{7,23},{8,0},{9,1},... | collective-permute-start | bytes 294920 | tf_op jit(solution)/shard_map/sent_near_by_core/ppermute | solution.py:23
  8.3 4.4 %collective-permute-start.3 = (bf16[2,96,128]{2,1,0:T(8,128)(2,1)S(1)}, bf16[2,96,128]{2,1,0:T(8,128)(2,1)S(1)}, u32[]{:S(2)}, u32[]{:S(2)}) collective-permute-start(bf16[2,96,128]{2,1,0:T(8,128)(2,1)S(1)} %get-tuple-element.36), channel_id=1, source_target_pairs={{0,4},{1,5},{2,6},{3,7},{4,0},{5,1},{6,2},{7,3},{8,12},{9,13},{10,... | collective-permute-start | bytes 147464 | tf_op jit(solution)/shard_map/sent_far_over_core/ppermute | solution.py:23
  8.5 7.0 %collective-permute-start.4 = (bf16[4,96,128]{2,1,0:T(8,128)(2,1)S(1)}, bf16[4,96,128]{2,1,0:T(8,128)(2,1)S(1)}, u32[]{:S(2)}, u32[]{:S(2)}) collective-permute-start(bf16[4,96,128]{2,1,0:T(8,128)(2,1)S(1)} %get-tuple-element.35.refs_0_), channel_id=1, source_target_pairs={{0,24},{1,25},{2,26},{3,27},{4,28},{5,29},{6,30},{7,31},{8,16},{9,... | collective-permute-start | bytes 294920 | tf_op jit(solution)/shard_map/sent_alone/ppermute | solution.py:23
  12.0 3.5 %collective-permute-start.5 = (bf16[4,96,128]{2,1,0:T(8,128)(2,1)S(1)}, bf16[4,96,128]{2,1,0:T(8,128)(2,1)S(1)}, u32[]{:S(2)}, u32[]{:S(2)}) collective-permute-start(bf16[4,96,128]{2,1,0:T(8,128)(2,1)S(1)} %get-tuple-element.48.refs_2_), channel_id=1, source_target_pairs={{0,4},{1,5},{2,6},{3,7},{4,0},{5,1},{6,2},{7,3},{8,12},{9,13},{10,... | collective-permute-start | bytes 294920 | tf_op jit(solution)/shard_map/kept_over_core/ppermute | solution.py:23
  12.2 10.6 %collective-permute-start.10 = (bf16[4,256,256]{2,1,0:T(8,128)(2,1)S(1)}, bf16[4,256,256]{2,1,0:T(8,128)(2,1)S(1)}, u32[]{:S(2)}, u32[]{:S(2)}) collective-permute-start(bf16[4,256,256]{2,1,0:T(8,128)(2,1)S(1)} %get-tuple-element.42.refs_8_.refs_6_.refs_4_.refs_1_), channel_id=1, source_target_pairs={{0,2},{1,3},{2,0},{3,1},{4,5},{5,4},{6,7},{7,6},{8,10},{9,11},{10,... | collective-permute-start | bytes 1572872 | tf_op jit(solution)/shard_map/integrals_other/ppermute | solution.py:23
  12.8 6.9 %collective-permute-start.6 = (bf16[2,2,96,128]{3,2,1,0:T(8,128)(2,1)S(1)}, bf16[2,2,96,128]{3,2,1,0:T(8,128)(2,1)S(1)}, u32[]{:S(2)}, u32[]{:S(2)}) collective-permute-start(bf16[2,2,96,128]{3,2,1,0:T(8,128)(2,1)S(1)} %pad_maximum_fusion.1), channel_id=1, source_target_pairs={{0,8},{1,9},{2,10},{3,11},{4,20},{5,21},{6,22},{7,23},{8,0},{9,1},... | collective-permute-start | bytes 294920 | tf_op jit(solution)/shard_map/sent_far_by_core/ppermute | solution.py:23
  15.5 4.6 %collective-permute-start.7 = (bf16[4,96,128]{2,1,0:T(8,128)(2,1)S(1)}, bf16[4,96,128]{2,1,0:T(8,128)(2,1)S(1)}, u32[]{:S(2)}, u32[]{:S(2)}) collective-permute-start(bf16[4,96,128]{2,1,0:T(8,128)(2,1)S(1)} %collective-permute-done.4.refs_3_), channel_id=1, source_target_pairs={{0,4},{1,5},{2,6},{3,7},{4,0},{5,1},{6,2},{7,3},{8,12},{9,13},{10,... | collective-permute-start | bytes 294920 | tf_op jit(solution)/shard_map/sent_alone_over_core/ppermute | solution.py:23
  15.6 9.3 %collective-permute-start.12 = (bf16[2,4,96,128]{3,2,1,0:T(8,128)(2,1)S(1)}, bf16[2,4,96,128]{3,2,1,0:T(8,128)(2,1)S(1)}, u32[]{:S(2)}, u32[]{:S(2)}) collective-permute-start(bf16[2,4,96,128]{3,2,1,0:T(8,128)(2,1)S(1)} %pad_maximum_fusion), channel_id=1, source_target_pairs={{0,24},{1,25},{2,26},{3,27},{4,20},{5,21},{6,22},{7,23},{8,16},{9,... | collective-permute-start | bytes 589832 | tf_op jit(solution)/shard_map/kept_by_core/ppermute | solution.py:23
  19.6 1.5 %collective-permute-start.9 = (bf16[2,2,96,128]{3,2,1,0:T(8,128)(2,1)S(1)}, bf16[2,2,96,128]{3,2,1,0:T(8,128)(2,1)S(1)}, u32[]{:S(2)}, u32[]{:S(2)}) collective-permute-start(bf16[2,2,96,128]{3,2,1,0:T(8,128)(2,1)S(1)} %collective-permute-done.8.refs_6_), channel_id=1, source_target_pairs={{0,4},{1,5},{2,6},{3,7},{4,0},{5,1},{6,2},{7,3},{8,12},{9,13},{10,... | collective-permute-start | bytes 294920 | tf_op jit(solution)/shard_map/sent_near_one_over_core/ppermute | solution.py:23
  20.2 1.4 %collective-permute-start.13 = (bf16[2,2,96,128]{3,2,1,0:T(8,128)(2,1)S(1)}, bf16[2,2,96,128]{3,2,1,0:T(8,128)(2,1)S(1)}, u32[]{:S(2)}, u32[]{:S(2)}) collective-permute-start(bf16[2,2,96,128]{3,2,1,0:T(8,128)(2,1)S(1)} %collective-permute-done.6.refs_4_), channel_id=1, source_target_pairs={{0,4},{1,5},{2,6},{3,7},{4,0},{5,1},{6,2},{7,3},{8,12},{9,13},{10,... | collective-permute-start | bytes 294920 | tf_op jit(solution)/shard_map/sent_far_one_over_core/ppermute | solution.py:23
  21.8 11.1 %collective-permute-start.17 = (f32[4,96,256]{2,1,0:T(8,128)S(1)}, f32[4,96,256]{2,1,0:T(8,128)S(1)}, u32[]{:S(2)}, u32[]{:S(2)}) collective-permute-start(f32[4,96,256]{2,1,0:T(8,128)S(1)} %shard_map.44), channel_id=1, source_target_pairs={{0,2},{1,3},{2,0},{3,1},{4,5},{5,4},{6,7},{7,6},{8,10},{9,11},{10,... | collective-permute-start | bytes 1179656 | tf_op jit(solution)/shard_map/sums_mine/ppermute | solution.py:23
  23.5 9.8 %collective-permute-start.18 = (f32[4,96,256]{2,1,0:T(8,128)S(1)}, f32[4,96,256]{2,1,0:T(8,128)S(1)}, u32[]{:S(2)}, u32[]{:S(2)}) collective-permute-start(f32[4,96,256]{2,1,0:T(8,128)S(1)} %shard_map.47), channel_id=1, source_target_pairs={{0,1},{1,0},{2,3},{3,2},{4,6},{5,7},{6,4},{7,5},{8,9},{9,8},{10,11... | collective-permute-start | bytes 1179656 | tf_op jit(solution)/shard_map/sums_other/ppermute | solution.py:23
  24.1 6.1 %collective-permute-start.11 = (bf16[4,96,128]{2,1,0:T(8,128)(2,1)S(1)}, bf16[4,96,128]{2,1,0:T(8,128)(2,1)S(1)}, u32[]{:S(2)}, u32[]{:S(2)}) collective-permute-start(bf16[4,96,128]{2,1,0:T(8,128)(2,1)S(1)} %get-tuple-element.48.refs_2_), channel_id=1, source_target_pairs={{0,8},{1,9},{2,10},{3,11},{4,12},{5,13},{6,14},{7,15},{8,0},{9,1},... | collective-permute-start | bytes 294920 | tf_op jit(solution)/shard_map/kept_alone/ppermute | solution.py:23
  30.2 1.6 %collective-permute-start.15 = (bf16[2,4,96,128]{3,2,1,0:T(8,128)(2,1)S(1)}, bf16[2,4,96,128]{3,2,1,0:T(8,128)(2,1)S(1)}, u32[]{:S(2)}, u32[]{:S(2)}) collective-permute-start(bf16[2,4,96,128]{3,2,1,0:T(8,128)(2,1)S(1)} %collective-permute-done.12.refs_1_), channel_id=1, source_target_pairs={{0,4},{1,5},{2,6},{3,7},{4,0},{5,1},{6,2},{7,3},{8,12},{9,13},{10,... | collective-permute-start | bytes 589832 | tf_op jit(solution)/shard_map/kept_one_over_core/ppermute | solution.py:23
  30.2 1.6 %collective-permute-start.16 = (bf16[4,96,128]{2,1,0:T(8,128)(2,1)S(1)}, bf16[4,96,128]{2,1,0:T(8,128)(2,1)S(1)}, u32[]{:S(2)}, u32[]{:S(2)}) collective-permute-start(bf16[4,96,128]{2,1,0:T(8,128)(2,1)S(1)} %collective-permute-done.11.refs_0_), channel_id=1, source_target_pairs={{0,4},{1,5},{2,6},{3,7},{4,0},{5,1},{6,2},{7,3},{8,12},{9,13},{10,... | collective-permute-start | bytes 294920 | tf_op jit(solution)/shard_map/kept_alone_over_core/ppermute | solution.py:23
